TPU v7x, 512 devices: a whole 4x4x16 slice. The times are simulated.
512 devices in a mesh: leaf: 512 (over y, x, z, core).
Axes of the slice: x: 4, y: 4, z: 16, core: 2. Of those that a mesh axis runs over, the one named last changes fastest.
Arguments:
- densities: float32 [16, 524288], P(None, 'leaf'), may hold values from -6 to 6
- points: float32 [3, 524288], P(None, 'leaf'), may hold values from 0 to 1
- area_normals: float32 [3, 524288], P(None, 'leaf'), may hold values from -0.234375 to 0.234375
- col_basis: float32 [64, 524288], P(None, 'leaf'), may hold values from -0.375 to 0.375
- row_basis: float32 [64, 524288], P(None, 'leaf'), may hold values from -0.75 to 0.75
- up_leaf: float32 [2048, 4096], P('leaf'), may hold values from -0.5 to 0.5
- up_mid: float32 [1024, 4096], P('leaf'), may hold values from -0.5 to 0.5
- down_leaf: float32 [2048, 4096], P('leaf'), may hold values from -0.5 to 0.5
- down_mid: float32 [1024, 4096], P('leaf'), may hold values from -0.5 to 0.5
- couple_leaf: float32 [2048, 6, 4096], P('leaf'), may hold values from -0.3125 to 0.3125
- couple_mid: float32 [1024, 6, 4096], P('leaf'), may hold values from -0.3125 to 0.3125
- couple_top: float32 [512, 16, 4096], P('leaf'), may hold values from -0.1875 to 0.1875
- near_list: int32 [2048, 8], P('leaf'), may hold values from 0 to 2047, as said below
- near_count: int32 [2048], P('leaf'), may hold values from 1 to 8
- adm_leaf: int32 [2048, 6], P('leaf'), may hold values from 0 to 2047, as said below
- adm_mid: int32 [1024, 6], P('leaf'), may hold values from 0 to 1023, as said below
- adm_top: int32 [512, 16], P('leaf'), may hold values from 0 to 511
Outputs:
- potential: float32 [16, 524288], P(None, 'leaf')
Inputs may be any that keep to these rules, and one draw needn't show every extreme that they name: `near_list`: entry 0 of each row is the leaf itself; every other entry lies within 4 leaves of it. `adm_leaf`: every source lies in the leaf range of the device just before or just after the one that holds the target leaf. `adm_mid`: every source lies among the middle-level clusters of the device just before or just after the one that holds the target.
All inputs are finite; a program needn't handle non-finite values.
Results may differ from a plain program's by a relative error of at most 0.0003.
Values sent between devices are 32-bit elements; how exact they have to be, the bound alone decides.
No kernel may reach another device: no remote copies, remote signals or barrier semaphores. Data moves between devices by JAX's collectives and lax.ppermute only.
A program may use at most 64 MiB of HBM per device.

v0:
```python
import math

import jax
import jax.numpy as jnp
from jax import lax
from jax.sharding import PartitionSpec as P

RHS = 16
LEAF = 256
RANK = 64
NEAR = 8
ADM_LEAF = 6
ADM_MID = 6
ADM_TOP = 16


smooth_sq = 0.01
four_pi = 4.0 * math.pi
highest = lax.Precision.HIGHEST


def with_halo(block, sides, width):
    for axis, dim in sides:
        count = lax.axis_size(axis)
        forward = [(i, i + 1) for i in range(count - 1)]
        backward = [(target, source) for source, target in forward]
        low = lax.ppermute(
            lax.slice_in_dim(block, block.shape[dim] - width, None, axis=dim), axis, forward
        )
        high = lax.ppermute(lax.slice_in_dim(block, 0, width, axis=dim), axis, backward)
        block = jnp.concatenate([low, block, high], axis=dim)
    return block


def kernel_block(target, source, normals):
    delta_x = target[0][None, :] - source[0][:, None]
    delta_y = target[1][None, :] - source[1][:, None]
    delta_z = target[2][None, :] - source[2][:, None]
    radius_sq = delta_x * delta_x + delta_y * delta_y + delta_z * delta_z + smooth_sq
    along = (
        normals[0][:, None] * delta_x
        + normals[1][:, None] * delta_y
        + normals[2][:, None] * delta_z
    )
    return along / (four_pi * radius_sq * jnp.sqrt(radius_sq))


def coefficients(dens_rows, basis_rows, cluster_count):
    return jnp.einsum(
        "rlp,klp->lrk",
        dens_rows.reshape(RHS, cluster_count, LEAF),
        basis_rows.reshape(RANK, cluster_count, LEAF),
        precision=highest,
    )


def climb(children, transfers):
    groups = transfers.shape[0]
    return jnp.einsum(
        "mcrk,mckj->mrj", children.reshape(groups, 2, RHS, RANK), transfers, precision=highest
    )


def descend(parents, transfers, coupled):
    groups = parents.shape[0]
    total = coupled.reshape(groups, 2, RHS, RANK) + jnp.einsum(
        "mrk,mckj->mcrj", parents, transfers, precision=highest
    )
    return total.reshape(groups * 2, RHS, RANK)


def couple(sources, blocks):
    return jnp.einsum("tark,takj->trj", sources, blocks, precision=highest)


def on_device(
    densities,
    points,
    area_normals,
    col_basis,
    row_basis,
    up_leaf,
    up_mid,
    down_leaf,
    down_mid,
    couple_leaf,
    couple_mid,
    couple_top,
    near_list,
    near_count,
    adm_leaf,
    adm_mid,
    adm_top,
):
    leaf_count = near_list.shape[0]
    mid_count = leaf_count // 2
    span_size = densities.shape[1]
    device_index = lax.axis_index("leaf")
    first_leaf = device_index * leaf_count
    stacked = jnp.concatenate([densities, points, area_normals], 0)
    widened = with_halo(stacked, (("leaf", 1),), span_size)
    own_leaf = coefficients(densities, col_basis, leaf_count)
    own_mid = climb(own_leaf, up_leaf.reshape(mid_count, 2, RANK, RANK))
    packed = jnp.concatenate(
        [own_leaf.reshape(leaf_count, RHS * RANK), own_mid.reshape(mid_count, RHS * RANK)], 0
    )
    rim_coefs = with_halo(packed, (("leaf", 0),), leaf_count + mid_count)
    rim_groups = rim_coefs.reshape(3, leaf_count + mid_count, RHS, RANK)
    wide_leaf = rim_groups[:, :leaf_count].reshape(3 * leaf_count, RHS, RANK)
    wide_mid = rim_groups[:, leaf_count:].reshape(3 * mid_count, RHS, RANK)
    wide_dens = widened[:RHS]
    wide_points = widened[RHS : RHS + 3]
    wide_normals = widened[RHS + 3 : RHS + 6]
    own_top = climb(own_mid, up_mid.reshape(1, 2, RANK, RANK))
    top_blocks = couple_top.reshape(1, ADM_TOP, RANK, RANK)
    every_top = lax.all_gather(own_top.reshape(1, RHS * RANK), "leaf", axis=0, tiled=True)
    chosen_top = jnp.take(every_top, adm_top[0], axis=0).reshape(1, ADM_TOP, RHS, RANK)
    top_field = couple(chosen_top, top_blocks)
    mid_base = device_index * mid_count - mid_count
    mid_sources = jnp.take(wide_mid, adm_mid - mid_base, axis=0)
    mid_couple = couple(mid_sources, couple_mid.reshape(mid_count, ADM_MID, RANK, RANK))
    mid_field = descend(top_field, down_mid.reshape(1, 2, RANK, RANK), mid_couple)
    leaf_base = first_leaf - leaf_count
    leaf_sources = jnp.take(wide_leaf, adm_leaf - leaf_base, axis=0)
    leaf_couple = couple(leaf_sources, couple_leaf.reshape(leaf_count, ADM_LEAF, RANK, RANK))
    leaf_field = descend(mid_field, down_leaf.reshape(mid_count, 2, RANK, RANK), leaf_couple)
    far_part = jnp.einsum(
        "lrk,klp->rlp", leaf_field, row_basis.reshape(RANK, leaf_count, LEAF), precision=highest
    ).reshape(RHS, span_size)

    def block_term(target, source_leaf):
        start = (source_leaf - leaf_base) * LEAF
        block = kernel_block(
            target,
            lax.dynamic_slice_in_dim(wide_points, start, LEAF, 1),
            lax.dynamic_slice_in_dim(wide_normals, start, LEAF, 1),
        )
        return jnp.dot(
            lax.dynamic_slice_in_dim(wide_dens, start, LEAF, 1), block, precision=highest
        )

    def one_leaf(item):
        local_leaf, sources, count = item
        target = lax.dynamic_slice_in_dim(points, local_leaf * LEAF, LEAF, 1)
        total = jnp.zeros((RHS, LEAF), jnp.float32)
        for slot_index in range(NEAR):
            term = block_term(target, sources[slot_index])
            total = total + jnp.where(slot_index < count, term, jnp.zeros_like(term))
        return total

    near_blocks = lax.map(
        one_leaf, (jnp.arange(leaf_count, dtype=jnp.int32), near_list, near_count)
    )
    near_part = jnp.transpose(near_blocks, (1, 0, 2)).reshape(RHS, span_size)
    return 0.5 * densities + near_part + far_part


def solution(mesh):
    return jax.shard_map(
        on_device,
        mesh=mesh,
        in_specs=(
            P(None, "leaf"),
            P(None, "leaf"),
            P(None, "leaf"),
            P(None, "leaf"),
            P(None, "leaf"),
            P("leaf", None),
            P("leaf", None),
            P("leaf", None),
            P("leaf", None),
            P("leaf", None, None),
            P("leaf", None, None),
            P("leaf", None, None),
            P("leaf", None),
            P("leaf"),
            P("leaf", None),
            P("leaf", None),
            P("leaf", None),
        ),
        out_specs=P(None, "leaf"),
        check_vma=False,
    )
```

profile of v0, /device:TPU:1, one launch (start us, length us, event | category | flops | bytes accessed | tf_op | source)
XLA Modules:
  0.0 237.5 jit_solution(17463821512557997660)
XLA Ops:
  6.6 1.0 reshape.249
  7.6 1.3 fusion.193
  9.4 8.8 %collective-permute-start.3 = (f32[6,1024]{1,0:T(8,128)S(1)}, f32[6,1024]{1,0:T(8,128)S(1)}, u32[]{:S(2)}, u32[]{:S(2)}) collective-permute-start(f32[6,1024]{1,0:T(8,128)S(1)} %pad_maximum_fusion.5), channel_id=1, source_target_pairs={{1,0},{2,1},{3,2},{4,3},{5,4},{6,5},{7,6},{8,7},{9,8},{10,9},{11,1... | collective-permute-start | bytes 73736 | tf_op jit(solution)/shard_map/ppermute | solution.py:30
  18.2 1.9 collective-permute-start.2
  20.1 0.9 pad_maximum_fusion.1
  21.0 2.4 %collective-permute-start.1 = (f32[22,1024]{1,0:T(8,128)S(1)}, f32[22,1024]{1,0:T(8,128)S(1)}, u32[]{:S(2)}, u32[]{:S(2)}) collective-permute-start(f32[22,1024]{1,0:T(8,128)S(1)} %pad_maximum_fusion.1), channel_id=1, source_target_pairs={{1,0},{2,1},{3,2},{4,3},{5,4},{6,5},{7,6},{8,7},{9,8},{10,9},{11,1... | collective-permute-start | bytes 270344 | tf_op jit(solution)/shard_map/ppermute | solution.py:30
  23.4 3.2 %collective-permute-start = (f32[22,1024]{1,0:T(8,128)S(1)}, f32[22,1024]{1,0:T(8,128)S(1)}, u32[]{:S(2)}, u32[]{:S(2)}) collective-permute-start(f32[22,1024]{1,0:T(8,128)S(1)} %pad_maximum_fusion.1), channel_id=1, source_target_pairs={{0,1},{1,2},{2,3},{3,4},{4,5},{5,6},{6,7},{7,8},{8,9},{9,10},{10,1... | collective-permute-start | bytes 270344 | tf_op jit(solution)/shard_map/ppermute | solution.py:27
  26.6 0.9 reshape.258
  27.7 0.7 reshape.295
  28.4 0.7 fusion.204
  29.0 0.7 compare_and_fusion
  29.7 0.7 compare_and_fusion.2
  30.5 0.7 compare_and_fusion.1
  31.3 1.4 reshape.253
  34.8 0.7 fusion.188
  36.1 73.6 %while.10 = (s32[]{:T(128)}, f32[4,16,256]{2,1,0:T(8,128)S(1)}, s32[4]{0:T(128)S(1)}, s32[4,8]{1,0:T(4,128)}, s32[]{:T(128)}, /*index=5*/f32[16,3072]{1,0:T(8,12...) while((s32[]{:T(128)}, f32[4,16,256]{2,1,0:T(8,128)S(1)}, ...), condition=%wide.region_1.2_spmd, body=%wide.region_0.1_spmd.sunk | while | flops 109637680 | bytes 556135 | solution.py:151
  36.1 0.7 constant_dynamic-slice_fusion.21
  36.8 0.7 fusion.260
  44.2 0.6 dynamic_slice.124
  54.5 0.7 constant_dynamic-slice_fusion.21
  55.2 0.7 fusion.260
  61.1 0.6 dynamic_slice.123
  62.6 0.6 dynamic_slice.124
  72.9 0.7 constant_dynamic-slice_fusion.21
  73.6 0.7 fusion.260
  79.6 0.6 dynamic_slice.123
  91.3 0.7 constant_dynamic-slice_fusion.21
  92.0 0.7 fusion.260
  98.0 0.6 dynamic_slice.123
  109.7 116.4 %all-gather.3.cloned.1.call-done = f32[512,1,1024]{2,1,0:T(1,128)} async-done(((f32[1,1,1024]{2,1,0:T(1,128)}), f32[512,1,1024]{2,1,0:T(1,128)}) %all-gather.3.cloned.1.call-update) | async-done | bytes 2097168 | tf_op jit(solution)/shard_map/all_gather | solution.py:116
  226.2 2.1 copy.67
  230.0 0.6 add_add_fusion
  (102 shorter events, 26.5 us)
Async XLA Ops:
  6.5 26.1 %copy-start.4 = (f32[2,6,4096]{2,0,1:T(2,128)S(1)}, f32[2,6,4096]{2,0,1:T(2,128)}, u32[]{:S(2)}) copy-start(f32[2,6,4096]{2,0,1:T(2,128)} %param.29) | copy-start | bytes 589828
  6.5 26.4 %copy-start.1 = (f32[1,16,4096]{2,1,0:T(8,128)S(1)}, f32[1,16,4096]{2,1,0:T(8,128)}, u32[]{:S(2)}) copy-start(f32[1,16,4096]{2,1,0:T(8,128)} %param.30) | copy-start | bytes 786436
  6.5 26.7 %copy-start.7 = (f32[2,4096]{1,0:T(2,128)S(1)}, f32[2,4096]{1,0:T(2,128)}, u32[]{:S(2)}) copy-start(f32[2,4096]{1,0:T(2,128)} %param.27) | copy-start | bytes 98308
  6.5 26.8 %copy-start.6 = (f32[4,4096]{1,0:T(4,128)S(1)}, f32[4,4096]{1,0:T(4,128)}, u32[]{:S(2)}) copy-start(f32[4,4096]{1,0:T(4,128)} %param.26) | copy-start | bytes 196612
  6.5 219.6 %all-gather.3.cloned.1.call-start = ((), (), s32[]{:S(2)}) async-start(), calls=%async_computation | async-start | bytes 2101248 | tf_op jit(solution)/shard_map/all_gather | solution.py:116
  9.4 24.1 %collective-permute-start.3 = (f32[6,1024]{1,0:T(8,128)S(1)}, f32[6,1024]{1,0:T(8,128)S(1)}, u32[]{:S(2)}, u32[]{:S(2)}) collective-permute-start(f32[6,1024]{1,0:T(8,128)S(1)} %pad_maximum_fusion.5), channel_id=1, source_target_pairs={{1,0},{2,1},{3,2},{4,3},{5,4},{6,5},{7,6},{8,7},{9,8},{10,9},{11,1... | collective-permute-start | bytes 73736 | tf_op jit(solution)/shard_map/ppermute | solution.py:30
  18.2 15.3 %collective-permute-start.2 = (f32[6,1024]{1,0:T(8,128)S(1)}, f32[6,1024]{1,0:T(8,128)S(1)}, u32[]{:S(2)}, u32[]{:S(2)}) collective-permute-start(f32[6,1024]{1,0:T(8,128)S(1)} %pad_maximum_fusion.5), channel_id=1, source_target_pairs={{0,1},{1,2},{2,3},{3,4},{4,5},{5,6},{6,7},{7,8},{8,9},{9,10},{10,1... | collective-permute-start | bytes 73736 | tf_op jit(solution)/shard_map/ppermute | solution.py:27
  21.0 14.9 %collective-permute-start.1 = (f32[22,1024]{1,0:T(8,128)S(1)}, f32[22,1024]{1,0:T(8,128)S(1)}, u32[]{:S(2)}, u32[]{:S(2)}) collective-permute-start(f32[22,1024]{1,0:T(8,128)S(1)} %pad_maximum_fusion.1), channel_id=1, source_target_pairs={{1,0},{2,1},{3,2},{4,3},{5,4},{6,5},{7,6},{8,7},{9,8},{10,9},{11,1... | collective-permute-start | bytes 270344 | tf_op jit(solution)/shard_map/ppermute | solution.py:30
  23.4 12.5 %collective-permute-start = (f32[22,1024]{1,0:T(8,128)S(1)}, f32[22,1024]{1,0:T(8,128)S(1)}, u32[]{:S(2)}, u32[]{:S(2)}) collective-permute-start(f32[22,1024]{1,0:T(8,128)S(1)} %pad_maximum_fusion.1), channel_id=1, source_target_pairs={{0,1},{1,2},{2,3},{3,4},{4,5},{5,6},{6,7},{7,8},{8,9},{9,10},{10,1... | collective-permute-start | bytes 270344 | tf_op jit(solution)/shard_map/ppermute | solution.py:27
  33.0 3.0 %copy-start = (f32[16,1024]{1,0:T(8,128)S(1)}, f32[16,1024]{1,0:T(8,128)}, u32[]{:S(2)}) copy-start(f32[16,1024]{1,0:T(8,128)} %param.19) | copy-start | bytes 196612
  33.0 3.0 %copy-start.3 = (f32[3,1024]{1,0:T(4,128)S(1)}, f32[3,1024]{1,0:T(4,128)}, u32[]{:S(2)}) copy-start(f32[3,1024]{1,0:T(4,128)} %param.20) | copy-start | bytes 36868
  33.0 3.0 %copy-start.5 = (f32[3,1024]{1,0:T(4,128)S(1)}, f32[3,1024]{1,0:T(4,128)}, u32[]{:S(2)}) copy-start(f32[3,1024]{1,0:T(4,128)} %param.21) | copy-start | bytes 36868
  33.5 2.6 %copy-start.8 = (s32[4]{0:T(128)S(1)}, s32[4]{0:T(128)}, u32[]{:S(2)}) copy-start(s32[4]{0:T(128)} %param.32) | copy-start | bytes 52
  109.7 120.0 %copy-start.2 = (f32[64,1024]{1,0:T(8,128)S(1)}, f32[64,1024]{1,0:T(8,128)}, u32[]{:S(2)}) copy-start(f32[64,1024]{1,0:T(8,128)} %param.23) | copy-start | bytes 786436
Sparse Core Ops, SparseCore 0:
  28.5 197.6 all-gather.2
where the time goes:
time: 239 us; the launch traced here: 237 us
  waiting for transfers between devices  116 us (49%)
  loops' own time  43.7 us (18%)
  matrix products  22 us (9%)
  local copies, waits for them, and re-layouts  20.9 us (9%)
  starting transfers between devices  16.3 us (7%)
  between operations  13.7 us (6%)
  other arithmetic  4.43 us (2%)
    all_gather x1, waiting for transfers between devices, on_device(): lax.all_gather(own_top.reshape(1, RHS * RANK), 'leaf', axis=0, tiled=True)  116 us
    another operation x1, loops' own time, on_device(): lax.map(one_leaf, (jnp.arange(leaf_count, dtype=jnp.int32), near_list, ne...  43.7 us
    dot_general x32, matrix products, block_term(): jnp.dot(lax.dynamic_slice_in_dim(wide_dens, start, LEAF, 1), block, preci...  18.1 us
    ppermute x2, starting transfers between devices, with_halo(): lax.ppermute(lax.slice_in_dim(block, 0, width, axis=dim), axis, backward)  11.2 us
    dynamic_slice x12, local copies, waits for them, and re-layouts, on_device(): lax.map(one_leaf, (jnp.arange(leaf_count, dtype=jnp.int32), near_list, ne...  7.88 us
    ppermute x2, starting transfers between devices, with_halo(): lax.ppermute(lax.slice_in_dim(block, block.shape[dim] - width, None, axis...  5.08 us
  transfers between devices with their start and end apart: 5, of which 1 were waited for; matrix products, arithmetic and copies ran while one was open for 17% of the time, Pallas kernels for 0%

commit v1 on v0

v1 whole, which is shorter than its diff:
```python
import math

import jax
import jax.numpy as jnp
from jax import lax
from jax.experimental import pallas as pl
from jax.experimental.pallas import tpu as pltpu
from jax.sharding import PartitionSpec as P

RHS = 16
LEAF = 256
RANK = 64
HALF = RANK // 2
LEAF_DEV = 4
MID_DEV = 2
NEAR = 8
ADM_LEAF = 6
ADM_MID = 6
ADM_TOP = 16
SPAN = LEAF_DEV * LEAF
CHUNKS = RANK * RANK // 128
FEATURES = 32
PACKED_ROWS = 32
COEF_ROW = 24

smooth_sq = 0.01
four_pi = 4.0 * math.pi
highest = lax.Precision.HIGHEST
f32 = jnp.float32
bf16 = jnp.bfloat16

SMEM = pl.BlockSpec(memory_space=pltpu.SMEM)
VMEM = pl.BlockSpec(memory_space=pltpu.VMEM)
ANY = pl.BlockSpec(memory_space=pl.ANY)


def dot(lhs, rhs, lhs_dim=1, rhs_dim=0):
    return lax.dot_general(
        lhs,
        rhs,
        (((lhs_dim,), (rhs_dim,)), ((), ())),
        precision=highest,
        preferred_element_type=f32,
    )


def even_odd(ref, index):
    even = ref[index, pl.ds(0, HALF, stride=2), :]
    odd = ref[index, pl.ds(1, HALF, stride=2), :]
    return jnp.concatenate([even[:, :RHS], odd[:, :RHS]], axis=1)


def pack(split):
    return jnp.concatenate([split[8 * g : 8 * g + 8] for g in range(4)], axis=1)


def unpack(tile):
    return jnp.concatenate([tile[:, 32 * g : 32 * g + 32] for g in range(4)], axis=0)


def fold(product):
    return product[:RANK, :RHS] + product[RANK:, RHS:]


def up_kernel(dens, points, normals, col_basis, up_leaf, up_mid, top_out, packed, leaf_rows, mid_rows, leaf_t, mid_t):
    packed[0:RHS, :] = dens[...]
    packed[RHS : RHS + 3, :] = points[...]
    packed[RHS + 3 : RHS + 6, :] = normals[...]
    packed[RHS + 6 : COEF_ROW, :] = jnp.zeros((COEF_ROW - RHS - 6, SPAN), f32)
    packed[COEF_ROW:, 6 * 128 :] = jnp.zeros((8, SPAN - 6 * 128), f32)
    for chunk in range(CHUNKS):
        lanes = slice(128 * chunk, 128 * chunk + 128)
        leaf_rows[8 * chunk : 8 * chunk + LEAF_DEV, :] = up_leaf[:, lanes]
        mid_rows[8 * chunk : 8 * chunk + MID_DEV, :] = up_mid[:, lanes]
    for c in range(LEAF_DEV):
        cols = slice(LEAF * c, LEAF * c + LEAF)
        leaf_t[c, :, 0:RHS] = dot(col_basis[:, cols], dens[:, cols], 1, 1)
    leaf_split = [even_odd(leaf_t, c) for c in range(LEAF_DEV)]
    for c in range(LEAF_DEV):
        packed[COEF_ROW:, 128 * c : 128 * c + 128] = pack(leaf_split[c])
    for m in range(MID_DEV):
        pair = (2 * m, 2 * m + 1)
        lhs = jnp.concatenate([leaf_rows[pl.ds(c, CHUNKS, stride=8), :] for c in pair], axis=0)
        rhs = jnp.concatenate([leaf_split[c] for c in pair], axis=0)
        mid_t[m, :, 0:RHS] = fold(dot(lhs, rhs, 0, 0))
    mid_split = [even_odd(mid_t, m) for m in range(MID_DEV)]
    for m in range(MID_DEV):
        packed[COEF_ROW:, 128 * (LEAF_DEV + m) : 128 * (LEAF_DEV + m) + 128] = pack(mid_split[m])
    lhs = jnp.concatenate([mid_rows[pl.ds(m, CHUNKS, stride=8), :] for m in range(MID_DEV)], axis=0)
    rhs = jnp.concatenate(mid_split, axis=0)
    leaf_t[0, :, 0:RHS] = fold(dot(lhs, rhs, 0, 0))
    tile = pack(even_odd(leaf_t, 0))
    for peer in range(top_out.shape[0]):
        top_out[peer] = tile


def up_call(dens, points, normals, col_basis, up_leaf, up_mid, peers):
    return pl.pallas_call(
        up_kernel,
        name="up_sweep",
        out_shape=(
            jax.ShapeDtypeStruct((peers, 8, 128), f32),
            jax.ShapeDtypeStruct((PACKED_ROWS, SPAN), f32),
        ),
        in_specs=[VMEM] * 6,
        out_specs=(VMEM, VMEM),
        scratch_shapes=[
            pltpu.VMEM((8 * CHUNKS, 128), f32),
            pltpu.VMEM((8 * CHUNKS, 128), f32),
            pltpu.VMEM((LEAF_DEV, RANK, 128), f32),
            pltpu.VMEM((MID_DEV, RANK, 128), f32),
        ],
        cost_estimate=pl.CostEstimate(flops=10_000_000, bytes_accessed=800_000, transcendentals=0),
    )(dens, points, normals, col_basis, up_leaf, up_mid)


def three_parts(values):
    first = values.astype(bf16).astype(f32)
    rest = values - first
    second = rest.astype(bf16).astype(f32)
    return first, second, (rest - second).astype(bf16).astype(f32)


def near_kernel(
    near_list,
    near_count,
    adm_leaf,
    adm_mid,
    own,
    low,
    high,
    couple_leaf,
    couple_mid,
    couple_top,
    down_mid,
    down_leaf,
    near_out,
    leaf_couple,
    mid_couple,
    top_mats,
    mid_mats,
    leaf_mats,
    feats,
    sources,
    targets,
    dens_parts,
    split_leaf,
    split_mid,
    rows,
    natural,
    work,
):
    halo = (low, own, high)
    first_leaf = near_list[0, 0]

    count = jnp.int32(0)
    for i in range(LEAF_DEV):
        limit = near_count[i]
        slots = [near_list[i, j] for j in range(NEAR)]
        used = [jnp.int32(j) < limit for j in range(NEAR)]
        for j in range(NEAR):
            uses = jnp.int32(0)
            fresh = used[j]
            for other in range(NEAR):
                same = jnp.logical_and(used[other], slots[other] == slots[j])
                uses = uses + same.astype(jnp.int32)
                if other < j:
                    fresh = jnp.logical_and(fresh, jnp.logical_not(same))
            work[0, count] = jnp.int32(i)
            work[1, count] = slots[j] - first_leaf + LEAF_DEV
            work[2, count] = uses
            count = count + fresh.astype(jnp.int32)
    work[0, count] = jnp.int32(0)
    work[1, count] = jnp.int32(0)
    work[2, count] = jnp.int32(0)

    for side in range(3):
        block = halo[side]
        place = block[RHS : RHS + 3, :] - 0.5
        normal = block[RHS + 3 : RHS + 6, :] * (1.0 / four_pi)
        p1, p2, p3 = three_parts(place)
        n1, n2, n3 = three_parts(normal)
        square = jnp.sum(place * place, axis=0, keepdims=True)
        inner = -jnp.sum(place * normal, axis=0, keepdims=True)
        ones = jnp.ones((3, SPAN), f32)
        zeros = jnp.zeros((8, SPAN), f32)
        s1, s2, s3 = three_parts(square)
        i1, i2, i3 = three_parts(inner)
        feats[0:8] = zeros
        feats[24:32] = zeros
        feats[32:40] = zeros
        feats[56:64] = zeros
        feats[0:1], feats[1:2], feats[2:3] = s1, s2, s3
        feats[3:6] = ones
        for slot, part in enumerate((p1, p1, p2, p2, p1, p3)):
            feats[6 + 3 * slot : 9 + 3 * slot] = part * -2.0
        feats[32:33], feats[33:34], feats[34:35] = i1, i2, i3
        for slot, part in enumerate((n1, n1, n2, n2, n1, n3)):
            feats[38 + 3 * slot : 41 + 3 * slot] = part
        for leaf in range(LEAF_DEV):
            cols = slice(LEAF * leaf, LEAF * leaf + LEAF)
            start = (LEAF_DEV * side + leaf) * LEAF
            sources[start : start + LEAF, :] = jnp.transpose(feats[:, cols]).astype(bf16)
            dens = block[0:RHS, cols]
            dens_high = dens.astype(bf16)
            dens_parts[LEAF_DEV * side + leaf, 0:RHS, :] = dens_high
            dens_parts[LEAF_DEV * side + leaf, RHS:, :] = (dens - dens_high.astype(f32)).astype(bf16)
        if side == 1:
            t1, t2, t3 = three_parts(square + smooth_sq)
            feats[0:3] = ones
            feats[3:4], feats[4:5], feats[5:6] = t1, t2, t3
            for slot, part in enumerate((p1, p2, p1, p2, p3, p1)):
                feats[6 + 3 * slot : 9 + 3 * slot] = part
            feats[24:32] = zeros
            target = feats[0:FEATURES, :].astype(bf16)
            blank = jnp.zeros((FEATURES, LEAF), bf16)
            for leaf in range(LEAF_DEV):
                piece = target[:, LEAF * leaf : LEAF * leaf + LEAF]
                targets[leaf, 0:FEATURES, 0:LEAF] = piece
                targets[leaf, 0:FEATURES, LEAF:] = blank
                targets[leaf, FEATURES:, 0:LEAF] = blank
                targets[leaf, FEATURES:, LEAF:] = piece

    for leaf in range(LEAF_DEV):
        near_out[leaf] = 0.5 * own[0:RHS, LEAF * leaf : LEAF * leaf + LEAF]

    def one_block(entry):
        leaf = work[0, entry]
        source = work[1, entry]
        uses = work[2, entry].astype(f32)
        start = pl.multiple_of(source * LEAF, LEAF)
        both = lax.dot_general(
            sources[pl.ds(start, LEAF), :],
            targets[leaf],
            (((1,), (0,)), ((), ())),
            preferred_element_type=f32,
        )
        inverse = lax.rsqrt(both[:, :LEAF])
        block = both[:, LEAF:] * (inverse * inverse * inverse)
        block_high = block.astype(bf16)
        block_low = (block - block_high.astype(f32)).astype(bf16)
        dens = dens_parts[source]
        first = lax.dot_general(dens, block_high, (((1,), (0,)), ((), ())), preferred_element_type=f32)
        second = lax.dot_general(dens[:RHS], block_low, (((1,), (0,)), ((), ())), preferred_element_type=f32)
        return leaf, uses * (first[:RHS] + first[RHS:] + second)

    def two_blocks(step, carry):
        leaf_a, term_a = one_block(2 * step)
        leaf_b, term_b = one_block(2 * step + 1)
        near_out[leaf_a] = near_out[leaf_a] + term_a
        near_out[leaf_b] = near_out[leaf_b] + term_b
        return carry

    lax.fori_loop(0, (count + 1) // 2, two_blocks, 0)

    for side in range(3):
        for c in range(LEAF_DEV):
            split_leaf[LEAF_DEV * side + c] = unpack(halo[side][COEF_ROW:, 128 * c : 128 * c + 128])
        for m in range(MID_DEV):
            lanes = slice(128 * (LEAF_DEV + m), 128 * (LEAF_DEV + m) + 128)
            split_mid[MID_DEV * side + m] = unpack(halo[side][COEF_ROW:, lanes])
    first_mid = first_leaf // 2
    for t in range(LEAF_DEV):
        for chunk in range(CHUNKS):
            rows[8 * chunk : 8 * chunk + ADM_LEAF, :] = couple_leaf[t, :, 128 * chunk : 128 * chunk + 128]
        lhs = jnp.concatenate([rows[pl.ds(a, CHUNKS, stride=8), :] for a in range(ADM_LEAF)], axis=0)
        rhs = jnp.concatenate(
            [split_leaf[adm_leaf[t, a] - first_leaf + LEAF_DEV] for a in range(ADM_LEAF)], axis=0
        )
        leaf_couple[t] = fold(dot(lhs, rhs, 0, 0))
    for t in range(MID_DEV):
        for chunk in range(CHUNKS):
            rows[8 * chunk : 8 * chunk + ADM_MID, :] = couple_mid[t, :, 128 * chunk : 128 * chunk + 128]
        lhs = jnp.concatenate([rows[pl.ds(a, CHUNKS, stride=8), :] for a in range(ADM_MID)], axis=0)
        rhs = jnp.concatenate(
            [split_mid[adm_mid[t, a] - first_mid + MID_DEV] for a in range(ADM_MID)], axis=0
        )
        mid_couple[t] = fold(dot(lhs, rhs, 0, 0))

    for chunk in range(CHUNKS):
        rows[16 * chunk : 16 * chunk + ADM_TOP, :] = couple_top[0, :, 128 * chunk : 128 * chunk + 128]
    for group in range(4):
        stack = jnp.concatenate(
            [rows[pl.ds(4 * group + a, CHUNKS, stride=16), :] for a in range(4)], axis=0
        )
        top_mats[:, 128 * group : 128 * group + 128] = jnp.transpose(stack)
    for source, result, number in ((down_mid, mid_mats, MID_DEV), (down_leaf, leaf_mats, LEAF_DEV)):
        for chunk in range(CHUNKS):
            rows[8 * chunk : 8 * chunk + number, :] = source[:, 128 * chunk : 128 * chunk + 128]
        for c in range(number):
            wide = rows[pl.ds(c, CHUNKS, stride=8), :]
            swapped = jnp.concatenate([wide[:, RANK:], wide[:, :RANK]], axis=1)
            natural[pl.ds(0, HALF, stride=2), :] = wide
            natural[pl.ds(1, HALF, stride=2), :] = swapped
            result[c] = jnp.transpose(natural[...])[:RANK]


def near_call(near_list, near_count, adm_leaf, adm_mid, own, low, high, couple_leaf, couple_mid, couple_top, down_mid, down_leaf):
    return pl.pallas_call(
        near_kernel,
        name="near_and_couplings",
        out_shape=(
            jax.ShapeDtypeStruct((LEAF_DEV, RHS, LEAF), f32),
            jax.ShapeDtypeStruct((LEAF_DEV, RANK, RHS), f32),
            jax.ShapeDtypeStruct((MID_DEV, RANK, RHS), f32),
            jax.ShapeDtypeStruct((128, ADM_TOP * HALF), f32),
            jax.ShapeDtypeStruct((MID_DEV, RANK, RANK), f32),
            jax.ShapeDtypeStruct((LEAF_DEV, RANK, RANK), f32),
        ),
        in_specs=[SMEM] * 4 + [VMEM] * 8,
        out_specs=(VMEM,) * 6,
        scratch_shapes=[
            pltpu.VMEM((2 * FEATURES, SPAN), f32),
            pltpu.VMEM((3 * SPAN, 2 * FEATURES), bf16),
            pltpu.VMEM((LEAF_DEV, 2 * FEATURES, 2 * LEAF), bf16),
            pltpu.VMEM((3 * LEAF_DEV, 2 * RHS, LEAF), bf16),
            pltpu.VMEM((3 * LEAF_DEV, HALF, HALF), f32),
            pltpu.VMEM((3 * MID_DEV, HALF, HALF), f32),
            pltpu.VMEM((16 * CHUNKS, 128), f32),
            pltpu.VMEM((RANK, 128), f32),
            pltpu.SMEM((3, LEAF_DEV * NEAR + 8), jnp.int32),
        ],
        compiler_params=pltpu.CompilerParams(vmem_limit_bytes=32 * 1024 * 1024),
        cost_estimate=pl.CostEstimate(flops=4_000_000_000, bytes_accessed=2_000_000, transcendentals=2_000_000),
    )(near_list, near_count, adm_leaf, adm_mid, own, low, high, couple_leaf, couple_mid, couple_top, down_mid, down_leaf)


def down_kernel(
    adm_top,
    near_list,
    own_tops,
    other_tops,
    near_part,
    leaf_couple,
    mid_couple,
    top_mats,
    mid_mats,
    leaf_mats,
    row_basis,
    out,
    tiles,
    sems,
):
    core = (near_list[0, 0] // LEAF_DEV) % 2
    for a in range(ADM_TOP):
        top = adm_top[0, a]
        mine = top % 2 == core
        row = top // 2

        @pl.when(mine)
        def _():
            pltpu.make_async_copy(own_tops.at[row], tiles.at[a], sems.at[a]).start()

        @pl.when(jnp.logical_not(mine))
        def _():
            pltpu.make_async_copy(other_tops.at[row], tiles.at[a], sems.at[a]).start()

    for a in range(ADM_TOP):
        pltpu.make_async_copy(own_tops.at[0], tiles.at[a], sems.at[a]).wait()
    chosen = jnp.concatenate([unpack(tiles[a]) for a in range(ADM_TOP)], axis=0)
    top_field = fold(dot(top_mats[...], chosen))
    for m in range(MID_DEV):
        mid_field = mid_couple[m] + dot(mid_mats[m], top_field)
        for c in (2 * m, 2 * m + 1):
            leaf_field = leaf_couple[c] + dot(leaf_mats[c], mid_field)
            cols = slice(LEAF * c, LEAF * c + LEAF)
            out[:, cols] = near_part[c] + dot(leaf_field, row_basis[:, cols], 0, 0)


def down_call(adm_top, near_list, own_tops, other_tops, *rest):
    return pl.pallas_call(
        down_kernel,
        name="down_sweep",
        out_shape=jax.ShapeDtypeStruct((RHS, SPAN), f32),
        in_specs=[SMEM] * 2 + [ANY] * 2 + [VMEM] * 7,
        out_specs=VMEM,
        scratch_shapes=[pltpu.VMEM((ADM_TOP, 8, 128), f32), pltpu.SemaphoreType.DMA((ADM_TOP,))],
        cost_estimate=pl.CostEstimate(flops=10_000_000, bytes_accessed=800_000, transcendentals=0),
    )(adm_top, near_list, own_tops, other_tops, *rest)


def solution(mesh):
    devices = mesh.devices.size
    cores = 2
    ring = 16
    planes = devices // (cores * ring)
    along_z = [
        [(plane * ring + z) * cores + core for z in range(ring)] for plane in range(planes) for core in range(cores)
    ]
    across = [
        [(plane * ring + z) * cores + core for plane in range(planes)] for z in range(ring) for core in range(cores)
    ]

    def on_device(
        densities,
        points,
        area_normals,
        col_basis,
        row_basis,
        up_leaf,
        up_mid,
        down_leaf,
        down_mid,
        couple_leaf,
        couple_mid,
        couple_top,
        near_list,
        near_count,
        adm_leaf,
        adm_mid,
        adm_top,
    ):
        own_top, packed = up_call(densities, points, area_normals, col_basis, up_leaf, up_mid, ring)
        ring_tops = lax.all_to_all(own_top, "leaf", 0, 0, axis_index_groups=along_z, tiled=True)
        low = lax.ppermute(packed, "leaf", [(i, (i + 1) % devices) for i in range(devices)])
        high = lax.ppermute(packed, "leaf", [((i + 1) % devices, i) for i in range(devices)])
        spread = jnp.broadcast_to(ring_tops.reshape(1, ring * 8, 128), (planes, ring * 8, 128))
        core_tops = lax.all_to_all(spread, "leaf", 0, 0, axis_index_groups=across, tiled=True)
        other_tops = lax.ppermute(core_tops, "leaf", [(i, i ^ 1) for i in range(devices)])
        near_part, leaf_couple, mid_couple, top_mats, mid_mats, leaf_mats = near_call(
            near_list, near_count, adm_leaf, adm_mid, packed, low, high, couple_leaf, couple_mid, couple_top, down_mid, down_leaf
        )
        return down_call(
            adm_top,
            near_list,
            core_tops.reshape(planes * ring, 8, 128),
            other_tops.reshape(planes * ring, 8, 128),
            near_part,
            leaf_couple,
            mid_couple,
            top_mats,
            mid_mats,
            leaf_mats,
            row_basis,
        )

    split_last = P(None, "leaf")
    split_first = P("leaf", None)
    split_three = P("leaf", None, None)
    return jax.shard_map(
        on_device,
        mesh=mesh,
        in_specs=(split_last,) * 5
        + (split_first,) * 4
        + (split_three,) * 3
        + (split_first, P("leaf"), split_first, split_first, split_first),
        out_specs=split_last,
        check_vma=False,
    )
```

time: 239 us -> 88.6 us (0.37)
  the two profiles are of different devices: /device:TPU:1 before, /device:TPU:8 now
where the time goes in v1:
time: 88.6 us; the launch traced here: 88.2 us
  blocking collectives  48.9 us (55%)
  Pallas kernels  16.6 us (19%)
  starting transfers between devices  9.1 us (10%)
  waiting for transfers between devices  8.1 us (9%)
  local copies, waits for them, and re-layouts  5.37 us (6%)
    all_to_all x1, blocking collectives, on_device(): lax.all_to_all(own_top, 'leaf', 0, 0, axis_index_groups=along_z, tiled=True)  27.9 us
    all_to_all x1, blocking collectives, on_device(): lax.all_to_all(spread, 'leaf', 0, 0, axis_index_groups=across, tiled=True)  21 us
    pallas_call x1, Pallas kernels, near_call(): pl.pallas_call(near_kernel, name='near_and_couplings', out_shape=(jax.Sha...  9.34 us
    ppermute x1, waiting for transfers between devices, on_device(): lax.ppermute(packed, 'leaf', [(i, (i + 1) % devices) for i in range(devic...  8.01 us
    unnamed x38, local copies, waits for them, and re-layouts  5.28 us
    ppermute x1, starting transfers between devices, on_device(): lax.ppermute(packed, 'leaf', [((i + 1) % devices, i) for i in range(devic...  5.14 us
    pallas_call x1, Pallas kernels, down_call(): pl.pallas_call(down_kernel, name='down_sweep', out_shape=jax.ShapeDtypeSt...  4.27 us
    pallas_call x1, Pallas kernels, up_call(): pl.pallas_call(up_kernel, name='up_sweep', out_shape=(jax.ShapeDtypeStruc...  2.98 us
  transfers between devices with their start and end apart: 3, of which 2 were waited for; matrix products, arithmetic and copies ran while one was open for 0% of the time, Pallas kernels for 11%

profile of v1, /device:TPU:8, one launch (start us, length us, event | category | flops | bytes accessed | tf_op | source)
XLA Modules:
  0.0 88.2 jit_solution(10588450847452716445)
XLA Ops:
  0.0 3.0 %up_sweep.1 = (f32[16,8,128]{2,1,0:T(8,128)}, f32[32,1024]{1,0:T(8,128)}) custom-call(f32[16,1024]{1,0:T(8,128)} %dens.1, f32[3,1024]{1,0:T(4,128)} %points.1, f32[3,1024]{1,0:T(4,128)} %normals.1, f32[64,1024]{1,0:T(8,128)} %col_basis.1, f32[4,4096]{1,0:T(4,128)} %up_leaf.1, f32[2,4096]{1,0:T(2,128)} %up_mid.1), custom_call_target="tpu_custom_call" | custom-call | flops 10000000 | bytes 800000 | tf_op jit(solution)/shard_map/up_sweep/pallas_call | solution.py:98
  3.0 27.9 %all_to_all.10 = f32[16,8,128]{2,1,0:T(8,128)S(1)} all-to-all(f32[16,8,128]{2,1,0:T(8,128)} %get-tuple-element.13), channel_id=1, replica_groups={{0,2,4,6,8,10,12,14,16,18,20,22,24,26,28,30},{1,3,5,7,9,11,13,15,17,19,..., dimensions={0} | all-to-all | bytes 131072 | tf_op jit(solution)/shard_map/all_to_all | solution.py:414
  30.9 0.1 broadcast_in_dim.8
  31.0 0.0 copy-start.8
  31.0 0.0 copy-start.17
  31.0 21.0 %all_to_all.11 = f32[16,128,128]{2,1,0:T(8,128)S(1)} all-to-all(f32[16,128,128]{2,1,0:T(8,128)S(1)} %broadcast_in_dim.8), channel_id=1, replica_groups={{0,32,64,96,128,160,192,224,256,288,320,352,384,416,448,480},{1,33,65,9..., dimensions={0} | all-to-all | bytes 2097152 | tf_op jit(solution)/shard_map/all_to_all | solution.py:418
  52.0 2.0 %collective-permute-start = (f32[16,128,128]{2,1,0:T(8,128)S(1)}, f32[16,128,128]{2,1,0:T(8,128)S(1)}, u32[]{:S(2)}, u32[]{:S(2)}) collective-permute-start(f32[16,128,128]{2,1,0:T(8,128)S(1)} %all_to_all.11), channel_id=1, source_target_pairs={{0,1},{1,0},{2,3},{3,2},{4,5},{5,4},{6,7},{7,6},{8,9},{9,8},{10,11... | collective-permute-start | bytes 3145736 | tf_op jit(solution)/shard_map/ppermute | solution.py:419
  54.0 0.0 copy-done.8
  54.0 5.1 %collective-permute-start.2 = (f32[32,1024]{1,0:T(8,128)S(1)}, f32[32,1024]{1,0:T(8,128)S(1)}, u32[]{:S(2)}, u32[]{:S(2)}) collective-permute-start(f32[32,1024]{1,0:T(8,128)S(1)} %copy-done.8), channel_id=1, source_target_pairs={{1,0},{2,1},{3,2},{4,3},{5,4},{6,5},{7,6},{8,7},{9,8},{10,9},{11,1... | collective-permute-start | bytes 393224 | tf_op jit(solution)/shard_map/ppermute | solution.py:416
  59.2 1.9 %collective-permute-start.1 = (f32[32,1024]{1,0:T(8,128)S(1)}, f32[32,1024]{1,0:T(8,128)S(1)}, u32[]{:S(2)}, u32[]{:S(2)}) collective-permute-start(f32[32,1024]{1,0:T(8,128)S(1)} %copy-done.8), channel_id=1, source_target_pairs={{0,1},{1,2},{2,3},{3,4},{4,5},{5,6},{6,7},{7,8},{8,9},{9,10},{10,1... | collective-permute-start | bytes 393224 | tf_op jit(solution)/shard_map/ppermute | solution.py:415
  61.1 0.1 copy.19.couple_mid
  61.3 0.0 copy-start.6
  61.3 0.0 copy-start.7
  61.3 0.0 copy-start.9
  61.3 0.0 copy-start.10
  61.3 0.0 copy-start.11
  61.3 0.0 copy-start.12
  61.3 0.0 copy-start.13
  61.4 0.2 copy.18.couple_leaf
  61.6 0.1 collective-permute-done.2.high
  61.7 8.0 %collective-permute-done.1.low = f32[32,1024]{1,0:T(8,128)S(1)} collective-permute-done((f32[32,1024]{1,0:T(8,128)S(1)}, f32[32,1024]{1,0:T(8,128)S(1)}, u32[]{:S(2)}, u32[]{:S(2)}) %collective-permute-start.1) | collective-permute-done | bytes 131104 | tf_op jit(solution)/shard_map/ppermute | solution.py:415
  69.7 0.0 copy-done.6
  69.7 9.3 %near_and_couplings.1 = (f32[4,16,256]{2,1,0:T(8,128)S(1)}, f32[4,64,16]{2,1,0:T(8,128)S(1)}, f32[2,64,16]{2,1,0:T(8,128)S(1)}, f32[128,512]{1,0:T(8,128)S(1)}, ...) custom-call(s32[4,8]{1,0:T(4,128)S(1)} %copy-done.6, s32[4]{0:T(128)S(1)} %copy-done.13, s32[4,6]{1,0:T(4,128)S(1)} %copy-done.11, ...), custom_call_target="tpu_custom_call" | custom-call | flops 4000000000 | bytes 2000000 | tf_op jit(solution)/shard_map/near_and_couplings/pallas_call | solution.py:299
  79.1 0.7 copy-done
  79.8 0.7 copy-done.1
  80.5 0.6 copy-done.2
  81.1 0.6 copy-done.3
  81.7 0.6 copy-done.4
  82.4 0.6 copy-done.5
  83.0 0.0 collective-permute-done
  83.0 1.0 %copy-done.15 = f32[16,128,128]{2,1,0:T(8,128)} copy-done((f32[16,128,128]{2,1,0:T(8,128)}, f32[16,128,128]{2,1,0:T(8,128)S(1)}, u32[]{:S(2)}) %copy-start.15) | copy-done | bytes 1048600
  84.0 4.3 %down_sweep.1 = f32[16,1024]{1,0:T(8,128)} custom-call(s32[1,16]{1,0:T(1,128)} %adm_top.1, s32[4,8]{1,0:T(4,128)} %near_list.3, f32[256,8,128]{2,1,0:T(8,128)} %bitcast.3, f32[256,8,128]{2,1,0:T(8,128)} %bitcast.4, f32[4,16,256]{2,1,0:T(8,128)} %copy-done.3, f32[4,64,16]{2,1,0:T(8,128)} %copy-done.1, f32[2,64,16]{2,1,0:T(8,128)} %copy-done.4, ...), custom_call_target="tpu_custom_call" | custom-call | flops 10000000 | bytes 800000 | tf_op jit(solution)/shard_map/down_sweep/pallas_call | solution.py:371
  (18 shorter events, 0.0 us)
Async XLA Ops:
  31.0 23.0 %copy-start.8 = (f32[32,1024]{1,0:T(8,128)S(1)}, f32[32,1024]{1,0:T(8,128)}, u32[]{:S(2)}) copy-start(f32[32,1024]{1,0:T(8,128)} %get-tuple-element.14.own) | copy-start | bytes 393220
  31.0 30.1 %copy-start.17 = (f32[2,6,4096]{2,0,1:T(2,128)S(1)}, f32[2,6,4096]{2,0,1:T(2,128)}, u32[]{:S(2)}) copy-start(f32[2,6,4096]{2,0,1:T(2,128)} %param.27) | copy-start | bytes 589828
  52.0 27.1 %copy-start.14 = (f32[16,128,128]{2,1,0:T(8,128)}, f32[16,128,128]{2,1,0:T(8,128)S(1)}, u32[]{:S(2)}) copy-start(f32[16,128,128]{2,1,0:T(8,128)S(1)} %all_to_all.11) | copy-start | bytes 3145732
  52.0 9.3 %copy-start.16 = (f32[4,6,4096]{2,0,1:T(4,128)S(1)}, f32[4,6,4096]{2,0,1:T(4,128)}, u32[]{:S(2)}) copy-start(f32[4,6,4096]{2,0,1:T(4,128)} %param.26) | copy-start | bytes 1179652
  52.0 31.0 %collective-permute-start = (f32[16,128,128]{2,1,0:T(8,128)S(1)}, f32[16,128,128]{2,1,0:T(8,128)S(1)}, u32[]{:S(2)}, u32[]{:S(2)}) collective-permute-start(f32[16,128,128]{2,1,0:T(8,128)S(1)} %all_to_all.11), channel_id=1, source_target_pairs={{0,1},{1,0},{2,3},{3,2},{4,5},{5,4},{6,7},{7,6},{8,9},{9,8},{10,11... | collective-permute-start | bytes 3145736 | tf_op jit(solution)/shard_map/ppermute | solution.py:419
  54.0 7.6 %collective-permute-start.2 = (f32[32,1024]{1,0:T(8,128)S(1)}, f32[32,1024]{1,0:T(8,128)S(1)}, u32[]{:S(2)}, u32[]{:S(2)}) collective-permute-start(f32[32,1024]{1,0:T(8,128)S(1)} %copy-done.8), channel_id=1, source_target_pairs={{1,0},{2,1},{3,2},{4,3},{5,4},{6,5},{7,6},{8,7},{9,8},{10,9},{11,1... | collective-permute-start | bytes 393224 | tf_op jit(solution)/shard_map/ppermute | solution.py:416
  59.2 10.5 %collective-permute-start.1 = (f32[32,1024]{1,0:T(8,128)S(1)}, f32[32,1024]{1,0:T(8,128)S(1)}, u32[]{:S(2)}, u32[]{:S(2)}) collective-permute-start(f32[32,1024]{1,0:T(8,128)S(1)} %copy-done.8), channel_id=1, source_target_pairs={{0,1},{1,2},{2,3},{3,4},{4,5},{5,6},{6,7},{7,8},{8,9},{9,10},{10,1... | collective-permute-start | bytes 393224 | tf_op jit(solution)/shard_map/ppermute | solution.py:415
  61.3 8.4 %copy-start.6 = (s32[4,8]{1,0:T(4,128)S(1)}, s32[4,8]{1,0:T(4,128)}, u32[]{:S(2)}) copy-start(s32[4,8]{1,0:T(4,128)} %near_list.3) | copy-start | bytes 388
  61.3 8.4 %copy-start.7 = (f32[1,16,4096]{2,1,0:T(8,128)S(1)}, f32[1,16,4096]{2,1,0:T(8,128)}, u32[]{:S(2)}) copy-start(f32[1,16,4096]{2,1,0:T(8,128)} %couple_top.1) | copy-start | bytes 786436
  61.3 8.4 %copy-start.9 = (f32[4,4096]{1,0:T(4,128)S(1)}, f32[4,4096]{1,0:T(4,128)}, u32[]{:S(2)}) copy-start(f32[4,4096]{1,0:T(4,128)} %down_leaf.1) | copy-start | bytes 196612
  61.3 8.4 %copy-start.10 = (f32[2,4096]{1,0:T(2,128)S(1)}, f32[2,4096]{1,0:T(2,128)}, u32[]{:S(2)}) copy-start(f32[2,4096]{1,0:T(2,128)} %down_mid.1) | copy-start | bytes 98308
  61.3 8.4 %copy-start.11 = (s32[4,6]{1,0:T(4,128)S(1)}, s32[4,6]{1,0:T(4,128)}, u32[]{:S(2)}) copy-start(s32[4,6]{1,0:T(4,128)} %adm_leaf.1) | copy-start | bytes 292
  61.3 8.4 %copy-start.12 = (s32[2,6]{1,0:T(2,128)S(1)}, s32[2,6]{1,0:T(2,128)}, u32[]{:S(2)}) copy-start(s32[2,6]{1,0:T(2,128)} %adm_mid.1) | copy-start | bytes 148
  61.3 8.4 %copy-start.13 = (s32[4]{0:T(128)S(1)}, s32[4]{0:T(128)}, u32[]{:S(2)}) copy-start(s32[4]{0:T(128)} %near_count.1) | copy-start | bytes 52
  79.1 0.7 copy-start
  79.8 0.7 copy-start.1
  80.5 0.6 copy-start.2
  81.1 0.6 copy-start.3
  81.7 0.6 copy-start.4
  82.4 0.6 copy-start.5
  83.0 1.0 %copy-start.15 = (f32[16,128,128]{2,1,0:T(8,128)}, f32[16,128,128]{2,1,0:T(8,128)S(1)}, u32[]{:S(2)}) copy-start(f32[16,128,128]{2,1,0:T(8,128)S(1)} %collective-permute-done) | copy-start | bytes 3145732

commit v2 on v1

--- a/solution.py
+++ b/solution.py
@@ -22,6 +22,7 @@
 FEATURES = 32
 PACKED_ROWS = 32
 COEF_ROW = 24
+VMEM_LIMIT = 16 * 1024 * 1024
 
 smooth_sq = 0.01
 four_pi = 4.0 * math.pi
@@ -31,7 +32,6 @@
 
 SMEM = pl.BlockSpec(memory_space=pltpu.SMEM)
 VMEM = pl.BlockSpec(memory_space=pltpu.VMEM)
-ANY = pl.BlockSpec(memory_space=pl.ANY)
 
 
 def dot(lhs, rhs, lhs_dim=1, rhs_dim=0):
@@ -114,6 +114,15 @@
     )(dens, points, normals, col_basis, up_leaf, up_mid)
 
 
+def two_parts(values):
+    first = values.astype(bf16)
+    return first, (values - first.astype(f32)).astype(bf16)
+
+
+def bf16_dot(lhs, rhs):
+    return lax.dot_general(lhs, rhs, (((1,), (0,)), ((), ())), preferred_element_type=f32)
+
+
 def three_parts(values):
     first = values.astype(bf16).astype(f32)
     rest = values - first
@@ -127,19 +136,18 @@
     adm_leaf,
     adm_mid,
     own,
-    low,
-    high,
+    same_chip,
+    next_chip,
     couple_leaf,
     couple_mid,
-    couple_top,
-    down_mid,
-    down_leaf,
+    leaf_mats,
+    row_basis,
+    adm_top,
+    base,
+    picks,
     near_out,
     leaf_couple,
     mid_couple,
-    top_mats,
-    mid_mats,
-    leaf_mats,
     feats,
     sources,
     targets,
@@ -147,11 +155,20 @@
     split_leaf,
     split_mid,
     rows,
-    natural,
     work,
 ):
-    halo = (low, own, high)
+    halo = (same_chip, own, next_chip)
     first_leaf = near_list[0, 0]
+    first_mid = first_leaf // 2
+    core = (first_leaf // LEAF_DEV) % 2
+
+    def held(place, number):
+        side = place // number
+        return jnp.where(core == 0, place + (2 - 2 * side) * number, place)
+
+    for a in range(ADM_TOP):
+        picks[0, a] = adm_top[0, a] // 2
+        picks[1, a] = (adm_top[0, a] % 2 == core).astype(jnp.int32)
 
     count = jnp.int32(0)
     for i in range(LEAF_DEV):
@@ -167,7 +184,7 @@
                 if other < j:
                     fresh = jnp.logical_and(fresh, jnp.logical_not(same))
             work[0, count] = jnp.int32(i)
-            work[1, count] = slots[j] - first_leaf + LEAF_DEV
+            work[1, count] = held(slots[j] - first_leaf + LEAF_DEV, LEAF_DEV)
             work[2, count] = uses
             count = count + fresh.astype(jnp.int32)
     work[0, count] = jnp.int32(0)
@@ -259,13 +276,12 @@
         for m in range(MID_DEV):
             lanes = slice(128 * (LEAF_DEV + m), 128 * (LEAF_DEV + m) + 128)
             split_mid[MID_DEV * side + m] = unpack(halo[side][COEF_ROW:, lanes])
-    first_mid = first_leaf // 2
     for t in range(LEAF_DEV):
         for chunk in range(CHUNKS):
             rows[8 * chunk : 8 * chunk + ADM_LEAF, :] = couple_leaf[t, :, 128 * chunk : 128 * chunk + 128]
         lhs = jnp.concatenate([rows[pl.ds(a, CHUNKS, stride=8), :] for a in range(ADM_LEAF)], axis=0)
         rhs = jnp.concatenate(
-            [split_leaf[adm_leaf[t, a] - first_leaf + LEAF_DEV] for a in range(ADM_LEAF)], axis=0
+            [split_leaf[held(adm_leaf[t, a] - first_leaf + LEAF_DEV, LEAF_DEV)] for a in range(ADM_LEAF)], axis=0
         )
         leaf_couple[t] = fold(dot(lhs, rhs, 0, 0))
     for t in range(MID_DEV):
@@ -273,17 +289,25 @@
             rows[8 * chunk : 8 * chunk + ADM_MID, :] = couple_mid[t, :, 128 * chunk : 128 * chunk + 128]
         lhs = jnp.concatenate([rows[pl.ds(a, CHUNKS, stride=8), :] for a in range(ADM_MID)], axis=0)
         rhs = jnp.concatenate(
-            [split_mid[adm_mid[t, a] - first_mid + MID_DEV] for a in range(ADM_MID)], axis=0
+            [split_mid[held(adm_mid[t, a] - first_mid + MID_DEV, MID_DEV)] for a in range(ADM_MID)], axis=0
         )
         mid_couple[t] = fold(dot(lhs, rhs, 0, 0))
-
+    for c in range(LEAF_DEV):
+        cols = slice(LEAF * c, LEAF * c + LEAF)
+        field = leaf_couple[c] + dot(leaf_mats[c], mid_couple[c // 2])
+        base[:, cols] = near_out[c] + dot(field, row_basis[:, cols], 0, 0)
+
+
+def matrix_kernel(couple_top, down_mid, down_leaf, row_basis, top_mats, leaf_mats, top_to_points, mid_mats, rows, natural):
     for chunk in range(CHUNKS):
         rows[16 * chunk : 16 * chunk + ADM_TOP, :] = couple_top[0, :, 128 * chunk : 128 * chunk + 128]
     for group in range(4):
         stack = jnp.concatenate(
             [rows[pl.ds(4 * group + a, CHUNKS, stride=16), :] for a in range(4)], axis=0
         )
-        top_mats[:, 128 * group : 128 * group + 128] = jnp.transpose(stack)
+        high, low = two_parts(jnp.transpose(stack))
+        top_mats[0:128, 128 * group : 128 * group + 128] = high
+        top_mats[128:, 128 * group : 128 * group + 128] = low
     for source, result, number in ((down_mid, mid_mats, MID_DEV), (down_leaf, leaf_mats, LEAF_DEV)):
         for chunk in range(CHUNKS):
             rows[8 * chunk : 8 * chunk + number, :] = source[:, 128 * chunk : 128 * chunk + 128]
@@ -293,90 +317,87 @@
             natural[pl.ds(0, HALF, stride=2), :] = wide
             natural[pl.ds(1, HALF, stride=2), :] = swapped
             result[c] = jnp.transpose(natural[...])[:RANK]
-
-
-def near_call(near_list, near_count, adm_leaf, adm_mid, own, low, high, couple_leaf, couple_mid, couple_top, down_mid, down_leaf):
+    for c in range(LEAF_DEV):
+        cols = slice(LEAF * c, LEAF * c + LEAF)
+        high, low = two_parts(dot(dot(leaf_mats[c], mid_mats[c // 2]), row_basis[:, cols], 0, 0))
+        top_to_points[0:RANK, cols] = high
+        top_to_points[RANK : 2 * RANK, cols] = high
+        top_to_points[2 * RANK :, cols] = low
+
+
+def matrix_call(*operands):
+    return pl.pallas_call(
+        matrix_kernel,
+        name="transposed_matrices",
+        out_shape=(
+            jax.ShapeDtypeStruct((256, ADM_TOP * HALF), bf16),
+            jax.ShapeDtypeStruct((LEAF_DEV, RANK, RANK), f32),
+            jax.ShapeDtypeStruct((3 * RANK, SPAN), bf16),
+        ),
+        in_specs=[VMEM] * 4,
+        out_specs=(VMEM,) * 3,
+        scratch_shapes=[
+            pltpu.VMEM((MID_DEV, RANK, RANK), f32),
+            pltpu.VMEM((16 * CHUNKS, 128), f32),
+            pltpu.VMEM((RANK, 128), f32),
+        ],
+        compiler_params=pltpu.CompilerParams(vmem_limit_bytes=VMEM_LIMIT),
+        cost_estimate=pl.CostEstimate(flops=2_000_000_000, bytes_accessed=2_000_000, transcendentals=0),
+    )(*operands)
+
+
+def near_call(near_list, near_count, adm_leaf, adm_mid, *rest):
     return pl.pallas_call(
         near_kernel,
         name="near_and_couplings",
         out_shape=(
-            jax.ShapeDtypeStruct((LEAF_DEV, RHS, LEAF), f32),
-            jax.ShapeDtypeStruct((LEAF_DEV, RANK, RHS), f32),
-            jax.ShapeDtypeStruct((MID_DEV, RANK, RHS), f32),
-            jax.ShapeDtypeStruct((128, ADM_TOP * HALF), f32),
-            jax.ShapeDtypeStruct((MID_DEV, RANK, RANK), f32),
-            jax.ShapeDtypeStruct((LEAF_DEV, RANK, RANK), f32),
+            jax.ShapeDtypeStruct((RHS, SPAN), f32),
+            jax.ShapeDtypeStruct((2, ADM_TOP), jnp.int32),
         ),
-        in_specs=[SMEM] * 4 + [VMEM] * 8,
-        out_specs=(VMEM,) * 6,
+        in_specs=[SMEM] * 4 + [VMEM] * 7 + [SMEM],
+        out_specs=(VMEM, SMEM),
         scratch_shapes=[
+            pltpu.VMEM((LEAF_DEV, RHS, LEAF), f32),
+            pltpu.VMEM((LEAF_DEV, RANK, RHS), f32),
+            pltpu.VMEM((MID_DEV, RANK, RHS), f32),
             pltpu.VMEM((2 * FEATURES, SPAN), f32),
             pltpu.VMEM((3 * SPAN, 2 * FEATURES), bf16),
             pltpu.VMEM((LEAF_DEV, 2 * FEATURES, 2 * LEAF), bf16),
             pltpu.VMEM((3 * LEAF_DEV, 2 * RHS, LEAF), bf16),
             pltpu.VMEM((3 * LEAF_DEV, HALF, HALF), f32),
             pltpu.VMEM((3 * MID_DEV, HALF, HALF), f32),
-            pltpu.VMEM((16 * CHUNKS, 128), f32),
-            pltpu.VMEM((RANK, 128), f32),
+            pltpu.VMEM((8 * CHUNKS, 128), f32),
             pltpu.SMEM((3, LEAF_DEV * NEAR + 8), jnp.int32),
         ],
-        compiler_params=pltpu.CompilerParams(vmem_limit_bytes=32 * 1024 * 1024),
+        compiler_params=pltpu.CompilerParams(vmem_limit_bytes=VMEM_LIMIT),
         cost_estimate=pl.CostEstimate(flops=4_000_000_000, bytes_accessed=2_000_000, transcendentals=2_000_000),
-    )(near_list, near_count, adm_leaf, adm_mid, own, low, high, couple_leaf, couple_mid, couple_top, down_mid, down_leaf)
-
-
-def down_kernel(
-    adm_top,
-    near_list,
-    own_tops,
-    other_tops,
-    near_part,
-    leaf_couple,
-    mid_couple,
-    top_mats,
-    mid_mats,
-    leaf_mats,
-    row_basis,
-    out,
-    tiles,
-    sems,
-):
-    core = (near_list[0, 0] // LEAF_DEV) % 2
+    )(near_list, near_count, adm_leaf, adm_mid, *rest)
+
+
+def down_kernel(picks, own_tops, other_tops, base, top_mats, top_to_points, out):
+    tiles = []
     for a in range(ADM_TOP):
-        top = adm_top[0, a]
-        mine = top % 2 == core
-        row = top // 2
-
-        @pl.when(mine)
-        def _():
-            pltpu.make_async_copy(own_tops.at[row], tiles.at[a], sems.at[a]).start()
-
-        @pl.when(jnp.logical_not(mine))
-        def _():
-            pltpu.make_async_copy(other_tops.at[row], tiles.at[a], sems.at[a]).start()
-
-    for a in range(ADM_TOP):
-        pltpu.make_async_copy(own_tops.at[0], tiles.at[a], sems.at[a]).wait()
-    chosen = jnp.concatenate([unpack(tiles[a]) for a in range(ADM_TOP)], axis=0)
-    top_field = fold(dot(top_mats[...], chosen))
-    for m in range(MID_DEV):
-        mid_field = mid_couple[m] + dot(mid_mats[m], top_field)
-        for c in (2 * m, 2 * m + 1):
-            leaf_field = leaf_couple[c] + dot(leaf_mats[c], mid_field)
-            cols = slice(LEAF * c, LEAF * c + LEAF)
-            out[:, cols] = near_part[c] + dot(leaf_field, row_basis[:, cols], 0, 0)
-
-
-def down_call(adm_top, near_list, own_tops, other_tops, *rest):
+        row = picks[0, a]
+        tiles.append(jnp.where(picks[1, a] == 1, own_tops[row], other_tops[row]))
+    chosen = jnp.concatenate([unpack(tile) for tile in tiles], axis=0)
+    high, low = two_parts(chosen)
+    product = bf16_dot(top_mats[...], jnp.concatenate([high, low], axis=1))
+    width = 2 * RHS
+    top_field = fold(product[:128, :width] + product[:128, width:] + product[128:, :width])
+    high, low = two_parts(jnp.transpose(top_field))
+    out[...] = base[...] + bf16_dot(jnp.concatenate([high, low, high], axis=1), top_to_points[...])
+
+
+def down_call(*operands):
     return pl.pallas_call(
         down_kernel,
         name="down_sweep",
         out_shape=jax.ShapeDtypeStruct((RHS, SPAN), f32),
-        in_specs=[SMEM] * 2 + [ANY] * 2 + [VMEM] * 7,
+        in_specs=[SMEM] + [VMEM] * 5,
         out_specs=VMEM,
-        scratch_shapes=[pltpu.VMEM((ADM_TOP, 8, 128), f32), pltpu.SemaphoreType.DMA((ADM_TOP,))],
+        compiler_params=pltpu.CompilerParams(vmem_limit_bytes=VMEM_LIMIT),
         cost_estimate=pl.CostEstimate(flops=10_000_000, bytes_accessed=800_000, transcendentals=0),
-    )(adm_top, near_list, own_tops, other_tops, *rest)
+    )(*operands)
 
 
 def solution(mesh):
@@ -411,27 +432,39 @@
         adm_top,
     ):
         own_top, packed = up_call(densities, points, area_normals, col_basis, up_leaf, up_mid, ring)
+        own_top, couple_top, down_mid, down_leaf = lax.optimization_barrier((own_top, couple_top, down_mid, down_leaf))
         ring_tops = lax.all_to_all(own_top, "leaf", 0, 0, axis_index_groups=along_z, tiled=True)
-        low = lax.ppermute(packed, "leaf", [(i, (i + 1) % devices) for i in range(devices)])
-        high = lax.ppermute(packed, "leaf", [((i + 1) % devices, i) for i in range(devices)])
+        same_chip = lax.ppermute(packed, "leaf", [(i, i ^ 1) for i in range(devices)])
+        next_chip = lax.ppermute(packed, "leaf", [(i, ((i + 1) ^ 1) - 1) for i in range(1, devices - 1)])
+        top_mats, leaf_mats, top_to_points = matrix_call(couple_top, down_mid, down_leaf, row_basis)
+        ring_tops, same_chip, next_chip, top_mats, leaf_mats, top_to_points = lax.optimization_barrier(
+            (ring_tops, same_chip, next_chip, top_mats, leaf_mats, top_to_points)
+        )
         spread = jnp.broadcast_to(ring_tops.reshape(1, ring * 8, 128), (planes, ring * 8, 128))
         core_tops = lax.all_to_all(spread, "leaf", 0, 0, axis_index_groups=across, tiled=True)
+        base, picks = near_call(
+            near_list,
+            near_count,
+            adm_leaf,
+            adm_mid,
+            packed,
+            same_chip,
+            next_chip,
+            couple_leaf,
+            couple_mid,
+            leaf_mats,
+            row_basis,
+            adm_top,
+        )
+        core_tops, base, picks = lax.optimization_barrier((core_tops, base, picks))
         other_tops = lax.ppermute(core_tops, "leaf", [(i, i ^ 1) for i in range(devices)])
-        near_part, leaf_couple, mid_couple, top_mats, mid_mats, leaf_mats = near_call(
-            near_list, near_count, adm_leaf, adm_mid, packed, low, high, couple_leaf, couple_mid, couple_top, down_mid, down_leaf
-        )
         return down_call(
-            adm_top,
-            near_list,
+            picks,
             core_tops.reshape(planes * ring, 8, 128),
             other_tops.reshape(planes * ring, 8, 128),
-            near_part,
-            leaf_couple,
-            mid_couple,
+            base,
             top_mats,
-            mid_mats,
-            leaf_mats,
-            row_basis,
+            top_to_points,
         )
 
     split_last = P(None, "leaf")

time: 88.6 us -> 63.6 us (0.72)
  the two profiles are of different devices: /device:TPU:8 before, /device:TPU:1 now
where the time goes in v2:
time: 63.6 us; the launch traced here: 63.1 us
  starting transfers between devices  34.5 us (54%)
  Pallas kernels  13.7 us (22%)
  waiting for transfers between devices  11 us (17%)
  local copies, waits for them, and re-layouts  3.73 us (6%)
    all_to_all x1, starting transfers between devices, on_device(): lax.all_to_all(own_top, 'leaf', 0, 0, axis_index_groups=along_z, tiled=True)  15.9 us
    pallas_call x1, Pallas kernels, near_call(): pl.pallas_call(near_kernel, name='near_and_couplings', out_shape=(jax.Sha...  7.65 us
    all_to_all x1, starting transfers between devices, on_device(): lax.all_to_all(spread, 'leaf', 0, 0, axis_index_groups=across, tiled=True)  6.89 us
    all_to_all x1, waiting for transfers between devices, on_device(): lax.all_to_all(spread, 'leaf', 0, 0, axis_index_groups=across, tiled=True)  5.4 us
    ppermute x1, starting transfers between devices, on_device(): lax.ppermute(core_tops, 'leaf', [(i, i ^ 1) for i in range(devices)])  5.4 us
    ppermute x1, starting transfers between devices, on_device(): lax.ppermute(packed, 'leaf', [(i, (i + 1 ^ 1) - 1) for i in range(1, devi...  4.39 us
    all_to_all x1, waiting for transfers between devices, on_device(): lax.all_to_all(own_top, 'leaf', 0, 0, axis_index_groups=along_z, tiled=True)  3.33 us
    pallas_call x1, Pallas kernels, up_call(): pl.pallas_call(up_kernel, name='up_sweep', out_shape=(jax.ShapeDtypeStruc...  3.03 us
  transfers between devices with their start and end apart: 5, of which 3 were waited for; matrix products, arithmetic and copies ran while one was open for 1% of the time, Pallas kernels for 14%

profile of v2, /device:TPU:1, one launch (start us, length us, event | category | flops | bytes accessed | tf_op | source)
XLA Modules:
  0.0 63.1 jit_solution(16136146640087926263)
XLA Ops:
  0.0 3.0 %up_sweep.1 = (f32[16,8,128]{2,1,0:T(8,128)}, f32[32,1024]{1,0:T(8,128)}) custom-call(f32[16,1024]{1,0:T(8,128)} %dens.1, f32[3,1024]{1,0:T(4,128)} %points.1, f32[3,1024]{1,0:T(4,128)} %normals.1, f32[64,1024]{1,0:T(8,128)} %col_basis.1, f32[4,4096]{1,0:T(4,128)} %up_leaf.1, f32[2,4096]{1,0:T(2,128)} %up_mid.1), custom_call_target="tpu_custom_call" | custom-call | flops 10000000 | bytes 800000 | tf_op jit(solution)/shard_map/up_sweep/pallas_call | solution.py:98
  3.0 15.9 %all-to-all-start = ((f32[16,8,128]{2,1,0:T(8,128)}), f32[16,8,128]{2,1,0:T(8,128)S(1)}, u32[]{:S(2)}, u32[]{:S(2)}) async-start(f32[16,8,128]{2,1,0:T(8,128)} %get-tuple-element.26), calls=%async_computation | async-start | bytes 131072 | tf_op jit(solution)/shard_map/all_to_all | solution.py:436
  18.9 4.4 %collective-permute-start.1 = (f32[32,1024]{1,0:T(8,128)}, f32[32,1024]{1,0:T(8,128)S(1)}, u32[]{:S(2)}, u32[]{:S(2)}) collective-permute-start(f32[32,1024]{1,0:T(8,128)} %get-tuple-element.27.own), channel_id=1, source_target_pairs={{1,2},{2,1},{3,4},{4,3},{5,6},{6,5},{7,8},{8,7},{9,10},{10,9},{11,... | collective-permute-start | bytes 393224 | tf_op jit(solution)/shard_map/ppermute | solution.py:438
  23.3 1.9 %collective-permute-start = (f32[32,1024]{1,0:T(8,128)}, f32[32,1024]{1,0:T(8,128)S(1)}, u32[]{:S(2)}, u32[]{:S(2)}) collective-permute-start(f32[32,1024]{1,0:T(8,128)} %get-tuple-element.27.own), channel_id=1, source_target_pairs={{0,1},{1,0},{2,3},{3,2},{4,5},{5,4},{6,7},{7,6},{8,9},{9,8},{10,11... | collective-permute-start | bytes 393224 | tf_op jit(solution)/shard_map/ppermute | solution.py:437
  25.2 0.0 copy-done
  25.3 0.0 copy-done.1
  25.3 0.0 copy-done.3
  25.3 0.0 copy-start.4
  25.3 0.7 %copy-done.4 = f32[2,4096]{1,0:T(2,128)S(1)} copy-done((f32[2,4096]{1,0:T(2,128)S(1)}, f32[2,4096]{1,0:T(2,128)}, u32[]{:S(2)}) %copy-start.4) | copy-done | bytes 32792
  26.0 1.1 %transposed_matrices.1 = (bf16[256,512]{1,0:T(8,128)(2,1)S(1)}, f32[4,64,64]{2,1,0:T(8,128)S(1)}, bf16[192,1024]{1,0:T(8,128)(2,1)S(1)}) custom-call(f32[1,16,4096]{2,1,0:T(8,128)S(1)} %copy-done, f32[2,4096]{1,0:T(2,128)S(1)} %copy-done.4, f32[4,4096]{1,0:T(4,128)S(1)} %copy-done.3, f32[64,1024]{1,0:T(8,128)S(1)} %copy-done.1), custom_call_target="tpu_custom_call" | custom-call | flops 2000000000 | bytes 2000000 | tf_op jit(solution)/shard_map/transposed_matrices/pallas_call | solution.py:329
  27.1 0.0 collective-permute-done.1.next_chip
  27.2 0.0 collective-permute-done.same_chip
  27.2 3.3 %all-to-all-done = f32[16,8,128]{2,1,0:T(8,128)S(1)} async-done(((f32[16,8,128]{2,1,0:T(8,128)}), f32[16,8,128]{2,1,0:T(8,128)S(1)}, u32[]{:S(2)}, u32[]{:S(2)}) %all-to-all-start) | async-done | bytes 65568 | tf_op jit(solution)/shard_map/all_to_all | solution.py:436
  30.5 1.1 %broadcast_in_dim.8 = f32[16,128,128]{2,1,0:T(8,128)} broadcast(f32[128,128]{1,0:T(8,128)S(1)} %bitcast.5), dimensions={1,2} | broadcast | bytes 1114112 | tf_op jit(solution)/shard_map/broadcast_in_dim | solution.py:443
  31.6 6.9 %all-to-all-start.1 = ((f32[16,128,128]{2,1,0:T(8,128)}), f32[16,128,128]{2,1,0:T(8,128)S(1)}, u32[]{:S(2)}, u32[]{:S(2)}) async-start(f32[16,128,128]{2,1,0:T(8,128)} %broadcast_in_dim.8), calls=%async_computation.1 | async-start | bytes 2097152 | tf_op jit(solution)/shard_map/all_to_all | solution.py:444
  38.5 0.0 copy-done.11
  38.5 0.0 copy-start.10
  38.5 0.1 copy.19.couple_mid
  38.6 0.9 %copy-done.10 = f32[4,6,4096]{2,0,1:T(4,128)S(1)} copy-done((f32[4,6,4096]{2,0,1:T(4,128)S(1)}, f32[4,6,4096]{2,0,1:T(4,128)}, u32[]{:S(2)}) %copy-start.10) | copy-done | bytes 393240
  39.5 0.0 copy-start.8
  39.5 0.0 copy-start.9
  39.5 0.2 copy.18.couple_leaf
  39.8 0.6 copy-done.2
  40.4 0.0 copy-done.5
  40.4 0.0 copy-done.6
  40.4 0.0 copy-done.7
  40.4 0.0 copy-done.8
  40.4 7.7 %near_and_couplings.1 = (f32[16,1024]{1,0:T(8,128)S(1)}, s32[2,16]{1,0:T(2,128)S(1)}) custom-call(s32[4,8]{1,0:T(4,128)S(1)} %copy-done.5, s32[4]{0:T(128)S(1)} %copy-done.8, s32[4,6]{1,0:T(4,128)S(1)} %copy-done.6, s32[2,6]{1,0:T(2,128)S(1)} %copy-done.7, f32[32,1024]{1,0:T(8,128)S(1)} %copy-done.2, f32[32,1024]{1,0:T(8,128)S(1)} %collective-permute-done.same_chip, ...), custom_call_target="tpu_custom_call" | custom-call | flops 4000000000 | bytes 2000000 | tf_op jit(solution)/shard_map/near_and_couplings/pallas_call | solution.py:350
  48.1 5.4 %all-to-all-done.1 = f32[16,128,128]{2,1,0:T(8,128)S(1)} async-done(((f32[16,128,128]{2,1,0:T(8,128)}), f32[16,128,128]{2,1,0:T(8,128)S(1)}, u32[]{:S(2)}, u32[]{:S(2)}) %all-to-all-start.1) | async-done | bytes 1048608 | tf_op jit(solution)/shard_map/all_to_all | solution.py:444
  53.5 5.4 %collective-permute-start.2 = (f32[16,128,128]{2,1,0:T(8,128)S(1)}, f32[16,128,128]{2,1,0:T(8,128)S(1)}, u32[]{:S(2)}, u32[]{:S(2)}) collective-permute-start(f32[16,128,128]{2,1,0:T(8,128)S(1)} %all-to-all-done.1), channel_id=1, source_target_pairs={{0,1},{1,0},{2,3},{3,2},{4,5},{5,4},{6,7},{7,6},{8,9},{9,8},{10,11... | collective-permute-start | bytes 3145736 | tf_op jit(solution)/shard_map/ppermute | solution.py:460
  58.9 2.3 %collective-permute-done.2 = f32[16,128,128]{2,1,0:T(8,128)S(1)} collective-permute-done((f32[16,128,128]{2,1,0:T(8,128)S(1)}, f32[16,128,128]{2,1,0:T(8,128)S(1)}, u32[]{:S(2)}, u32[]{:S(2)}) %collective-permute-start.2) | collective-permute-done | bytes 1048608 | tf_op jit(solution)/shard_map/ppermute | solution.py:460
  61.2 1.9 %down_sweep.1 = f32[16,1024]{1,0:T(8,128)} custom-call(s32[2,16]{1,0:T(2,128)S(1)} %get-tuple-element.40.picks, f32[256,8,128]{2,1,0:T(8,128)S(1)} %bitcast.3, f32[256,8,128]{2,1,0:T(8,128)S(1)} %bitcast.4, f32[16,1024]{1,0:T(8,128)S(1)} %get-tuple-element.42.base, bf16[256,512]{1,0:T(8,128)(2,1)S(1)} %get-tuple-element.43.top_mats, ...), custom_call_target="tpu_custom_call" | custom-call | flops 10000000 | bytes 800000 | tf_op jit(solution)/shard_map/down_sweep/pallas_call | solution.py:392
  (9 shorter events, 0.0 us)
Async XLA Ops:
  0.0 25.2 %copy-start = (f32[1,16,4096]{2,1,0:T(8,128)S(1)}, f32[1,16,4096]{2,1,0:T(8,128)}, u32[]{:S(2)}) copy-start(f32[1,16,4096]{2,1,0:T(8,128)} %couple_top) | copy-start | bytes 786436
  0.0 25.3 %copy-start.1 = (f32[64,1024]{1,0:T(8,128)S(1)}, f32[64,1024]{1,0:T(8,128)}, u32[]{:S(2)}) copy-start(f32[64,1024]{1,0:T(8,128)} %row_basis.3) | copy-start | bytes 786436
  3.0 22.2 %copy-start.3 = (f32[4,4096]{1,0:T(4,128)S(1)}, f32[4,4096]{1,0:T(4,128)}, u32[]{:S(2)}) copy-start(f32[4,4096]{1,0:T(4,128)} %down_leaf) | copy-start | bytes 196612
  3.0 27.5 %all-to-all-start = ((f32[16,8,128]{2,1,0:T(8,128)}), f32[16,8,128]{2,1,0:T(8,128)S(1)}, u32[]{:S(2)}, u32[]{:S(2)}) async-start(f32[16,8,128]{2,1,0:T(8,128)} %get-tuple-element.26), calls=%async_computation | async-start | bytes 131072 | tf_op jit(solution)/shard_map/all_to_all | solution.py:436
  18.9 8.2 %collective-permute-start.1 = (f32[32,1024]{1,0:T(8,128)}, f32[32,1024]{1,0:T(8,128)S(1)}, u32[]{:S(2)}, u32[]{:S(2)}) collective-permute-start(f32[32,1024]{1,0:T(8,128)} %get-tuple-element.27.own), channel_id=1, source_target_pairs={{1,2},{2,1},{3,4},{4,3},{5,6},{6,5},{7,8},{8,7},{9,10},{10,9},{11,... | collective-permute-start | bytes 393224 | tf_op jit(solution)/shard_map/ppermute | solution.py:438
  23.3 3.8 %collective-permute-start = (f32[32,1024]{1,0:T(8,128)}, f32[32,1024]{1,0:T(8,128)S(1)}, u32[]{:S(2)}, u32[]{:S(2)}) collective-permute-start(f32[32,1024]{1,0:T(8,128)} %get-tuple-element.27.own), channel_id=1, source_target_pairs={{0,1},{1,0},{2,3},{3,2},{4,5},{5,4},{6,7},{7,6},{8,9},{9,8},{10,11... | collective-permute-start | bytes 393224 | tf_op jit(solution)/shard_map/ppermute | solution.py:437
  25.3 0.8 %copy-start.4 = (f32[2,4096]{1,0:T(2,128)S(1)}, f32[2,4096]{1,0:T(2,128)}, u32[]{:S(2)}) copy-start(f32[2,4096]{1,0:T(2,128)} %down_mid) | copy-start | bytes 98308
  31.6 6.9 %copy-start.11 = (f32[2,6,4096]{2,0,1:T(2,128)S(1)}, f32[2,6,4096]{2,0,1:T(2,128)}, u32[]{:S(2)}) copy-start(f32[2,6,4096]{2,0,1:T(2,128)} %param.27) | copy-start | bytes 589828
  31.6 21.9 %all-to-all-start.1 = ((f32[16,128,128]{2,1,0:T(8,128)}), f32[16,128,128]{2,1,0:T(8,128)S(1)}, u32[]{:S(2)}, u32[]{:S(2)}) async-start(f32[16,128,128]{2,1,0:T(8,128)} %broadcast_in_dim.8), calls=%async_computation.1 | async-start | bytes 2097152 | tf_op jit(solution)/shard_map/all_to_all | solution.py:444
  38.5 1.0 %copy-start.10 = (f32[4,6,4096]{2,0,1:T(4,128)S(1)}, f32[4,6,4096]{2,0,1:T(4,128)}, u32[]{:S(2)}) copy-start(f32[4,6,4096]{2,0,1:T(4,128)} %param.26) | copy-start | bytes 1179652
  39.5 0.9 %copy-start.2 = (f32[32,1024]{1,0:T(8,128)S(1)}, f32[32,1024]{1,0:T(8,128)}, u32[]{:S(2)}) copy-start(f32[32,1024]{1,0:T(8,128)} %get-tuple-element.27.own) | copy-start | bytes 393220
  39.5 0.9 %copy-start.5 = (s32[4,8]{1,0:T(4,128)S(1)}, s32[4,8]{1,0:T(4,128)}, u32[]{:S(2)}) copy-start(s32[4,8]{1,0:T(4,128)} %near_list.1) | copy-start | bytes 388
  39.5 0.9 %copy-start.6 = (s32[4,6]{1,0:T(4,128)S(1)}, s32[4,6]{1,0:T(4,128)}, u32[]{:S(2)}) copy-start(s32[4,6]{1,0:T(4,128)} %adm_leaf.1) | copy-start | bytes 292
  39.5 0.9 %copy-start.7 = (s32[2,6]{1,0:T(2,128)S(1)}, s32[2,6]{1,0:T(2,128)}, u32[]{:S(2)}) copy-start(s32[2,6]{1,0:T(2,128)} %adm_mid.1) | copy-start | bytes 148
  39.5 0.9 %copy-start.8 = (s32[4]{0:T(128)S(1)}, s32[4]{0:T(128)}, u32[]{:S(2)}) copy-start(s32[4]{0:T(128)} %near_count.1) | copy-start | bytes 52
  39.5 0.9 %copy-start.9 = (s32[1,16]{1,0:T(1,128)S(1)}, s32[1,16]{1,0:T(1,128)}, u32[]{:S(2)}) copy-start(s32[1,16]{1,0:T(1,128)} %adm_top.1) | copy-start | bytes 196
  53.5 7.7 %collective-permute-start.2 = (f32[16,128,128]{2,1,0:T(8,128)S(1)}, f32[16,128,128]{2,1,0:T(8,128)S(1)}, u32[]{:S(2)}, u32[]{:S(2)}) collective-permute-start(f32[16,128,128]{2,1,0:T(8,128)S(1)} %all-to-all-done.1), channel_id=1, source_target_pairs={{0,1},{1,0},{2,3},{3,2},{4,5},{5,4},{6,7},{7,6},{8,9},{9,8},{10,11... | collective-permute-start | bytes 3145736 | tf_op jit(solution)/shard_map/ppermute | solution.py:460

commit v3 on v2

--- a/solution.py
+++ b/solution.py
@@ -21,7 +21,9 @@
 CHUNKS = RANK * RANK // 128
 FEATURES = 32
 PACKED_ROWS = 32
+WANTED_ROW = 22
 COEF_ROW = 24
+GROUP = 8
 VMEM_LIMIT = 16 * 1024 * 1024
 
 smooth_sq = 0.01
@@ -62,47 +64,75 @@
     return product[:RANK, :RHS] + product[RANK:, RHS:]
 
 
-def up_kernel(dens, points, normals, col_basis, up_leaf, up_mid, top_out, packed, leaf_rows, mid_rows, leaf_t, mid_t):
-    packed[0:RHS, :] = dens[...]
-    packed[RHS : RHS + 3, :] = points[...]
-    packed[RHS + 3 : RHS + 6, :] = normals[...]
-    packed[RHS + 6 : COEF_ROW, :] = jnp.zeros((COEF_ROW - RHS - 6, SPAN), f32)
-    packed[COEF_ROW:, 6 * 128 :] = jnp.zeros((8, SPAN - 6 * 128), f32)
+def dot_parts(lhs, rhs, lhs_dim=1, rhs_dim=0):
+    lhs_high, lhs_low = two_parts(lhs)
+    rhs_high, rhs_low = two_parts(rhs)
+    return lax.dot_general(
+        jnp.concatenate([lhs_high, lhs_high, lhs_low], axis=lhs_dim),
+        jnp.concatenate([rhs_high, rhs_low, rhs_high], axis=rhs_dim),
+        (((lhs_dim,), (rhs_dim,)), ((), ())),
+        preferred_element_type=f32,
+    )
+
+
+def up_kernel(dens, col_basis, up_leaf, up_mid, top_out, coefs, leaf_rows, mid_rows, leaf_t, mid_t):
     for chunk in range(CHUNKS):
         lanes = slice(128 * chunk, 128 * chunk + 128)
         leaf_rows[8 * chunk : 8 * chunk + LEAF_DEV, :] = up_leaf[:, lanes]
         mid_rows[8 * chunk : 8 * chunk + MID_DEV, :] = up_mid[:, lanes]
     for c in range(LEAF_DEV):
         cols = slice(LEAF * c, LEAF * c + LEAF)
-        leaf_t[c, :, 0:RHS] = dot(col_basis[:, cols], dens[:, cols], 1, 1)
+        leaf_t[c, :, 0:RHS] = dot_parts(col_basis[:, cols], dens[:, cols], 1, 1)
     leaf_split = [even_odd(leaf_t, c) for c in range(LEAF_DEV)]
     for c in range(LEAF_DEV):
-        packed[COEF_ROW:, 128 * c : 128 * c + 128] = pack(leaf_split[c])
+        coefs[:, 128 * c : 128 * c + 128] = pack(leaf_split[c])
     for m in range(MID_DEV):
         pair = (2 * m, 2 * m + 1)
         lhs = jnp.concatenate([leaf_rows[pl.ds(c, CHUNKS, stride=8), :] for c in pair], axis=0)
         rhs = jnp.concatenate([leaf_split[c] for c in pair], axis=0)
-        mid_t[m, :, 0:RHS] = fold(dot(lhs, rhs, 0, 0))
+        mid_t[m, :, 0:RHS] = fold(dot_parts(lhs, rhs, 0, 0))
     mid_split = [even_odd(mid_t, m) for m in range(MID_DEV)]
     for m in range(MID_DEV):
-        packed[COEF_ROW:, 128 * (LEAF_DEV + m) : 128 * (LEAF_DEV + m) + 128] = pack(mid_split[m])
+        coefs[:, 128 * (LEAF_DEV + m) : 128 * (LEAF_DEV + m) + 128] = pack(mid_split[m])
     lhs = jnp.concatenate([mid_rows[pl.ds(m, CHUNKS, stride=8), :] for m in range(MID_DEV)], axis=0)
     rhs = jnp.concatenate(mid_split, axis=0)
-    leaf_t[0, :, 0:RHS] = fold(dot(lhs, rhs, 0, 0))
+    leaf_t[0, :, 0:RHS] = fold(dot_parts(lhs, rhs, 0, 0))
     tile = pack(even_odd(leaf_t, 0))
     for peer in range(top_out.shape[0]):
         top_out[peer] = tile
 
 
-def up_call(dens, points, normals, col_basis, up_leaf, up_mid, peers):
+def pack_kernel(dens, points, normals, coefs, adm_top, packed):
+    packed[0:RHS, :] = dens[...]
+    packed[RHS : RHS + 3, :] = points[...]
+    packed[RHS + 3 : RHS + 6, :] = normals[...]
+    packed[WANTED_ROW:COEF_ROW, :] = jnp.zeros((COEF_ROW - WANTED_ROW, SPAN), f32)
+    packed[WANTED_ROW : WANTED_ROW + 1, 0:ADM_TOP] = adm_top[...].astype(f32)
+    packed[COEF_ROW:, 0 : 6 * 128] = coefs[...]
+    packed[COEF_ROW:, 6 * 128 :] = jnp.zeros((8, SPAN - 6 * 128), f32)
+
+
+def pack_call(*operands):
+    return pl.pallas_call(
+        pack_kernel,
+        name="packed_for_neighbours",
+        out_shape=jax.ShapeDtypeStruct((PACKED_ROWS, SPAN), f32),
+        in_specs=[VMEM] * 5,
+        out_specs=VMEM,
+        compiler_params=pltpu.CompilerParams(vmem_limit_bytes=VMEM_LIMIT),
+        cost_estimate=pl.CostEstimate(flops=100_000_000, bytes_accessed=400_000, transcendentals=0),
+    )(*operands)
+
+
+def up_call(dens, col_basis, up_leaf, up_mid, peers):
     return pl.pallas_call(
         up_kernel,
         name="up_sweep",
         out_shape=(
             jax.ShapeDtypeStruct((peers, 8, 128), f32),
-            jax.ShapeDtypeStruct((PACKED_ROWS, SPAN), f32),
+            jax.ShapeDtypeStruct((8, 6 * 128), f32),
         ),
-        in_specs=[VMEM] * 6,
+        in_specs=[VMEM] * 4,
         out_specs=(VMEM, VMEM),
         scratch_shapes=[
             pltpu.VMEM((8 * CHUNKS, 128), f32),
@@ -111,7 +141,7 @@
             pltpu.VMEM((MID_DEV, RANK, 128), f32),
         ],
         cost_estimate=pl.CostEstimate(flops=10_000_000, bytes_accessed=800_000, transcendentals=0),
-    )(dens, points, normals, col_basis, up_leaf, up_mid)
+    )(dens, col_basis, up_leaf, up_mid)
 
 
 def two_parts(values):
@@ -143,9 +173,11 @@
     leaf_mats,
     row_basis,
     adm_top,
+    wanted,
     base,
-    picks,
+    plan,
     near_out,
+    near_t,
     leaf_couple,
     mid_couple,
     feats,
@@ -166,9 +198,10 @@
         side = place // number
         return jnp.where(core == 0, place + (2 - 2 * side) * number, place)
 
-    for a in range(ADM_TOP):
-        picks[0, a] = adm_top[0, a] // 2
-        picks[1, a] = (adm_top[0, a] % 2 == core).astype(jnp.int32)
+    for row, tops in ((0, adm_top), (2, wanted)):
+        for a in range(ADM_TOP):
+            plan[row, a] = tops[0, a] // 2
+            plan[row + 1, a] = (tops[0, a] % 2 == core).astype(jnp.int32)
 
     count = jnp.int32(0)
     for i in range(LEAF_DEV):
@@ -187,9 +220,10 @@
             work[1, count] = held(slots[j] - first_leaf + LEAF_DEV, LEAF_DEV)
             work[2, count] = uses
             count = count + fresh.astype(jnp.int32)
-    work[0, count] = jnp.int32(0)
-    work[1, count] = jnp.int32(0)
-    work[2, count] = jnp.int32(0)
+    for extra in range(GROUP):
+        work[0, count + extra] = jnp.int32(0)
+        work[1, count + extra] = jnp.int32(0)
+        work[2, count + extra] = jnp.int32(0)
 
     for side in range(3):
         block = halo[side]
@@ -203,25 +237,26 @@
         zeros = jnp.zeros((8, SPAN), f32)
         s1, s2, s3 = three_parts(square)
         i1, i2, i3 = three_parts(inner)
-        feats[0:8] = zeros
-        feats[24:32] = zeros
-        feats[32:40] = zeros
-        feats[56:64] = zeros
         feats[0:1], feats[1:2], feats[2:3] = s1, s2, s3
         feats[3:6] = ones
         for slot, part in enumerate((p1, p1, p2, p2, p1, p3)):
             feats[6 + 3 * slot : 9 + 3 * slot] = part * -2.0
+        feats[24:32] = zeros
+        feats[32:40] = zeros
         feats[32:33], feats[33:34], feats[34:35] = i1, i2, i3
         for slot, part in enumerate((n1, n1, n2, n2, n1, n3)):
             feats[38 + 3 * slot : 41 + 3 * slot] = part
+        feats[56:64] = zeros
         for leaf in range(LEAF_DEV):
             cols = slice(LEAF * leaf, LEAF * leaf + LEAF)
-            start = (LEAF_DEV * side + leaf) * LEAF
-            sources[start : start + LEAF, :] = jnp.transpose(feats[:, cols]).astype(bf16)
-            dens = block[0:RHS, cols]
-            dens_high = dens.astype(bf16)
-            dens_parts[LEAF_DEV * side + leaf, 0:RHS, :] = dens_high
-            dens_parts[LEAF_DEV * side + leaf, RHS:, :] = (dens - dens_high.astype(f32)).astype(bf16)
+            place_held = LEAF_DEV * side + leaf
+            sources[place_held, :, 0:LEAF] = feats[0:FEATURES, cols].astype(bf16)
+            sources[place_held, :, LEAF:] = feats[FEATURES:, cols].astype(bf16)
+            dens_high, dens_low = two_parts(block[0:RHS, cols])
+            dens_parts[place_held, 0:RHS, 0:LEAF] = dens_high
+            dens_parts[place_held, 0:RHS, LEAF:] = dens_high
+            dens_parts[place_held, RHS:, 0:LEAF] = dens_low
+            dens_parts[place_held, RHS:, LEAF:] = jnp.zeros((RHS, LEAF), bf16)
         if side == 1:
             t1, t2, t3 = three_parts(square + smooth_sq)
             feats[0:3] = ones
@@ -229,46 +264,37 @@
             for slot, part in enumerate((p1, p2, p1, p2, p3, p1)):
                 feats[6 + 3 * slot : 9 + 3 * slot] = part
             feats[24:32] = zeros
-            target = feats[0:FEATURES, :].astype(bf16)
-            blank = jnp.zeros((FEATURES, LEAF), bf16)
             for leaf in range(LEAF_DEV):
-                piece = target[:, LEAF * leaf : LEAF * leaf + LEAF]
-                targets[leaf, 0:FEATURES, 0:LEAF] = piece
-                targets[leaf, 0:FEATURES, LEAF:] = blank
-                targets[leaf, FEATURES:, 0:LEAF] = blank
-                targets[leaf, FEATURES:, LEAF:] = piece
-
-    for leaf in range(LEAF_DEV):
-        near_out[leaf] = 0.5 * own[0:RHS, LEAF * leaf : LEAF * leaf + LEAF]
+                targets[leaf] = jnp.transpose(feats[0:FEATURES, LEAF * leaf : LEAF * leaf + LEAF]).astype(bf16)
+
+    near_t[...] = jnp.zeros((LEAF_DEV, LEAF, 2 * RHS), f32)
 
     def one_block(entry):
         leaf = work[0, entry]
         source = work[1, entry]
         uses = work[2, entry].astype(f32)
-        start = pl.multiple_of(source * LEAF, LEAF)
-        both = lax.dot_general(
-            sources[pl.ds(start, LEAF), :],
-            targets[leaf],
-            (((1,), (0,)), ((), ())),
+        both = bf16_dot(targets[leaf], sources[source])
+        inverse = lax.rsqrt(both[:, :LEAF])
+        block = both[:, LEAF:] * (inverse * inverse * inverse)
+        high, low = two_parts(block)
+        term = lax.dot_general(
+            jnp.concatenate([high, low], axis=1),
+            dens_parts[source],
+            (((1,), (1,)), ((), ())),
             preferred_element_type=f32,
         )
-        inverse = lax.rsqrt(both[:, :LEAF])
-        block = both[:, LEAF:] * (inverse * inverse * inverse)
-        block_high = block.astype(bf16)
-        block_low = (block - block_high.astype(f32)).astype(bf16)
-        dens = dens_parts[source]
-        first = lax.dot_general(dens, block_high, (((1,), (0,)), ((), ())), preferred_element_type=f32)
-        second = lax.dot_general(dens[:RHS], block_low, (((1,), (0,)), ((), ())), preferred_element_type=f32)
-        return leaf, uses * (first[:RHS] + first[RHS:] + second)
-
-    def two_blocks(step, carry):
-        leaf_a, term_a = one_block(2 * step)
-        leaf_b, term_b = one_block(2 * step + 1)
-        near_out[leaf_a] = near_out[leaf_a] + term_a
-        near_out[leaf_b] = near_out[leaf_b] + term_b
+        return leaf, uses * term
+
+    def some_blocks(step, carry):
+        results = [one_block(GROUP * step + k) for k in range(GROUP)]
+        for leaf, term in results:
+            near_t[leaf] = near_t[leaf] + term
         return carry
 
-    lax.fori_loop(0, (count + 1) // 2, two_blocks, 0)
+    lax.fori_loop(0, (count + GROUP - 1) // GROUP, some_blocks, 0)
+    for leaf in range(LEAF_DEV):
+        total = jnp.transpose(near_t[leaf])
+        near_out[leaf] = 0.5 * own[0:RHS, LEAF * leaf : LEAF * leaf + LEAF] + total[:RHS] + total[RHS:]
 
     for side in range(3):
         for c in range(LEAF_DEV):
@@ -276,22 +302,18 @@
         for m in range(MID_DEV):
             lanes = slice(128 * (LEAF_DEV + m), 128 * (LEAF_DEV + m) + 128)
             split_mid[MID_DEV * side + m] = unpack(halo[side][COEF_ROW:, lanes])
-    for t in range(LEAF_DEV):
-        for chunk in range(CHUNKS):
-            rows[8 * chunk : 8 * chunk + ADM_LEAF, :] = couple_leaf[t, :, 128 * chunk : 128 * chunk + 128]
-        lhs = jnp.concatenate([rows[pl.ds(a, CHUNKS, stride=8), :] for a in range(ADM_LEAF)], axis=0)
-        rhs = jnp.concatenate(
-            [split_leaf[held(adm_leaf[t, a] - first_leaf + LEAF_DEV, LEAF_DEV)] for a in range(ADM_LEAF)], axis=0
-        )
-        leaf_couple[t] = fold(dot(lhs, rhs, 0, 0))
-    for t in range(MID_DEV):
-        for chunk in range(CHUNKS):
-            rows[8 * chunk : 8 * chunk + ADM_MID, :] = couple_mid[t, :, 128 * chunk : 128 * chunk + 128]
-        lhs = jnp.concatenate([rows[pl.ds(a, CHUNKS, stride=8), :] for a in range(ADM_MID)], axis=0)
-        rhs = jnp.concatenate(
-            [split_mid[held(adm_mid[t, a] - first_mid + MID_DEV, MID_DEV)] for a in range(ADM_MID)], axis=0
-        )
-        mid_couple[t] = fold(dot(lhs, rhs, 0, 0))
+    for couple, number, adm, split, offset, result in (
+        (couple_leaf, LEAF_DEV, adm_leaf, split_leaf, first_leaf, leaf_couple),
+        (couple_mid, MID_DEV, adm_mid, split_mid, first_mid, mid_couple),
+    ):
+        slots = couple.shape[0]
+        for a in range(slots):
+            for chunk in range(CHUNKS):
+                rows[a, 8 * chunk : 8 * chunk + number, :] = couple[a, :, 128 * chunk : 128 * chunk + 128]
+        for t in range(number):
+            lhs = jnp.concatenate([rows[a, pl.ds(t, CHUNKS, stride=8), :] for a in range(slots)], axis=0)
+            rhs = jnp.concatenate([split[held(adm[t, a] - offset + number, number)] for a in range(slots)], axis=0)
+            result[t] = fold(dot(lhs, rhs, 0, 0))
     for c in range(LEAF_DEV):
         cols = slice(LEAF * c, LEAF * c + LEAF)
         field = leaf_couple[c] + dot(leaf_mats[c], mid_couple[c // 2])
@@ -352,21 +374,22 @@
         name="near_and_couplings",
         out_shape=(
             jax.ShapeDtypeStruct((RHS, SPAN), f32),
-            jax.ShapeDtypeStruct((2, ADM_TOP), jnp.int32),
+            jax.ShapeDtypeStruct((4, ADM_TOP), jnp.int32),
         ),
-        in_specs=[SMEM] * 4 + [VMEM] * 7 + [SMEM],
+        in_specs=[SMEM] * 4 + [VMEM] * 7 + [SMEM] * 2,
         out_specs=(VMEM, SMEM),
         scratch_shapes=[
             pltpu.VMEM((LEAF_DEV, RHS, LEAF), f32),
+            pltpu.VMEM((LEAF_DEV, LEAF, 2 * RHS), f32),
             pltpu.VMEM((LEAF_DEV, RANK, RHS), f32),
             pltpu.VMEM((MID_DEV, RANK, RHS), f32),
             pltpu.VMEM((2 * FEATURES, SPAN), f32),
-            pltpu.VMEM((3 * SPAN, 2 * FEATURES), bf16),
-            pltpu.VMEM((LEAF_DEV, 2 * FEATURES, 2 * LEAF), bf16),
-            pltpu.VMEM((3 * LEAF_DEV, 2 * RHS, LEAF), bf16),
+            pltpu.VMEM((3 * LEAF_DEV, FEATURES, 2 * LEAF), bf16),
+            pltpu.VMEM((LEAF_DEV, LEAF, FEATURES), bf16),
+            pltpu.VMEM((3 * LEAF_DEV, 2 * RHS, 2 * LEAF), bf16),
             pltpu.VMEM((3 * LEAF_DEV, HALF, HALF), f32),
             pltpu.VMEM((3 * MID_DEV, HALF, HALF), f32),
-            pltpu.VMEM((8 * CHUNKS, 128), f32),
+            pltpu.VMEM((ADM_LEAF, 8 * CHUNKS, 128), f32),
             pltpu.SMEM((3, LEAF_DEV * NEAR + 8), jnp.int32),
         ],
         compiler_params=pltpu.CompilerParams(vmem_limit_bytes=VMEM_LIMIT),
@@ -374,16 +397,55 @@
     )(near_list, near_count, adm_leaf, adm_mid, *rest)
 
 
-def down_kernel(picks, own_tops, other_tops, base, top_mats, top_to_points, out):
-    tiles = []
-    for a in range(ADM_TOP):
-        row = picks[0, a]
-        tiles.append(jnp.where(picks[1, a] == 1, own_tops[row], other_tops[row]))
-    chosen = jnp.concatenate([unpack(tile) for tile in tiles], axis=0)
+def top_share(top_mats, chosen):
     high, low = two_parts(chosen)
     product = bf16_dot(top_mats[...], jnp.concatenate([high, low], axis=1))
     width = 2 * RHS
-    top_field = fold(product[:128, :width] + product[:128, width:] + product[128:, :width])
+    return fold(product[:128, :width] + product[:128, width:] + product[128:, :width])
+
+
+def held_tops(plan, row, tops):
+    return [
+        jnp.where(plan[row + 1, a] == 1, tops[plan[row, a]], jnp.zeros((8, 128), f32)) for a in range(ADM_TOP)
+    ]
+
+
+def answer_kernel(plan, own_tops, out):
+    for a, tile in enumerate(held_tops(plan, 2, own_tops)):
+        out[a] = tile
+
+
+def answer_call(plan, own_tops):
+    return pl.pallas_call(
+        answer_kernel,
+        name="answer",
+        out_shape=jax.ShapeDtypeStruct((ADM_TOP, 8, 128), f32),
+        in_specs=[SMEM, VMEM],
+        out_specs=VMEM,
+        compiler_params=pltpu.CompilerParams(vmem_limit_bytes=VMEM_LIMIT),
+        cost_estimate=pl.CostEstimate(flops=1_000_000, bytes_accessed=100_000, transcendentals=0),
+    )(plan, own_tops)
+
+
+def own_kernel(plan, own_tops, top_mats, out):
+    out[...] = top_share(top_mats, jnp.concatenate([unpack(tile) for tile in held_tops(plan, 0, own_tops)], axis=0))
+
+
+def own_call(plan, own_tops, top_mats):
+    return pl.pallas_call(
+        own_kernel,
+        name="own_tops",
+        out_shape=jax.ShapeDtypeStruct((RANK, RHS), f32),
+        in_specs=[SMEM, VMEM, VMEM],
+        out_specs=VMEM,
+        compiler_params=pltpu.CompilerParams(vmem_limit_bytes=VMEM_LIMIT),
+        cost_estimate=pl.CostEstimate(flops=400_000_000, bytes_accessed=400_000, transcendentals=0),
+    )(plan, own_tops, top_mats)
+
+
+def down_kernel(received, own_share, base, top_mats, top_to_points, out):
+    chosen = jnp.concatenate([unpack(received[a]) for a in range(ADM_TOP)], axis=0)
+    top_field = own_share[...] + top_share(top_mats, chosen)
     high, low = two_parts(jnp.transpose(top_field))
     out[...] = base[...] + bf16_dot(jnp.concatenate([high, low, high], axis=1), top_to_points[...])
 
@@ -393,7 +455,7 @@
         down_kernel,
         name="down_sweep",
         out_shape=jax.ShapeDtypeStruct((RHS, SPAN), f32),
-        in_specs=[SMEM] + [VMEM] * 5,
+        in_specs=[VMEM] * 5,
         out_specs=VMEM,
         compiler_params=pltpu.CompilerParams(vmem_limit_bytes=VMEM_LIMIT),
         cost_estimate=pl.CostEstimate(flops=10_000_000, bytes_accessed=800_000, transcendentals=0),
@@ -431,8 +493,11 @@
         adm_mid,
         adm_top,
     ):
-        own_top, packed = up_call(densities, points, area_normals, col_basis, up_leaf, up_mid, ring)
-        own_top, couple_top, down_mid, down_leaf = lax.optimization_barrier((own_top, couple_top, down_mid, down_leaf))
+        own_top, coefs = up_call(densities, col_basis, up_leaf, up_mid, ring)
+        own_top, coefs, couple_top, down_mid, down_leaf = lax.optimization_barrier(
+            (own_top, coefs, couple_top, down_mid, down_leaf)
+        )
+        packed = pack_call(densities, points, area_normals, coefs, adm_top)
         ring_tops = lax.all_to_all(own_top, "leaf", 0, 0, axis_index_groups=along_z, tiled=True)
         same_chip = lax.ppermute(packed, "leaf", [(i, i ^ 1) for i in range(devices)])
         next_chip = lax.ppermute(packed, "leaf", [(i, ((i + 1) ^ 1) - 1) for i in range(1, devices - 1)])
@@ -442,7 +507,8 @@
         )
         spread = jnp.broadcast_to(ring_tops.reshape(1, ring * 8, 128), (planes, ring * 8, 128))
         core_tops = lax.all_to_all(spread, "leaf", 0, 0, axis_index_groups=across, tiled=True)
-        base, picks = near_call(
+        wanted = same_chip[WANTED_ROW : WANTED_ROW + 1, 0:ADM_TOP].astype(jnp.int32)
+        base, plan = near_call(
             near_list,
             near_count,
             adm_leaf,
@@ -450,18 +516,22 @@
             packed,
             same_chip,
             next_chip,
-            couple_leaf,
-            couple_mid,
+            jnp.swapaxes(couple_leaf, 0, 1),
+            jnp.swapaxes(couple_mid, 0, 1),
             leaf_mats,
             row_basis,
             adm_top,
+            wanted,
         )
-        core_tops, base, picks = lax.optimization_barrier((core_tops, base, picks))
-        other_tops = lax.ppermute(core_tops, "leaf", [(i, i ^ 1) for i in range(devices)])
+        core_tops, base, plan = lax.optimization_barrier((core_tops, base, plan))
+        core_tops = core_tops.reshape(planes * ring, 8, 128)
+        answers = answer_call(plan, core_tops)
+        received = lax.ppermute(answers, "leaf", [(i, i ^ 1) for i in range(devices)])
+        answers, plan, core_tops = lax.optimization_barrier((answers, plan, core_tops))
+        own_share = own_call(plan, core_tops, top_mats)
         return down_call(
-            picks,
-            core_tops.reshape(planes * ring, 8, 128),
-            other_tops.reshape(planes * ring, 8, 128),
+            received,
+            own_share,
             base,
             top_mats,
             top_to_points,

time: 63.6 us -> 62 us (0.975)
  local copies, waits for them, and re-layouts: 3.73 us -> 1.79 us
  waiting for transfers between devices: 11 us -> 11.7 us
    all_to_all x1, waiting for transfers between devices: 5.4 us -> 7.74 us  [on_device(): lax.all_to_all(spread, 'leaf', 0, 0, axis_index_groups=across, tiled=True)]
    ppermute x1, waiting for transfers between devices: 2.26 us -> 0.01 us  [on_device(): lax.ppermute(answers, 'leaf', [(i, i ^ 1) for i in range(devices)])]
    unnamed x26 -> x30, local copies, waits for them, and re-layouts: 2.64 us -> 0.7 us
    pallas_call x0 -> x3, Pallas kernels: none -> 1.67 us  [the longest x1 1.06 us: own_call(): pl.pallas_call(own_kernel, name='own_tops', out_shape=jax.ShapeDtypeStruc...]
    pallas_call x1, Pallas kernels: 7.65 us -> 6.51 us  [near_call(): pl.pallas_call(near_kernel, name='near_and_couplings', out_shape=(jax.Sha...]
  transfers between devices with their start and end apart: 5 -> 5, of which waited for: 3 -> 3; matrix products, arithmetic and copies ran while one was open for 1% -> 0% of each run, Pallas kernels for 14% -> 14%
where the time goes in v3:
time: 62 us; the launch traced here: 61.6 us
  starting transfers between devices  34.5 us (56%)
  Pallas kernels  13.4 us (22%)
  waiting for transfers between devices  11.7 us (19%)
  local copies, waits for them, and re-layouts  1.79 us (3%)
    all_to_all x1, starting transfers between devices, on_device(): lax.all_to_all(own_top, 'leaf', 0, 0, axis_index_groups=along_z, tiled=True)  15.9 us
    all_to_all x1, waiting for transfers between devices, on_device(): lax.all_to_all(spread, 'leaf', 0, 0, axis_index_groups=across, tiled=True)  7.74 us
    all_to_all x1, starting transfers between devices, on_device(): lax.all_to_all(spread, 'leaf', 0, 0, axis_index_groups=across, tiled=True)  6.89 us
    pallas_call x1, Pallas kernels, near_call(): pl.pallas_call(near_kernel, name='near_and_couplings', out_shape=(jax.Sha...  6.51 us
    ppermute x1, starting transfers between devices, on_device(): lax.ppermute(answers, 'leaf', [(i, i ^ 1) for i in range(devices)])  5.44 us
    ppermute x1, starting transfers between devices, on_device(): lax.ppermute(packed, 'leaf', [(i, (i + 1 ^ 1) - 1) for i in range(1, devi...  4.39 us
    all_to_all x1, waiting for transfers between devices, on_device(): lax.all_to_all(own_top, 'leaf', 0, 0, axis_index_groups=along_z, tiled=True)  3.52 us
    pallas_call x1, Pallas kernels, up_call(): pl.pallas_call(up_kernel, name='up_sweep', out_shape=(jax.ShapeDtypeStruc...  2.68 us
  transfers between devices with their start and end apart: 5, of which 3 were waited for; matrix products, arithmetic and copies ran while one was open for 0% of the time, Pallas kernels for 14%

profile of v3, /device:TPU:1, one launch (start us, length us, event | category | flops | bytes accessed | tf_op | source)
XLA Modules:
  0.0 61.6 jit_solution(15696912113334216620)
XLA Ops:
  0.0 0.0 copy-start.2
  0.0 2.7 %up_sweep.1 = (f32[16,8,128]{2,1,0:T(8,128)}, f32[8,768]{1,0:T(8,128)}) custom-call(f32[16,1024]{1,0:T(8,128)} %dens.3, f32[64,1024]{1,0:T(8,128)} %col_basis.1, f32[4,4096]{1,0:T(4,128)} %up_leaf.1, f32[2,4096]{1,0:T(2,128)} %up_mid.1), custom_call_target="tpu_custom_call" | custom-call | flops 10000000 | bytes 800000 | tf_op jit(solution)/shard_map/up_sweep/pallas_call | solution.py:128
  2.7 15.9 %all-to-all-start = ((f32[16,8,128]{2,1,0:T(8,128)}), f32[16,8,128]{2,1,0:T(8,128)S(1)}, u32[]{:S(2)}, u32[]{:S(2)}) async-start(f32[16,8,128]{2,1,0:T(8,128)} %get-tuple-element.30), calls=%async_computation | async-start | bytes 131072 | tf_op jit(solution)/shard_map/all_to_all | solution.py:501
  18.6 0.0 copy-done.8
  18.6 0.0 copy-done.9
  18.6 0.0 copy-done.14
  18.6 0.0 copy-done.7
  18.7 0.0 copy-start.5
  18.7 0.0 copy-start.6
  18.7 4.4 %collective-permute-start.1 = (f32[32,1024]{1,0:T(8,128)S(1)}, f32[32,1024]{1,0:T(8,128)S(1)}, u32[]{:S(2)}, u32[]{:S(2)}) collective-permute-start(f32[32,1024]{1,0:T(8,128)S(1)} %packed_for_neighbours.1.own), channel_id=1, source_target_pairs={{1,2},{2,1},{3,4},{4,3},{5,6},{6,5},{7,8},{8,7},{9,10},{10,9},{11,... | collective-permute-start | bytes 393224 | tf_op jit(solution)/shard_map/ppermute | solution.py:503
  23.1 1.9 %collective-permute-start = (f32[32,1024]{1,0:T(8,128)S(1)}, f32[32,1024]{1,0:T(8,128)S(1)}, u32[]{:S(2)}, u32[]{:S(2)}) collective-permute-start(f32[32,1024]{1,0:T(8,128)S(1)} %packed_for_neighbours.1.own), channel_id=1, source_target_pairs={{0,1},{1,0},{2,3},{3,2},{4,5},{5,4},{6,7},{7,6},{8,9},{9,8},{10,11... | collective-permute-start | bytes 393224 | tf_op jit(solution)/shard_map/ppermute | solution.py:502
  25.1 1.1 %transposed_matrices.1 = (bf16[256,512]{1,0:T(8,128)(2,1)S(1)}, f32[4,64,64]{2,1,0:T(8,128)S(1)}, bf16[192,1024]{1,0:T(8,128)(2,1)S(1)}) custom-call(f32[1,16,4096]{2,1,0:T(8,128)S(1)} %copy-done.2, f32[2,4096]{1,0:T(2,128)S(1)} %copy-done.6, f32[4,4096]{1,0:T(4,128)S(1)} %copy-done.5, f32[64,1024]{1,0:T(8,128)S(1)} %copy-done.3), custom_call_target="tpu_custom_call" | custom-call | flops 2000000000 | bytes 2000000 | tf_op jit(solution)/shard_map/transposed_matrices/pallas_call | solution.py:351
  26.2 0.5 collective-permute-done.1.next_chip
  26.6 0.0 collective-permute-done.same_chip
  26.6 3.5 %all-to-all-done = f32[16,8,128]{2,1,0:T(8,128)S(1)} async-done(((f32[16,8,128]{2,1,0:T(8,128)}), f32[16,8,128]{2,1,0:T(8,128)S(1)}, u32[]{:S(2)}, u32[]{:S(2)}) %all-to-all-start) | async-done | bytes 65568 | tf_op jit(solution)/shard_map/all_to_all | solution.py:501
  30.2 1.1 %broadcast_in_dim.8 = f32[16,128,128]{2,1,0:T(8,128)} broadcast(f32[128,128]{1,0:T(8,128)S(1)} %bitcast.8), dimensions={1,2} | broadcast | bytes 1114112 | tf_op jit(solution)/shard_map/broadcast_in_dim | solution.py:508
  31.3 6.9 %all-to-all-start.1 = ((f32[16,128,128]{2,1,0:T(8,128)}), f32[16,128,128]{2,1,0:T(8,128)S(1)}, u32[]{:S(2)}, u32[]{:S(2)}) async-start(f32[16,128,128]{2,1,0:T(8,128)} %broadcast_in_dim.8), calls=%async_computation.1 | async-start | bytes 2097152 | tf_op jit(solution)/shard_map/all_to_all | solution.py:509
  38.2 0.0 copy-start.10
  38.2 0.0 copy-start.12
  38.2 0.0 copy-start.13
  38.2 0.0 copy-done.1
  38.2 0.0 copy-done.4
  38.2 0.0 copy-done.11
  38.2 0.6 %copy-done.10 = s32[4,8]{1,0:T(4,128)S(1)} copy-done((s32[4,8]{1,0:T(4,128)S(1)}, s32[4,8]{1,0:T(4,128)}, u32[]{:S(2)}) %copy-start.10) | copy-done | bytes 152
  38.9 0.0 copy-done.12
  38.9 6.5 %near_and_couplings.1 = (f32[16,1024]{1,0:T(8,128)S(1)}, s32[4,16]{1,0:T(4,128)S(1)}) custom-call(s32[4,8]{1,0:T(4,128)S(1)} %copy-done.10, s32[4]{0:T(128)S(1)} %copy-done.13, s32[4,6]{1,0:T(4,128)S(1)} %copy-done.11, s32[2,6]{1,0:T(2,128)S(1)} %copy-done.12, f32[32,1024]{1,0:T(8,128)S(1)} %packed_for_neighbours.1.own, ...), custom_call_target="tpu_custom_call" | custom-call | flops 4000000000 | bytes 2000000 | tf_op jit(solution)/shard_map/near_and_couplings/pallas_call | solution.py:372
  45.4 7.7 %all-to-all-done.1 = f32[16,128,128]{2,1,0:T(8,128)S(1)} async-done(((f32[16,128,128]{2,1,0:T(8,128)}), f32[16,128,128]{2,1,0:T(8,128)S(1)}, u32[]{:S(2)}, u32[]{:S(2)}) %all-to-all-start.1) | async-done | bytes 1048608 | tf_op jit(solution)/shard_map/all_to_all | solution.py:509
  53.1 0.6 answer.1
  53.7 5.4 %collective-permute-start.2 = (f32[16,8,128]{2,1,0:T(8,128)S(1)}, f32[16,8,128]{2,1,0:T(8,128)S(1)}, u32[]{:S(2)}, u32[]{:S(2)}) collective-permute-start(f32[16,8,128]{2,1,0:T(8,128)S(1)} %answer.1), channel_id=1, source_target_pairs={{0,1},{1,0},{2,3},{3,2},{4,5},{5,4},{6,7},{7,6},{8,9},{9,8},{10,11... | collective-permute-start | bytes 196616 | tf_op jit(solution)/shard_map/ppermute | solution.py:529
  59.2 1.1 %own_tops.1.own_share = f32[64,16]{1,0:T(8,128)S(1)} custom-call(s32[4,16]{1,0:T(4,128)S(1)} %get-tuple-element.46.plan, f32[256,8,128]{2,1,0:T(8,128)S(1)} %bitcast.5, bf16[256,512]{1,0:T(8,128)(2,1)S(1)} %get-tuple-element.48.top_mats), custom_call_target="tpu_custom_call" | custom-call | flops 400000000 | bytes 400000 | tf_op jit(solution)/shard_map/own_tops/pallas_call | solution.py:435
  60.2 0.0 collective-permute-done.2.received
  60.3 1.4 %down_sweep.1 = f32[16,1024]{1,0:T(8,128)} custom-call(f32[16,8,128]{2,1,0:T(8,128)S(1)} %collective-permute-done.2.received, f32[64,16]{1,0:T(8,128)S(1)} %own_tops.1.own_share, f32[16,1024]{1,0:T(8,128)S(1)} %get-tuple-element.49.base, bf16[256,512]{1,0:T(8,128)(2,1)S(1)} %get-tuple-element.48.top_mats, bf16[192,1024]{1,0:T(8,128)(2,1)S(1)} %get-tuple-element.50.top_to_points), custom_call_target="tpu_custom_call" | custom-call | flops 10000000 | bytes 800000 | tf_op jit(solution)/shard_map/down_sweep/pallas_call | solution.py:454
  (17 shorter events, 0.0 us)
Async XLA Ops:
  0.0 18.6 %copy-start.8 = (f32[3,1024]{1,0:T(4,128)S(1)}, f32[3,1024]{1,0:T(4,128)}, u32[]{:S(2)}) copy-start(f32[3,1024]{1,0:T(4,128)} %points.1) | copy-start | bytes 36868
  0.0 18.6 %copy-start.9 = (f32[3,1024]{1,0:T(4,128)S(1)}, f32[3,1024]{1,0:T(4,128)}, u32[]{:S(2)}) copy-start(f32[3,1024]{1,0:T(4,128)} %normals.1) | copy-start | bytes 36868
  0.0 18.6 %copy-start.14 = (s32[1,16]{1,0:T(1,128)S(1)}, s32[1,16]{1,0:T(1,128)}, u32[]{:S(2)}) copy-start(s32[1,16]{1,0:T(1,128)} %adm_top.3) | copy-start | bytes 196
  0.0 25.0 %copy-start.2 = (f32[1,16,4096]{2,1,0:T(8,128)S(1)}, f32[1,16,4096]{2,1,0:T(8,128)}, u32[]{:S(2)}) copy-start(f32[1,16,4096]{2,1,0:T(8,128)} %couple_top) | copy-start | bytes 786436
  2.7 15.9 %copy-start.7 = (f32[8,768]{1,0:T(8,128)S(1)}, f32[8,768]{1,0:T(8,128)}, u32[]{:S(2)}) copy-start(f32[8,768]{1,0:T(8,128)} %get-tuple-element.31.coefs) | copy-start | bytes 73732
  2.7 15.9 %copy-start = (f32[16,1024]{1,0:T(8,128)S(1)}, f32[16,1024]{1,0:T(8,128)}, u32[]{:S(2)}) copy-start(f32[16,1024]{1,0:T(8,128)} %dens.3) | copy-start | bytes 196612
  2.7 22.3 %copy-start.3 = (f32[64,1024]{1,0:T(8,128)S(1)}, f32[64,1024]{1,0:T(8,128)}, u32[]{:S(2)}) copy-start(f32[64,1024]{1,0:T(8,128)} %row_basis.3) | copy-start | bytes 786436
  2.7 27.5 %all-to-all-start = ((f32[16,8,128]{2,1,0:T(8,128)}), f32[16,8,128]{2,1,0:T(8,128)S(1)}, u32[]{:S(2)}, u32[]{:S(2)}) async-start(f32[16,8,128]{2,1,0:T(8,128)} %get-tuple-element.30), calls=%async_computation | async-start | bytes 131072 | tf_op jit(solution)/shard_map/all_to_all | solution.py:501
  18.7 6.4 %copy-start.5 = (f32[4,4096]{1,0:T(4,128)S(1)}, f32[4,4096]{1,0:T(4,128)}, u32[]{:S(2)}) copy-start(f32[4,4096]{1,0:T(4,128)} %down_leaf) | copy-start | bytes 196612
  18.7 6.4 %copy-start.6 = (f32[2,4096]{1,0:T(2,128)S(1)}, f32[2,4096]{1,0:T(2,128)}, u32[]{:S(2)}) copy-start(f32[2,4096]{1,0:T(2,128)} %down_mid) | copy-start | bytes 98308
  18.7 7.9 %collective-permute-start.1 = (f32[32,1024]{1,0:T(8,128)S(1)}, f32[32,1024]{1,0:T(8,128)S(1)}, u32[]{:S(2)}, u32[]{:S(2)}) collective-permute-start(f32[32,1024]{1,0:T(8,128)S(1)} %packed_for_neighbours.1.own), channel_id=1, source_target_pairs={{1,2},{2,1},{3,4},{4,3},{5,6},{6,5},{7,8},{8,7},{9,10},{10,9},{11,... | collective-permute-start | bytes 393224 | tf_op jit(solution)/shard_map/ppermute | solution.py:503
  23.1 3.5 %collective-permute-start = (f32[32,1024]{1,0:T(8,128)S(1)}, f32[32,1024]{1,0:T(8,128)S(1)}, u32[]{:S(2)}, u32[]{:S(2)}) collective-permute-start(f32[32,1024]{1,0:T(8,128)S(1)} %packed_for_neighbours.1.own), channel_id=1, source_target_pairs={{0,1},{1,0},{2,3},{3,2},{4,5},{5,4},{6,7},{7,6},{8,9},{9,8},{10,11... | collective-permute-start | bytes 393224 | tf_op jit(solution)/shard_map/ppermute | solution.py:502
  31.3 7.0 %copy-start.1 = (f32[4,6,4096]{2,0,1:T(4,128)S(1)}, f32[4,6,4096]{2,0,1:T(4,128)}, u32[]{:S(2)}) copy-start(f32[4,6,4096]{2,0,1:T(4,128)} %param.26) | copy-start | bytes 1179652
  31.3 7.0 %copy-start.4 = (f32[2,6,4096]{2,0,1:T(2,128)S(1)}, f32[2,6,4096]{2,0,1:T(2,128)}, u32[]{:S(2)}) copy-start(f32[2,6,4096]{2,0,1:T(2,128)} %param.27) | copy-start | bytes 589828
  31.3 7.0 %copy-start.11 = (s32[4,6]{1,0:T(4,128)S(1)}, s32[4,6]{1,0:T(4,128)}, u32[]{:S(2)}) copy-start(s32[4,6]{1,0:T(4,128)} %adm_leaf.1) | copy-start | bytes 292
  31.3 21.9 %all-to-all-start.1 = ((f32[16,128,128]{2,1,0:T(8,128)}), f32[16,128,128]{2,1,0:T(8,128)S(1)}, u32[]{:S(2)}, u32[]{:S(2)}) async-start(f32[16,128,128]{2,1,0:T(8,128)} %broadcast_in_dim.8), calls=%async_computation.1 | async-start | bytes 2097152 | tf_op jit(solution)/shard_map/all_to_all | solution.py:509
  38.2 0.7 %copy-start.10 = (s32[4,8]{1,0:T(4,128)S(1)}, s32[4,8]{1,0:T(4,128)}, u32[]{:S(2)}) copy-start(s32[4,8]{1,0:T(4,128)} %near_list.1) | copy-start | bytes 388
  38.2 0.7 %copy-start.12 = (s32[2,6]{1,0:T(2,128)S(1)}, s32[2,6]{1,0:T(2,128)}, u32[]{:S(2)}) copy-start(s32[2,6]{1,0:T(2,128)} %adm_mid.1) | copy-start | bytes 148
  38.2 0.7 %copy-start.13 = (s32[4]{0:T(128)S(1)}, s32[4]{0:T(128)}, u32[]{:S(2)}) copy-start(s32[4]{0:T(128)} %near_count.1) | copy-start | bytes 52
  53.7 6.5 %collective-permute-start.2 = (f32[16,8,128]{2,1,0:T(8,128)S(1)}, f32[16,8,128]{2,1,0:T(8,128)S(1)}, u32[]{:S(2)}, u32[]{:S(2)}) collective-permute-start(f32[16,8,128]{2,1,0:T(8,128)S(1)} %answer.1), channel_id=1, source_target_pairs={{0,1},{1,0},{2,3},{3,2},{4,5},{5,4},{6,7},{7,6},{8,9},{9,8},{10,11... | collective-permute-start | bytes 196616 | tf_op jit(solution)/shard_map/ppermute | solution.py:529

commit v4 on v3

--- a/solution.py
+++ b/solution.py
@@ -25,6 +25,11 @@
 COEF_ROW = 24
 GROUP = 8
 VMEM_LIMIT = 16 * 1024 * 1024
+CORES = 2
+RING = 16
+PLANES = 16
+FIRST_Z = 11
+FIRST_PLANE = 10
 
 smooth_sq = 0.01
 four_pi = 4.0 * math.pi
@@ -200,8 +205,10 @@
 
     for row, tops in ((0, adm_top), (2, wanted)):
         for a in range(ADM_TOP):
-            plan[row, a] = tops[0, a] // 2
-            plan[row + 1, a] = (tops[0, a] % 2 == core).astype(jnp.int32)
+            plane = tops[0, a] // (CORES * RING)
+            z = tops[0, a] // CORES % RING
+            plan[row, a] = (plane + PLANES - FIRST_PLANE) % PLANES * RING + (z + RING - FIRST_Z) % RING
+            plan[row + 1, a] = (tops[0, a] % CORES == core).astype(jnp.int32)
 
     count = jnp.int32(0)
     for i in range(LEAF_DEV):
@@ -464,15 +471,10 @@
 
 def solution(mesh):
     devices = mesh.devices.size
-    cores = 2
-    ring = 16
-    planes = devices // (cores * ring)
-    along_z = [
-        [(plane * ring + z) * cores + core for z in range(ring)] for plane in range(planes) for core in range(cores)
-    ]
-    across = [
-        [(plane * ring + z) * cores + core for plane in range(planes)] for z in range(ring) for core in range(cores)
-    ]
+    ring = [(FIRST_Z + i) % RING for i in range(RING)]
+    planes = [(FIRST_PLANE + i) % PLANES for i in range(PLANES)]
+    along_z = [[(p * RING + z) * CORES + c for z in ring] for p in range(PLANES) for c in range(CORES)]
+    across = [[(p * RING + z) * CORES + c for p in planes] for z in range(RING) for c in range(CORES)]
 
     def on_device(
         densities,
@@ -493,7 +495,7 @@
         adm_mid,
         adm_top,
     ):
-        own_top, coefs = up_call(densities, col_basis, up_leaf, up_mid, ring)
+        own_top, coefs = up_call(densities, col_basis, up_leaf, up_mid, RING)
         own_top, coefs, couple_top, down_mid, down_leaf = lax.optimization_barrier(
             (own_top, coefs, couple_top, down_mid, down_leaf)
         )
@@ -505,7 +507,7 @@
         ring_tops, same_chip, next_chip, top_mats, leaf_mats, top_to_points = lax.optimization_barrier(
             (ring_tops, same_chip, next_chip, top_mats, leaf_mats, top_to_points)
         )
-        spread = jnp.broadcast_to(ring_tops.reshape(1, ring * 8, 128), (planes, ring * 8, 128))
+        spread = jnp.broadcast_to(ring_tops.reshape(1, RING * 8, 128), (PLANES, RING * 8, 128))
         core_tops = lax.all_to_all(spread, "leaf", 0, 0, axis_index_groups=across, tiled=True)
         wanted = same_chip[WANTED_ROW : WANTED_ROW + 1, 0:ADM_TOP].astype(jnp.int32)
         base, plan = near_call(
@@ -524,7 +526,7 @@
             wanted,
         )
         core_tops, base, plan = lax.optimization_barrier((core_tops, base, plan))
-        core_tops = core_tops.reshape(planes * ring, 8, 128)
+        core_tops = core_tops.reshape(PLANES * RING, 8, 128)
         answers = answer_call(plan, core_tops)
         received = lax.ppermute(answers, "leaf", [(i, i ^ 1) for i in range(devices)])
         answers, plan, core_tops = lax.optimization_barrier((answers, plan, core_tops))

time: 62 us -> 56.3 us (0.908)
  waiting for transfers between devices: 11.7 us -> 2.27 us
  starting transfers between devices: 34.5 us -> 36.4 us
  Pallas kernels: 13.4 us -> 15.2 us
    all_to_all x1, waiting for transfers between devices: 7.74 us -> 1.92 us  [on_device(): lax.all_to_all(spread, 'leaf', 0, 0, axis_index_groups=across, tiled=True)]
    all_to_all x1, waiting for transfers between devices: 3.52 us -> 0.01 us  [on_device(): lax.all_to_all(own_top, 'leaf', 0, 0, axis_index_groups=along_z, tiled=True)]
    all_to_all x1, starting transfers between devices: 6.89 us -> 9.27 us  [on_device(): lax.all_to_all(spread, 'leaf', 0, 0, axis_index_groups=across, tiled=True)]
    pallas_call x1, Pallas kernels: 6.51 us -> 8.36 us  [near_call(): pl.pallas_call(near_kernel, name='near_and_couplings', out_shape=(jax.Sha...]
    ppermute x1, starting transfers between devices: 5.44 us -> 4.46 us  [on_device(): lax.ppermute(answers, 'leaf', [(i, i ^ 1) for i in range(devices)])]
    all_to_all x1, starting transfers between devices: 15.9 us -> 16.6 us  [on_device(): lax.all_to_all(own_top, 'leaf', 0, 0, axis_index_groups=along_z, tiled=True)]
  transfers between devices with their start and end apart: 5 -> 5, of which waited for: 3 -> 2; matrix products, arithmetic and copies ran while one was open for 0% -> 0% of each run, Pallas kernels for 14% -> 19%
where the time goes in v4:
time: 56.3 us; the launch traced here: 55.9 us
  starting transfers between devices  36.4 us (65%)
  Pallas kernels  15.2 us (27%)
  waiting for transfers between devices  2.27 us (4%)
  local copies, waits for them, and re-layouts  1.79 us (3%)
    all_to_all x1, starting transfers between devices, on_device(): lax.all_to_all(own_top, 'leaf', 0, 0, axis_index_groups=along_z, tiled=True)  16.6 us
    all_to_all x1, starting transfers between devices, on_device(): lax.all_to_all(spread, 'leaf', 0, 0, axis_index_groups=across, tiled=True)  9.27 us
    pallas_call x1, Pallas kernels, near_call(): pl.pallas_call(near_kernel, name='near_and_couplings', out_shape=(jax.Sha...  8.36 us
    ppermute x1, starting transfers between devices, on_device(): lax.ppermute(answers, 'leaf', [(i, i ^ 1) for i in range(devices)])  4.46 us
    ppermute x1, starting transfers between devices, on_device(): lax.ppermute(packed, 'leaf', [(i, (i + 1 ^ 1) - 1) for i in range(1, devi...  4.2 us
    pallas_call x1, Pallas kernels, up_call(): pl.pallas_call(up_kernel, name='up_sweep', out_shape=(jax.ShapeDtypeStruc...  2.68 us
    ppermute x1, starting transfers between devices, on_device(): lax.ppermute(packed, 'leaf', [(i, i ^ 1) for i in range(devices)])  1.92 us
    all_to_all x1, waiting for transfers between devices, on_device(): lax.all_to_all(spread, 'leaf', 0, 0, axis_index_groups=across, tiled=True)  1.92 us
  transfers between devices with their start and end apart: 5, of which 2 were waited for; matrix products, arithmetic and copies ran while one was open for 0% of the time, Pallas kernels for 19%

profile of v4, /device:TPU:1, one launch (start us, length us, event | category | flops | bytes accessed | tf_op | source)
XLA Modules:
  0.0 55.9 jit_solution(10786553131950390152)
XLA Ops:
  0.0 0.0 copy-start.2
  0.0 2.7 %up_sweep.1 = (f32[16,8,128]{2,1,0:T(8,128)}, f32[8,768]{1,0:T(8,128)}) custom-call(f32[16,1024]{1,0:T(8,128)} %dens.3, f32[64,1024]{1,0:T(8,128)} %col_basis.1, f32[4,4096]{1,0:T(4,128)} %up_leaf.1, f32[2,4096]{1,0:T(2,128)} %up_mid.1), custom_call_target="tpu_custom_call" | custom-call | flops 10000000 | bytes 800000 | tf_op jit(solution)/shard_map/up_sweep/pallas_call | solution.py:133
  2.7 16.6 %all-to-all-start = ((f32[16,8,128]{2,1,0:T(8,128)}), f32[16,8,128]{2,1,0:T(8,128)S(1)}, u32[]{:S(2)}, u32[]{:S(2)}) async-start(f32[16,8,128]{2,1,0:T(8,128)} %get-tuple-element.30), calls=%async_computation | async-start | bytes 131072 | tf_op jit(solution)/shard_map/all_to_all | solution.py:503
  19.3 0.0 copy-done.8
  19.3 0.0 copy-start.5
  19.3 0.0 copy-start.6
  19.4 4.2 %collective-permute-start.1 = (f32[32,1024]{1,0:T(8,128)S(1)}, f32[32,1024]{1,0:T(8,128)S(1)}, u32[]{:S(2)}, u32[]{:S(2)}) collective-permute-start(f32[32,1024]{1,0:T(8,128)S(1)} %packed_for_neighbours.1.own), channel_id=1, source_target_pairs={{1,2},{2,1},{3,4},{4,3},{5,6},{6,5},{7,8},{8,7},{9,10},{10,9},{11,... | collective-permute-start | bytes 393224 | tf_op jit(solution)/shard_map/ppermute | solution.py:505
  23.6 1.9 %collective-permute-start = (f32[32,1024]{1,0:T(8,128)S(1)}, f32[32,1024]{1,0:T(8,128)S(1)}, u32[]{:S(2)}, u32[]{:S(2)}) collective-permute-start(f32[32,1024]{1,0:T(8,128)S(1)} %packed_for_neighbours.1.own), channel_id=1, source_target_pairs={{0,1},{1,0},{2,3},{3,2},{4,5},{5,4},{6,7},{7,6},{8,9},{9,8},{10,11... | collective-permute-start | bytes 393224 | tf_op jit(solution)/shard_map/ppermute | solution.py:504
  25.5 0.0 copy-done.2
  25.5 0.0 copy-done.3
  25.5 0.0 copy-done.5
  25.5 0.0 copy-done.6
  25.6 1.1 %transposed_matrices.1 = (bf16[256,512]{1,0:T(8,128)(2,1)S(1)}, f32[4,64,64]{2,1,0:T(8,128)S(1)}, bf16[192,1024]{1,0:T(8,128)(2,1)S(1)}) custom-call(f32[1,16,4096]{2,1,0:T(8,128)S(1)} %copy-done.2, f32[2,4096]{1,0:T(2,128)S(1)} %copy-done.6, f32[4,4096]{1,0:T(4,128)S(1)} %copy-done.5, f32[64,1024]{1,0:T(8,128)S(1)} %copy-done.3), custom_call_target="tpu_custom_call" | custom-call | flops 2000000000 | bytes 2000000 | tf_op jit(solution)/shard_map/transposed_matrices/pallas_call | solution.py:358
  26.7 0.3 collective-permute-done.1.next_chip
  27.0 0.0 collective-permute-done.same_chip
  27.0 0.0 all-to-all-done
  27.0 1.1 %broadcast_in_dim.8 = f32[16,128,128]{2,1,0:T(8,128)} broadcast(f32[128,128]{1,0:T(8,128)S(1)} %bitcast.8), dimensions={1,2} | broadcast | bytes 1114112 | tf_op jit(solution)/shard_map/broadcast_in_dim | solution.py:510
  28.1 9.3 %all-to-all-start.1 = ((f32[16,128,128]{2,1,0:T(8,128)}), f32[16,128,128]{2,1,0:T(8,128)S(1)}, u32[]{:S(2)}, u32[]{:S(2)}) async-start(f32[16,128,128]{2,1,0:T(8,128)} %broadcast_in_dim.8), calls=%async_computation.1 | async-start | bytes 2097152 | tf_op jit(solution)/shard_map/all_to_all | solution.py:511
  37.4 0.0 copy-start.10
  37.4 0.0 copy-start.12
  37.4 0.0 copy-start.13
  37.5 0.0 copy-done.1
  37.5 0.0 copy-done.4
  37.5 0.6 %copy-done.10 = s32[4,8]{1,0:T(4,128)S(1)} copy-done((s32[4,8]{1,0:T(4,128)S(1)}, s32[4,8]{1,0:T(4,128)}, u32[]{:S(2)}) %copy-start.10) | copy-done | bytes 152
  38.1 0.0 copy-done.12
  38.1 8.4 %near_and_couplings.1 = (f32[16,1024]{1,0:T(8,128)S(1)}, s32[4,16]{1,0:T(4,128)S(1)}) custom-call(s32[4,8]{1,0:T(4,128)S(1)} %copy-done.10, s32[4]{0:T(128)S(1)} %copy-done.13, s32[4,6]{1,0:T(4,128)S(1)} %copy-done.11, s32[2,6]{1,0:T(2,128)S(1)} %copy-done.12, f32[32,1024]{1,0:T(8,128)S(1)} %packed_for_neighbours.1.own, ...), custom_call_target="tpu_custom_call" | custom-call | flops 4000000000 | bytes 2000000 | tf_op jit(solution)/shard_map/near_and_couplings/pallas_call | solution.py:379
  46.5 1.9 %all-to-all-done.1 = f32[16,128,128]{2,1,0:T(8,128)S(1)} async-done(((f32[16,128,128]{2,1,0:T(8,128)}), f32[16,128,128]{2,1,0:T(8,128)S(1)}, u32[]{:S(2)}, u32[]{:S(2)}) %all-to-all-start.1) | async-done | bytes 1048608 | tf_op jit(solution)/shard_map/all_to_all | solution.py:511
  48.4 0.6 %answer.1 = f32[16,8,128]{2,1,0:T(8,128)S(1)} custom-call(s32[4,16]{1,0:T(4,128)S(1)} %get-tuple-element.46.plan, f32[256,8,128]{2,1,0:T(8,128)S(1)} %bitcast.4), custom_call_target="tpu_custom_call" | custom-call | flops 1000000 | bytes 100000 | tf_op jit(solution)/shard_map/answer/pallas_call | solution.py:426
  49.0 4.5 %collective-permute-start.2 = (f32[16,8,128]{2,1,0:T(8,128)S(1)}, f32[16,8,128]{2,1,0:T(8,128)S(1)}, u32[]{:S(2)}, u32[]{:S(2)}) collective-permute-start(f32[16,8,128]{2,1,0:T(8,128)S(1)} %answer.1), channel_id=1, source_target_pairs={{0,1},{1,0},{2,3},{3,2},{4,5},{5,4},{6,7},{7,6},{8,9},{9,8},{10,11... | collective-permute-start | bytes 196616 | tf_op jit(solution)/shard_map/ppermute | solution.py:531
  53.5 1.1 %own_tops.1.own_share = f32[64,16]{1,0:T(8,128)S(1)} custom-call(s32[4,16]{1,0:T(4,128)S(1)} %get-tuple-element.46.plan, f32[256,8,128]{2,1,0:T(8,128)S(1)} %bitcast.5, bf16[256,512]{1,0:T(8,128)(2,1)S(1)} %get-tuple-element.48.top_mats), custom_call_target="tpu_custom_call" | custom-call | flops 400000000 | bytes 400000 | tf_op jit(solution)/shard_map/own_tops/pallas_call | solution.py:442
  54.5 0.0 collective-permute-done.2.received
  54.5 1.4 %down_sweep.1 = f32[16,1024]{1,0:T(8,128)} custom-call(f32[16,8,128]{2,1,0:T(8,128)S(1)} %collective-permute-done.2.received, f32[64,16]{1,0:T(8,128)S(1)} %own_tops.1.own_share, f32[16,1024]{1,0:T(8,128)S(1)} %get-tuple-element.49.base, bf16[256,512]{1,0:T(8,128)(2,1)S(1)} %get-tuple-element.48.top_mats, bf16[192,1024]{1,0:T(8,128)(2,1)S(1)} %get-tuple-element.50.top_to_points), custom_call_target="tpu_custom_call" | custom-call | flops 10000000 | bytes 800000 | tf_op jit(solution)/shard_map/down_sweep/pallas_call | solution.py:461
  (17 shorter events, 0.0 us)
Async XLA Ops:
  0.0 19.3 %copy-start.8 = (f32[3,1024]{1,0:T(4,128)S(1)}, f32[3,1024]{1,0:T(4,128)}, u32[]{:S(2)}) copy-start(f32[3,1024]{1,0:T(4,128)} %points.1) | copy-start | bytes 36868
  0.0 19.3 %copy-start.9 = (f32[3,1024]{1,0:T(4,128)S(1)}, f32[3,1024]{1,0:T(4,128)}, u32[]{:S(2)}) copy-start(f32[3,1024]{1,0:T(4,128)} %normals.1) | copy-start | bytes 36868
  0.0 19.3 %copy-start.14 = (s32[1,16]{1,0:T(1,128)S(1)}, s32[1,16]{1,0:T(1,128)}, u32[]{:S(2)}) copy-start(s32[1,16]{1,0:T(1,128)} %adm_top.3) | copy-start | bytes 196
  0.0 25.5 %copy-start.2 = (f32[1,16,4096]{2,1,0:T(8,128)S(1)}, f32[1,16,4096]{2,1,0:T(8,128)}, u32[]{:S(2)}) copy-start(f32[1,16,4096]{2,1,0:T(8,128)} %couple_top) | copy-start | bytes 786436
  2.7 16.6 %copy-start.7 = (f32[8,768]{1,0:T(8,128)S(1)}, f32[8,768]{1,0:T(8,128)}, u32[]{:S(2)}) copy-start(f32[8,768]{1,0:T(8,128)} %get-tuple-element.31.coefs) | copy-start | bytes 73732
  2.7 16.6 %copy-start = (f32[16,1024]{1,0:T(8,128)S(1)}, f32[16,1024]{1,0:T(8,128)}, u32[]{:S(2)}) copy-start(f32[16,1024]{1,0:T(8,128)} %dens.3) | copy-start | bytes 196612
  2.7 22.8 %copy-start.3 = (f32[64,1024]{1,0:T(8,128)S(1)}, f32[64,1024]{1,0:T(8,128)}, u32[]{:S(2)}) copy-start(f32[64,1024]{1,0:T(8,128)} %row_basis.3) | copy-start | bytes 786436
  2.7 24.3 %all-to-all-start = ((f32[16,8,128]{2,1,0:T(8,128)}), f32[16,8,128]{2,1,0:T(8,128)S(1)}, u32[]{:S(2)}, u32[]{:S(2)}) async-start(f32[16,8,128]{2,1,0:T(8,128)} %get-tuple-element.30), calls=%async_computation | async-start | bytes 131072 | tf_op jit(solution)/shard_map/all_to_all | solution.py:503
  19.3 6.2 %copy-start.5 = (f32[4,4096]{1,0:T(4,128)S(1)}, f32[4,4096]{1,0:T(4,128)}, u32[]{:S(2)}) copy-start(f32[4,4096]{1,0:T(4,128)} %down_leaf) | copy-start | bytes 196612
  19.3 6.2 %copy-start.6 = (f32[2,4096]{1,0:T(2,128)S(1)}, f32[2,4096]{1,0:T(2,128)}, u32[]{:S(2)}) copy-start(f32[2,4096]{1,0:T(2,128)} %down_mid) | copy-start | bytes 98308
  19.4 7.7 %collective-permute-start.1 = (f32[32,1024]{1,0:T(8,128)S(1)}, f32[32,1024]{1,0:T(8,128)S(1)}, u32[]{:S(2)}, u32[]{:S(2)}) collective-permute-start(f32[32,1024]{1,0:T(8,128)S(1)} %packed_for_neighbours.1.own), channel_id=1, source_target_pairs={{1,2},{2,1},{3,4},{4,3},{5,6},{6,5},{7,8},{8,7},{9,10},{10,9},{11,... | collective-permute-start | bytes 393224 | tf_op jit(solution)/shard_map/ppermute | solution.py:505
  23.6 3.4 %collective-permute-start = (f32[32,1024]{1,0:T(8,128)S(1)}, f32[32,1024]{1,0:T(8,128)S(1)}, u32[]{:S(2)}, u32[]{:S(2)}) collective-permute-start(f32[32,1024]{1,0:T(8,128)S(1)} %packed_for_neighbours.1.own), channel_id=1, source_target_pairs={{0,1},{1,0},{2,3},{3,2},{4,5},{5,4},{6,7},{7,6},{8,9},{9,8},{10,11... | collective-permute-start | bytes 393224 | tf_op jit(solution)/shard_map/ppermute | solution.py:504
  28.1 9.3 %copy-start.1 = (f32[4,6,4096]{2,0,1:T(4,128)S(1)}, f32[4,6,4096]{2,0,1:T(4,128)}, u32[]{:S(2)}) copy-start(f32[4,6,4096]{2,0,1:T(4,128)} %param.26) | copy-start | bytes 1179652
  28.1 9.3 %copy-start.4 = (f32[2,6,4096]{2,0,1:T(2,128)S(1)}, f32[2,6,4096]{2,0,1:T(2,128)}, u32[]{:S(2)}) copy-start(f32[2,6,4096]{2,0,1:T(2,128)} %param.27) | copy-start | bytes 589828
  28.1 9.3 %copy-start.11 = (s32[4,6]{1,0:T(4,128)S(1)}, s32[4,6]{1,0:T(4,128)}, u32[]{:S(2)}) copy-start(s32[4,6]{1,0:T(4,128)} %adm_leaf.1) | copy-start | bytes 292
  28.1 20.3 %all-to-all-start.1 = ((f32[16,128,128]{2,1,0:T(8,128)}), f32[16,128,128]{2,1,0:T(8,128)S(1)}, u32[]{:S(2)}, u32[]{:S(2)}) async-start(f32[16,128,128]{2,1,0:T(8,128)} %broadcast_in_dim.8), calls=%async_computation.1 | async-start | bytes 2097152 | tf_op jit(solution)/shard_map/all_to_all | solution.py:511
  37.4 0.7 %copy-start.10 = (s32[4,8]{1,0:T(4,128)S(1)}, s32[4,8]{1,0:T(4,128)}, u32[]{:S(2)}) copy-start(s32[4,8]{1,0:T(4,128)} %near_list.1) | copy-start | bytes 388
  37.4 0.7 %copy-start.12 = (s32[2,6]{1,0:T(2,128)S(1)}, s32[2,6]{1,0:T(2,128)}, u32[]{:S(2)}) copy-start(s32[2,6]{1,0:T(2,128)} %adm_mid.1) | copy-start | bytes 148
  37.4 0.7 %copy-start.13 = (s32[4]{0:T(128)S(1)}, s32[4]{0:T(128)}, u32[]{:S(2)}) copy-start(s32[4]{0:T(128)} %near_count.1) | copy-start | bytes 52
  49.0 5.5 %collective-permute-start.2 = (f32[16,8,128]{2,1,0:T(8,128)S(1)}, f32[16,8,128]{2,1,0:T(8,128)S(1)}, u32[]{:S(2)}, u32[]{:S(2)}) collective-permute-start(f32[16,8,128]{2,1,0:T(8,128)S(1)} %answer.1), channel_id=1, source_target_pairs={{0,1},{1,0},{2,3},{3,2},{4,5},{5,4},{6,7},{7,6},{8,9},{9,8},{10,11... | collective-permute-start | bytes 196616 | tf_op jit(solution)/shard_map/ppermute | solution.py:531

commit v5 on v4

--- a/solution.py
+++ b/solution.py
@@ -292,13 +292,22 @@
         )
         return leaf, uses * term
 
-    def some_blocks(step, carry):
-        results = [one_block(GROUP * step + k) for k in range(GROUP)]
+    def blocks_from(first, size):
+        results = [one_block(first + k) for k in range(size)]
         for leaf, term in results:
             near_t[leaf] = near_t[leaf] + term
+
+    def many_blocks(step, carry):
+        blocks_from(2 * GROUP * step, 2 * GROUP)
         return carry
 
-    lax.fori_loop(0, (count + GROUP - 1) // GROUP, some_blocks, 0)
+    def some_blocks(step, carry):
+        blocks_from(GROUP * step, GROUP)
+        return carry
+
+    groups = (count + GROUP - 1) // GROUP
+    lax.fori_loop(0, groups // 2, many_blocks, 0)
+    lax.fori_loop(groups // 2 * 2, groups, some_blocks, 0)
     for leaf in range(LEAF_DEV):
         total = jnp.transpose(near_t[leaf])
         near_out[leaf] = 0.5 * own[0:RHS, LEAF * leaf : LEAF * leaf + LEAF] + total[:RHS] + total[RHS:]

time: 56.3 us -> 56.3 us (level)
  transfers between devices with their start and end apart: 5 -> 5, of which waited for: 2 -> 2; matrix products, arithmetic and copies ran while one was open for 0% -> 0% of each run, Pallas kernels for 19% -> 18%
where the time goes in v5:
time: 56.3 us; the launch traced here: 55.9 us
  starting transfers between devices  36.4 us (65%)
  Pallas kernels  14.8 us (26%)
  waiting for transfers between devices  2.67 us (5%)
  local copies, waits for them, and re-layouts  1.79 us (3%)
    all_to_all x1, starting transfers between devices, on_device(): lax.all_to_all(own_top, 'leaf', 0, 0, axis_index_groups=along_z, tiled=True)  16.6 us
    all_to_all x1, starting transfers between devices, on_device(): lax.all_to_all(spread, 'leaf', 0, 0, axis_index_groups=across, tiled=True)  9.27 us
    pallas_call x1, Pallas kernels, near_call(): pl.pallas_call(near_kernel, name='near_and_couplings', out_shape=(jax.Sha...  7.97 us
    ppermute x1, starting transfers between devices, on_device(): lax.ppermute(answers, 'leaf', [(i, i ^ 1) for i in range(devices)])  4.46 us
    ppermute x1, starting transfers between devices, on_device(): lax.ppermute(packed, 'leaf', [(i, (i + 1 ^ 1) - 1) for i in range(1, devi...  4.2 us
    pallas_call x1, Pallas kernels, up_call(): pl.pallas_call(up_kernel, name='up_sweep', out_shape=(jax.ShapeDtypeStruc...  2.68 us
    all_to_all x1, waiting for transfers between devices, on_device(): lax.all_to_all(spread, 'leaf', 0, 0, axis_index_groups=across, tiled=True)  2.31 us
    ppermute x1, starting transfers between devices, on_device(): lax.ppermute(packed, 'leaf', [(i, i ^ 1) for i in range(devices)])  1.92 us
  transfers between devices with their start and end apart: 5, of which 2 were waited for; matrix products, arithmetic and copies ran while one was open for 0% of the time, Pallas kernels for 18%

profile of v5, /device:TPU:1, one launch (start us, length us, event | category | flops | bytes accessed | tf_op | source)
XLA Modules:
  0.0 55.9 jit_solution(10558463363849360097)
XLA Ops:
  0.0 0.0 copy-start.2
  0.0 2.7 %up_sweep.1 = (f32[16,8,128]{2,1,0:T(8,128)}, f32[8,768]{1,0:T(8,128)}) custom-call(f32[16,1024]{1,0:T(8,128)} %dens.3, f32[64,1024]{1,0:T(8,128)} %col_basis.1, f32[4,4096]{1,0:T(4,128)} %up_leaf.1, f32[2,4096]{1,0:T(2,128)} %up_mid.1), custom_call_target="tpu_custom_call" | custom-call | flops 10000000 | bytes 800000 | tf_op jit(solution)/shard_map/up_sweep/pallas_call | solution.py:133
  2.7 16.6 %all-to-all-start = ((f32[16,8,128]{2,1,0:T(8,128)}), f32[16,8,128]{2,1,0:T(8,128)S(1)}, u32[]{:S(2)}, u32[]{:S(2)}) async-start(f32[16,8,128]{2,1,0:T(8,128)} %get-tuple-element.30), calls=%async_computation | async-start | bytes 131072 | tf_op jit(solution)/shard_map/all_to_all | solution.py:512
  19.3 0.0 copy-done.8
  19.3 0.0 copy-start.5
  19.3 0.0 copy-start.6
  19.4 4.2 %collective-permute-start.1 = (f32[32,1024]{1,0:T(8,128)S(1)}, f32[32,1024]{1,0:T(8,128)S(1)}, u32[]{:S(2)}, u32[]{:S(2)}) collective-permute-start(f32[32,1024]{1,0:T(8,128)S(1)} %packed_for_neighbours.1.own), channel_id=1, source_target_pairs={{1,2},{2,1},{3,4},{4,3},{5,6},{6,5},{7,8},{8,7},{9,10},{10,9},{11,... | collective-permute-start | bytes 393224 | tf_op jit(solution)/shard_map/ppermute | solution.py:514
  23.6 1.9 %collective-permute-start = (f32[32,1024]{1,0:T(8,128)S(1)}, f32[32,1024]{1,0:T(8,128)S(1)}, u32[]{:S(2)}, u32[]{:S(2)}) collective-permute-start(f32[32,1024]{1,0:T(8,128)S(1)} %packed_for_neighbours.1.own), channel_id=1, source_target_pairs={{0,1},{1,0},{2,3},{3,2},{4,5},{5,4},{6,7},{7,6},{8,9},{9,8},{10,11... | collective-permute-start | bytes 393224 | tf_op jit(solution)/shard_map/ppermute | solution.py:513
  25.5 0.0 copy-done.2
  25.5 0.0 copy-done.3
  25.5 0.0 copy-done.5
  25.5 0.0 copy-done.6
  25.6 1.1 %transposed_matrices.1 = (bf16[256,512]{1,0:T(8,128)(2,1)S(1)}, f32[4,64,64]{2,1,0:T(8,128)S(1)}, bf16[192,1024]{1,0:T(8,128)(2,1)S(1)}) custom-call(f32[1,16,4096]{2,1,0:T(8,128)S(1)} %copy-done.2, f32[2,4096]{1,0:T(2,128)S(1)} %copy-done.6, f32[4,4096]{1,0:T(4,128)S(1)} %copy-done.5, f32[64,1024]{1,0:T(8,128)S(1)} %copy-done.3), custom_call_target="tpu_custom_call" | custom-call | flops 2000000000 | bytes 2000000 | tf_op jit(solution)/shard_map/transposed_matrices/pallas_call | solution.py:367
  26.7 0.3 collective-permute-done.1.next_chip
  27.0 0.0 collective-permute-done.same_chip
  27.0 0.0 all-to-all-done
  27.0 1.1 %broadcast_in_dim.8 = f32[16,128,128]{2,1,0:T(8,128)} broadcast(f32[128,128]{1,0:T(8,128)S(1)} %bitcast.8), dimensions={1,2} | broadcast | bytes 1114112 | tf_op jit(solution)/shard_map/broadcast_in_dim | solution.py:519
  28.1 9.3 %all-to-all-start.1 = ((f32[16,128,128]{2,1,0:T(8,128)}), f32[16,128,128]{2,1,0:T(8,128)S(1)}, u32[]{:S(2)}, u32[]{:S(2)}) async-start(f32[16,128,128]{2,1,0:T(8,128)} %broadcast_in_dim.8), calls=%async_computation.1 | async-start | bytes 2097152 | tf_op jit(solution)/shard_map/all_to_all | solution.py:520
  37.4 0.0 copy-start.10
  37.4 0.0 copy-start.12
  37.4 0.0 copy-start.13
  37.5 0.0 copy-done.1
  37.5 0.0 copy-done.4
  37.5 0.6 %copy-done.10 = s32[4,8]{1,0:T(4,128)S(1)} copy-done((s32[4,8]{1,0:T(4,128)S(1)}, s32[4,8]{1,0:T(4,128)}, u32[]{:S(2)}) %copy-start.10) | copy-done | bytes 152
  38.1 0.0 copy-done.12
  38.1 8.0 %near_and_couplings.1 = (f32[16,1024]{1,0:T(8,128)S(1)}, s32[4,16]{1,0:T(4,128)S(1)}) custom-call(s32[4,8]{1,0:T(4,128)S(1)} %copy-done.10, s32[4]{0:T(128)S(1)} %copy-done.13, s32[4,6]{1,0:T(4,128)S(1)} %copy-done.11, s32[2,6]{1,0:T(2,128)S(1)} %copy-done.12, f32[32,1024]{1,0:T(8,128)S(1)} %packed_for_neighbours.1.own, ...), custom_call_target="tpu_custom_call" | custom-call | flops 4000000000 | bytes 2000000 | tf_op jit(solution)/shard_map/near_and_couplings/pallas_call | solution.py:388
  46.1 2.3 %all-to-all-done.1 = f32[16,128,128]{2,1,0:T(8,128)S(1)} async-done(((f32[16,128,128]{2,1,0:T(8,128)}), f32[16,128,128]{2,1,0:T(8,128)S(1)}, u32[]{:S(2)}, u32[]{:S(2)}) %all-to-all-start.1) | async-done | bytes 1048608 | tf_op jit(solution)/shard_map/all_to_all | solution.py:520
  48.4 0.6 %answer.1 = f32[16,8,128]{2,1,0:T(8,128)S(1)} custom-call(s32[4,16]{1,0:T(4,128)S(1)} %get-tuple-element.46.plan, f32[256,8,128]{2,1,0:T(8,128)S(1)} %bitcast.4), custom_call_target="tpu_custom_call" | custom-call | flops 1000000 | bytes 100000 | tf_op jit(solution)/shard_map/answer/pallas_call | solution.py:435
  49.0 4.5 %collective-permute-start.2 = (f32[16,8,128]{2,1,0:T(8,128)S(1)}, f32[16,8,128]{2,1,0:T(8,128)S(1)}, u32[]{:S(2)}, u32[]{:S(2)}) collective-permute-start(f32[16,8,128]{2,1,0:T(8,128)S(1)} %answer.1), channel_id=1, source_target_pairs={{0,1},{1,0},{2,3},{3,2},{4,5},{5,4},{6,7},{7,6},{8,9},{9,8},{10,11... | collective-permute-start | bytes 196616 | tf_op jit(solution)/shard_map/ppermute | solution.py:540
  53.5 1.1 %own_tops.1.own_share = f32[64,16]{1,0:T(8,128)S(1)} custom-call(s32[4,16]{1,0:T(4,128)S(1)} %get-tuple-element.46.plan, f32[256,8,128]{2,1,0:T(8,128)S(1)} %bitcast.5, bf16[256,512]{1,0:T(8,128)(2,1)S(1)} %get-tuple-element.48.top_mats), custom_call_target="tpu_custom_call" | custom-call | flops 400000000 | bytes 400000 | tf_op jit(solution)/shard_map/own_tops/pallas_call | solution.py:451
  54.5 0.0 collective-permute-done.2.received
  54.5 1.4 %down_sweep.1 = f32[16,1024]{1,0:T(8,128)} custom-call(f32[16,8,128]{2,1,0:T(8,128)S(1)} %collective-permute-done.2.received, f32[64,16]{1,0:T(8,128)S(1)} %own_tops.1.own_share, f32[16,1024]{1,0:T(8,128)S(1)} %get-tuple-element.49.base, bf16[256,512]{1,0:T(8,128)(2,1)S(1)} %get-tuple-element.48.top_mats, bf16[192,1024]{1,0:T(8,128)(2,1)S(1)} %get-tuple-element.50.top_to_points), custom_call_target="tpu_custom_call" | custom-call | flops 10000000 | bytes 800000 | tf_op jit(solution)/shard_map/down_sweep/pallas_call | solution.py:470
  (17 shorter events, 0.0 us)
Async XLA Ops:
  0.0 19.3 %copy-start.8 = (f32[3,1024]{1,0:T(4,128)S(1)}, f32[3,1024]{1,0:T(4,128)}, u32[]{:S(2)}) copy-start(f32[3,1024]{1,0:T(4,128)} %points.1) | copy-start | bytes 36868
  0.0 19.3 %copy-start.9 = (f32[3,1024]{1,0:T(4,128)S(1)}, f32[3,1024]{1,0:T(4,128)}, u32[]{:S(2)}) copy-start(f32[3,1024]{1,0:T(4,128)} %normals.1) | copy-start | bytes 36868
  0.0 19.3 %copy-start.14 = (s32[1,16]{1,0:T(1,128)S(1)}, s32[1,16]{1,0:T(1,128)}, u32[]{:S(2)}) copy-start(s32[1,16]{1,0:T(1,128)} %adm_top.3) | copy-start | bytes 196
  0.0 25.5 %copy-start.2 = (f32[1,16,4096]{2,1,0:T(8,128)S(1)}, f32[1,16,4096]{2,1,0:T(8,128)}, u32[]{:S(2)}) copy-start(f32[1,16,4096]{2,1,0:T(8,128)} %couple_top) | copy-start | bytes 786436
  2.7 16.6 %copy-start.7 = (f32[8,768]{1,0:T(8,128)S(1)}, f32[8,768]{1,0:T(8,128)}, u32[]{:S(2)}) copy-start(f32[8,768]{1,0:T(8,128)} %get-tuple-element.31.coefs) | copy-start | bytes 73732
  2.7 16.6 %copy-start = (f32[16,1024]{1,0:T(8,128)S(1)}, f32[16,1024]{1,0:T(8,128)}, u32[]{:S(2)}) copy-start(f32[16,1024]{1,0:T(8,128)} %dens.3) | copy-start | bytes 196612
  2.7 22.8 %copy-start.3 = (f32[64,1024]{1,0:T(8,128)S(1)}, f32[64,1024]{1,0:T(8,128)}, u32[]{:S(2)}) copy-start(f32[64,1024]{1,0:T(8,128)} %row_basis.3) | copy-start | bytes 786436
  2.7 24.3 %all-to-all-start = ((f32[16,8,128]{2,1,0:T(8,128)}), f32[16,8,128]{2,1,0:T(8,128)S(1)}, u32[]{:S(2)}, u32[]{:S(2)}) async-start(f32[16,8,128]{2,1,0:T(8,128)} %get-tuple-element.30), calls=%async_computation | async-start | bytes 131072 | tf_op jit(solution)/shard_map/all_to_all | solution.py:512
  19.3 6.2 %copy-start.5 = (f32[4,4096]{1,0:T(4,128)S(1)}, f32[4,4096]{1,0:T(4,128)}, u32[]{:S(2)}) copy-start(f32[4,4096]{1,0:T(4,128)} %down_leaf) | copy-start | bytes 196612
  19.3 6.2 %copy-start.6 = (f32[2,4096]{1,0:T(2,128)S(1)}, f32[2,4096]{1,0:T(2,128)}, u32[]{:S(2)}) copy-start(f32[2,4096]{1,0:T(2,128)} %down_mid) | copy-start | bytes 98308
  19.4 7.7 %collective-permute-start.1 = (f32[32,1024]{1,0:T(8,128)S(1)}, f32[32,1024]{1,0:T(8,128)S(1)}, u32[]{:S(2)}, u32[]{:S(2)}) collective-permute-start(f32[32,1024]{1,0:T(8,128)S(1)} %packed_for_neighbours.1.own), channel_id=1, source_target_pairs={{1,2},{2,1},{3,4},{4,3},{5,6},{6,5},{7,8},{8,7},{9,10},{10,9},{11,... | collective-permute-start | bytes 393224 | tf_op jit(solution)/shard_map/ppermute | solution.py:514
  23.6 3.4 %collective-permute-start = (f32[32,1024]{1,0:T(8,128)S(1)}, f32[32,1024]{1,0:T(8,128)S(1)}, u32[]{:S(2)}, u32[]{:S(2)}) collective-permute-start(f32[32,1024]{1,0:T(8,128)S(1)} %packed_for_neighbours.1.own), channel_id=1, source_target_pairs={{0,1},{1,0},{2,3},{3,2},{4,5},{5,4},{6,7},{7,6},{8,9},{9,8},{10,11... | collective-permute-start | bytes 393224 | tf_op jit(solution)/shard_map/ppermute | solution.py:513
  28.1 9.3 %copy-start.1 = (f32[4,6,4096]{2,0,1:T(4,128)S(1)}, f32[4,6,4096]{2,0,1:T(4,128)}, u32[]{:S(2)}) copy-start(f32[4,6,4096]{2,0,1:T(4,128)} %param.26) | copy-start | bytes 1179652
  28.1 9.3 %copy-start.4 = (f32[2,6,4096]{2,0,1:T(2,128)S(1)}, f32[2,6,4096]{2,0,1:T(2,128)}, u32[]{:S(2)}) copy-start(f32[2,6,4096]{2,0,1:T(2,128)} %param.27) | copy-start | bytes 589828
  28.1 9.3 %copy-start.11 = (s32[4,6]{1,0:T(4,128)S(1)}, s32[4,6]{1,0:T(4,128)}, u32[]{:S(2)}) copy-start(s32[4,6]{1,0:T(4,128)} %adm_leaf.1) | copy-start | bytes 292
  28.1 20.3 %all-to-all-start.1 = ((f32[16,128,128]{2,1,0:T(8,128)}), f32[16,128,128]{2,1,0:T(8,128)S(1)}, u32[]{:S(2)}, u32[]{:S(2)}) async-start(f32[16,128,128]{2,1,0:T(8,128)} %broadcast_in_dim.8), calls=%async_computation.1 | async-start | bytes 2097152 | tf_op jit(solution)/shard_map/all_to_all | solution.py:520
  37.4 0.7 %copy-start.10 = (s32[4,8]{1,0:T(4,128)S(1)}, s32[4,8]{1,0:T(4,128)}, u32[]{:S(2)}) copy-start(s32[4,8]{1,0:T(4,128)} %near_list.1) | copy-start | bytes 388
  37.4 0.7 %copy-start.12 = (s32[2,6]{1,0:T(2,128)S(1)}, s32[2,6]{1,0:T(2,128)}, u32[]{:S(2)}) copy-start(s32[2,6]{1,0:T(2,128)} %adm_mid.1) | copy-start | bytes 148
  37.4 0.7 %copy-start.13 = (s32[4]{0:T(128)S(1)}, s32[4]{0:T(128)}, u32[]{:S(2)}) copy-start(s32[4]{0:T(128)} %near_count.1) | copy-start | bytes 52
  49.0 5.5 %collective-permute-start.2 = (f32[16,8,128]{2,1,0:T(8,128)S(1)}, f32[16,8,128]{2,1,0:T(8,128)S(1)}, u32[]{:S(2)}, u32[]{:S(2)}) collective-permute-start(f32[16,8,128]{2,1,0:T(8,128)S(1)} %answer.1), channel_id=1, source_target_pairs={{0,1},{1,0},{2,3},{3,2},{4,5},{5,4},{6,7},{7,6},{8,9},{9,8},{10,11... | collective-permute-start | bytes 196616 | tf_op jit(solution)/shard_map/ppermute | solution.py:540

commit v6 on v5

--- a/solution.py
+++ b/solution.py
@@ -28,7 +28,7 @@
 CORES = 2
 RING = 16
 PLANES = 16
-FIRST_Z = 11
+FIRST_Z = 12
 FIRST_PLANE = 10
 
 smooth_sq = 0.01

time: 56.3 us -> 55.9 us (level)
  starting transfers between devices: 36.4 us -> 35.4 us
  waiting for transfers between devices: 2.67 us -> 3.25 us
where the time goes in v6:
time: 55.9 us; the launch traced here: 55.5 us
  starting transfers between devices  35.4 us (63%)
  Pallas kernels  14.8 us (26%)
  waiting for transfers between devices  3.25 us (6%)
  local copies, waits for them, and re-layouts  1.79 us (3%)
    all_to_all x1, starting transfers between devices, on_device(): lax.all_to_all(own_top, 'leaf', 0, 0, axis_index_groups=along_z, tiled=True)  16.1 us
    all_to_all x1, starting transfers between devices, on_device(): lax.all_to_all(spread, 'leaf', 0, 0, axis_index_groups=across, tiled=True)  8.98 us
    pallas_call x1, Pallas kernels, near_call(): pl.pallas_call(near_kernel, name='near_and_couplings', out_shape=(jax.Sha...  7.96 us
    ppermute x1, starting transfers between devices, on_device(): lax.ppermute(answers, 'leaf', [(i, i ^ 1) for i in range(devices)])  4.22 us
    ppermute x1, starting transfers between devices, on_device(): lax.ppermute(packed, 'leaf', [(i, (i + 1 ^ 1) - 1) for i in range(1, devi...  4.21 us
    pallas_call x1, Pallas kernels, up_call(): pl.pallas_call(up_kernel, name='up_sweep', out_shape=(jax.ShapeDtypeStruc...  2.68 us
    all_to_all x1, waiting for transfers between devices, on_device(): lax.all_to_all(spread, 'leaf', 0, 0, axis_index_groups=across, tiled=True)  2.51 us
    ppermute x1, starting transfers between devices, on_device(): lax.ppermute(packed, 'leaf', [(i, i ^ 1) for i in range(devices)])  1.92 us
  transfers between devices with their start and end apart: 5, of which 2 were waited for; matrix products, arithmetic and copies ran while one was open for 0% of the time, Pallas kernels for 18%

profile of v6, /device:TPU:1, one launch (start us, length us, event | category | flops | bytes accessed | tf_op | source)
XLA Modules:
  0.0 55.5 jit_solution(3462212952012045874)
XLA Ops:
  0.0 0.0 copy-start.2
  0.0 2.7 %up_sweep.1 = (f32[16,8,128]{2,1,0:T(8,128)}, f32[8,768]{1,0:T(8,128)}) custom-call(f32[16,1024]{1,0:T(8,128)} %dens.3, f32[64,1024]{1,0:T(8,128)} %col_basis.1, f32[4,4096]{1,0:T(4,128)} %up_leaf.1, f32[2,4096]{1,0:T(2,128)} %up_mid.1), custom_call_target="tpu_custom_call" | custom-call | flops 10000000 | bytes 800000 | tf_op jit(solution)/shard_map/up_sweep/pallas_call | solution.py:133
  2.7 16.1 %all-to-all-start = ((f32[16,8,128]{2,1,0:T(8,128)}), f32[16,8,128]{2,1,0:T(8,128)S(1)}, u32[]{:S(2)}, u32[]{:S(2)}) async-start(f32[16,8,128]{2,1,0:T(8,128)} %get-tuple-element.30), calls=%async_computation | async-start | bytes 131072 | tf_op jit(solution)/shard_map/all_to_all | solution.py:512
  18.8 0.0 copy-done.8
  18.8 0.0 copy-done.9
  18.8 0.0 copy-done.14
  18.8 0.0 copy-done.7
  18.8 0.0 copy-done
  18.8 0.0 copy-start.5
  18.8 0.0 copy-start.6
  18.9 4.2 %collective-permute-start.1 = (f32[32,1024]{1,0:T(8,128)S(1)}, f32[32,1024]{1,0:T(8,128)S(1)}, u32[]{:S(2)}, u32[]{:S(2)}) collective-permute-start(f32[32,1024]{1,0:T(8,128)S(1)} %packed_for_neighbours.1.own), channel_id=1, source_target_pairs={{1,2},{2,1},{3,4},{4,3},{5,6},{6,5},{7,8},{8,7},{9,10},{10,9},{11,... | collective-permute-start | bytes 393224 | tf_op jit(solution)/shard_map/ppermute | solution.py:514
  23.1 1.9 %collective-permute-start = (f32[32,1024]{1,0:T(8,128)S(1)}, f32[32,1024]{1,0:T(8,128)S(1)}, u32[]{:S(2)}, u32[]{:S(2)}) collective-permute-start(f32[32,1024]{1,0:T(8,128)S(1)} %packed_for_neighbours.1.own), channel_id=1, source_target_pairs={{0,1},{1,0},{2,3},{3,2},{4,5},{5,4},{6,7},{7,6},{8,9},{9,8},{10,11... | collective-permute-start | bytes 393224 | tf_op jit(solution)/shard_map/ppermute | solution.py:513
  25.0 0.0 copy-done.2
  25.0 0.0 copy-done.3
  25.1 1.1 %transposed_matrices.1 = (bf16[256,512]{1,0:T(8,128)(2,1)S(1)}, f32[4,64,64]{2,1,0:T(8,128)S(1)}, bf16[192,1024]{1,0:T(8,128)(2,1)S(1)}) custom-call(f32[1,16,4096]{2,1,0:T(8,128)S(1)} %copy-done.2, f32[2,4096]{1,0:T(2,128)S(1)} %copy-done.6, f32[4,4096]{1,0:T(4,128)S(1)} %copy-done.5, f32[64,1024]{1,0:T(8,128)S(1)} %copy-done.3), custom_call_target="tpu_custom_call" | custom-call | flops 2000000000 | bytes 2000000 | tf_op jit(solution)/shard_map/transposed_matrices/pallas_call | solution.py:367
  26.2 0.7 %collective-permute-done.1.next_chip = f32[32,1024]{1,0:T(8,128)S(1)} collective-permute-done((f32[32,1024]{1,0:T(8,128)S(1)}, f32[32,1024]{1,0:T(8,128)S(1)}, u32[]{:S(2)}, u32[]{:S(2)}) %collective-permute-start.1) | collective-permute-done | bytes 131104 | tf_op jit(solution)/shard_map/ppermute | solution.py:514
  26.9 0.0 collective-permute-done.same_chip
  26.9 0.0 all-to-all-done
  26.9 1.1 %broadcast_in_dim.8 = f32[16,128,128]{2,1,0:T(8,128)} broadcast(f32[128,128]{1,0:T(8,128)S(1)} %bitcast.8), dimensions={1,2} | broadcast | bytes 1114112 | tf_op jit(solution)/shard_map/broadcast_in_dim | solution.py:519
  28.0 9.0 %all-to-all-start.1 = ((f32[16,128,128]{2,1,0:T(8,128)}), f32[16,128,128]{2,1,0:T(8,128)S(1)}, u32[]{:S(2)}, u32[]{:S(2)}) async-start(f32[16,128,128]{2,1,0:T(8,128)} %broadcast_in_dim.8), calls=%async_computation.1 | async-start | bytes 2097152 | tf_op jit(solution)/shard_map/all_to_all | solution.py:520
  37.0 0.0 copy-start.10
  37.0 0.0 copy-start.12
  37.1 0.0 copy-start.13
  37.1 0.6 %copy-done.10 = s32[4,8]{1,0:T(4,128)S(1)} copy-done((s32[4,8]{1,0:T(4,128)S(1)}, s32[4,8]{1,0:T(4,128)}, u32[]{:S(2)}) %copy-start.10) | copy-done | bytes 152
  37.7 0.0 copy-done.12
  37.7 8.0 %near_and_couplings.1 = (f32[16,1024]{1,0:T(8,128)S(1)}, s32[4,16]{1,0:T(4,128)S(1)}) custom-call(s32[4,8]{1,0:T(4,128)S(1)} %copy-done.10, s32[4]{0:T(128)S(1)} %copy-done.13, s32[4,6]{1,0:T(4,128)S(1)} %copy-done.11, s32[2,6]{1,0:T(2,128)S(1)} %copy-done.12, f32[32,1024]{1,0:T(8,128)S(1)} %packed_for_neighbours.1.own, ...), custom_call_target="tpu_custom_call" | custom-call | flops 4000000000 | bytes 2000000 | tf_op jit(solution)/shard_map/near_and_couplings/pallas_call | solution.py:388
  45.7 2.5 %all-to-all-done.1 = f32[16,128,128]{2,1,0:T(8,128)S(1)} async-done(((f32[16,128,128]{2,1,0:T(8,128)}), f32[16,128,128]{2,1,0:T(8,128)S(1)}, u32[]{:S(2)}, u32[]{:S(2)}) %all-to-all-start.1) | async-done | bytes 1048608 | tf_op jit(solution)/shard_map/all_to_all | solution.py:520
  48.2 0.6 %answer.1 = f32[16,8,128]{2,1,0:T(8,128)S(1)} custom-call(s32[4,16]{1,0:T(4,128)S(1)} %get-tuple-element.46.plan, f32[256,8,128]{2,1,0:T(8,128)S(1)} %bitcast.4), custom_call_target="tpu_custom_call" | custom-call | flops 1000000 | bytes 100000 | tf_op jit(solution)/shard_map/answer/pallas_call | solution.py:435
  48.8 4.2 %collective-permute-start.2 = (f32[16,8,128]{2,1,0:T(8,128)S(1)}, f32[16,8,128]{2,1,0:T(8,128)S(1)}, u32[]{:S(2)}, u32[]{:S(2)}) collective-permute-start(f32[16,8,128]{2,1,0:T(8,128)S(1)} %answer.1), channel_id=1, source_target_pairs={{0,1},{1,0},{2,3},{3,2},{4,5},{5,4},{6,7},{7,6},{8,9},{9,8},{10,11... | collective-permute-start | bytes 196616 | tf_op jit(solution)/shard_map/ppermute | solution.py:540
  53.0 1.1 %own_tops.1.own_share = f32[64,16]{1,0:T(8,128)S(1)} custom-call(s32[4,16]{1,0:T(4,128)S(1)} %get-tuple-element.46.plan, f32[256,8,128]{2,1,0:T(8,128)S(1)} %bitcast.5, bf16[256,512]{1,0:T(8,128)(2,1)S(1)} %get-tuple-element.48.top_mats), custom_call_target="tpu_custom_call" | custom-call | flops 400000000 | bytes 400000 | tf_op jit(solution)/shard_map/own_tops/pallas_call | solution.py:451
  54.1 0.0 collective-permute-done.2.received
  54.1 1.4 %down_sweep.1 = f32[16,1024]{1,0:T(8,128)} custom-call(f32[16,8,128]{2,1,0:T(8,128)S(1)} %collective-permute-done.2.received, f32[64,16]{1,0:T(8,128)S(1)} %own_tops.1.own_share, f32[16,1024]{1,0:T(8,128)S(1)} %get-tuple-element.49.base, bf16[256,512]{1,0:T(8,128)(2,1)S(1)} %get-tuple-element.48.top_mats, bf16[192,1024]{1,0:T(8,128)(2,1)S(1)} %get-tuple-element.50.top_to_points), custom_call_target="tpu_custom_call" | custom-call | flops 10000000 | bytes 800000 | tf_op jit(solution)/shard_map/down_sweep/pallas_call | solution.py:470
  (17 shorter events, 0.0 us)
Async XLA Ops:
  0.0 18.8 %copy-start.8 = (f32[3,1024]{1,0:T(4,128)S(1)}, f32[3,1024]{1,0:T(4,128)}, u32[]{:S(2)}) copy-start(f32[3,1024]{1,0:T(4,128)} %points.1) | copy-start | bytes 36868
  0.0 18.8 %copy-start.9 = (f32[3,1024]{1,0:T(4,128)S(1)}, f32[3,1024]{1,0:T(4,128)}, u32[]{:S(2)}) copy-start(f32[3,1024]{1,0:T(4,128)} %normals.1) | copy-start | bytes 36868
  0.0 18.8 %copy-start.14 = (s32[1,16]{1,0:T(1,128)S(1)}, s32[1,16]{1,0:T(1,128)}, u32[]{:S(2)}) copy-start(s32[1,16]{1,0:T(1,128)} %adm_top.3) | copy-start | bytes 196
  0.0 25.0 %copy-start.2 = (f32[1,16,4096]{2,1,0:T(8,128)S(1)}, f32[1,16,4096]{2,1,0:T(8,128)}, u32[]{:S(2)}) copy-start(f32[1,16,4096]{2,1,0:T(8,128)} %couple_top) | copy-start | bytes 786436
  2.7 16.1 %copy-start.7 = (f32[8,768]{1,0:T(8,128)S(1)}, f32[8,768]{1,0:T(8,128)}, u32[]{:S(2)}) copy-start(f32[8,768]{1,0:T(8,128)} %get-tuple-element.31.coefs) | copy-start | bytes 73732
  2.7 16.1 %copy-start = (f32[16,1024]{1,0:T(8,128)S(1)}, f32[16,1024]{1,0:T(8,128)}, u32[]{:S(2)}) copy-start(f32[16,1024]{1,0:T(8,128)} %dens.3) | copy-start | bytes 196612
  2.7 22.3 %copy-start.3 = (f32[64,1024]{1,0:T(8,128)S(1)}, f32[64,1024]{1,0:T(8,128)}, u32[]{:S(2)}) copy-start(f32[64,1024]{1,0:T(8,128)} %row_basis.3) | copy-start | bytes 786436
  2.7 24.2 %all-to-all-start = ((f32[16,8,128]{2,1,0:T(8,128)}), f32[16,8,128]{2,1,0:T(8,128)S(1)}, u32[]{:S(2)}, u32[]{:S(2)}) async-start(f32[16,8,128]{2,1,0:T(8,128)} %get-tuple-element.30), calls=%async_computation | async-start | bytes 131072 | tf_op jit(solution)/shard_map/all_to_all | solution.py:512
  18.8 6.2 %copy-start.5 = (f32[4,4096]{1,0:T(4,128)S(1)}, f32[4,4096]{1,0:T(4,128)}, u32[]{:S(2)}) copy-start(f32[4,4096]{1,0:T(4,128)} %down_leaf) | copy-start | bytes 196612
  18.8 6.2 %copy-start.6 = (f32[2,4096]{1,0:T(2,128)S(1)}, f32[2,4096]{1,0:T(2,128)}, u32[]{:S(2)}) copy-start(f32[2,4096]{1,0:T(2,128)} %down_mid) | copy-start | bytes 98308
  18.9 8.0 %collective-permute-start.1 = (f32[32,1024]{1,0:T(8,128)S(1)}, f32[32,1024]{1,0:T(8,128)S(1)}, u32[]{:S(2)}, u32[]{:S(2)}) collective-permute-start(f32[32,1024]{1,0:T(8,128)S(1)} %packed_for_neighbours.1.own), channel_id=1, source_target_pairs={{1,2},{2,1},{3,4},{4,3},{5,6},{6,5},{7,8},{8,7},{9,10},{10,9},{11,... | collective-permute-start | bytes 393224 | tf_op jit(solution)/shard_map/ppermute | solution.py:514
  23.1 3.8 %collective-permute-start = (f32[32,1024]{1,0:T(8,128)S(1)}, f32[32,1024]{1,0:T(8,128)S(1)}, u32[]{:S(2)}, u32[]{:S(2)}) collective-permute-start(f32[32,1024]{1,0:T(8,128)S(1)} %packed_for_neighbours.1.own), channel_id=1, source_target_pairs={{0,1},{1,0},{2,3},{3,2},{4,5},{5,4},{6,7},{7,6},{8,9},{9,8},{10,11... | collective-permute-start | bytes 393224 | tf_op jit(solution)/shard_map/ppermute | solution.py:513
  28.0 9.0 %copy-start.1 = (f32[4,6,4096]{2,0,1:T(4,128)S(1)}, f32[4,6,4096]{2,0,1:T(4,128)}, u32[]{:S(2)}) copy-start(f32[4,6,4096]{2,0,1:T(4,128)} %param.26) | copy-start | bytes 1179652
  28.0 9.0 %copy-start.4 = (f32[2,6,4096]{2,0,1:T(2,128)S(1)}, f32[2,6,4096]{2,0,1:T(2,128)}, u32[]{:S(2)}) copy-start(f32[2,6,4096]{2,0,1:T(2,128)} %param.27) | copy-start | bytes 589828
  28.0 9.1 %copy-start.11 = (s32[4,6]{1,0:T(4,128)S(1)}, s32[4,6]{1,0:T(4,128)}, u32[]{:S(2)}) copy-start(s32[4,6]{1,0:T(4,128)} %adm_leaf.1) | copy-start | bytes 292
  28.0 20.2 %all-to-all-start.1 = ((f32[16,128,128]{2,1,0:T(8,128)}), f32[16,128,128]{2,1,0:T(8,128)S(1)}, u32[]{:S(2)}, u32[]{:S(2)}) async-start(f32[16,128,128]{2,1,0:T(8,128)} %broadcast_in_dim.8), calls=%async_computation.1 | async-start | bytes 2097152 | tf_op jit(solution)/shard_map/all_to_all | solution.py:520
  37.0 0.7 %copy-start.10 = (s32[4,8]{1,0:T(4,128)S(1)}, s32[4,8]{1,0:T(4,128)}, u32[]{:S(2)}) copy-start(s32[4,8]{1,0:T(4,128)} %near_list.1) | copy-start | bytes 388
  37.0 0.7 %copy-start.12 = (s32[2,6]{1,0:T(2,128)S(1)}, s32[2,6]{1,0:T(2,128)}, u32[]{:S(2)}) copy-start(s32[2,6]{1,0:T(2,128)} %adm_mid.1) | copy-start | bytes 148
  37.1 0.7 %copy-start.13 = (s32[4]{0:T(128)S(1)}, s32[4]{0:T(128)}, u32[]{:S(2)}) copy-start(s32[4]{0:T(128)} %near_count.1) | copy-start | bytes 52
  48.8 5.3 %collective-permute-start.2 = (f32[16,8,128]{2,1,0:T(8,128)S(1)}, f32[16,8,128]{2,1,0:T(8,128)S(1)}, u32[]{:S(2)}, u32[]{:S(2)}) collective-permute-start(f32[16,8,128]{2,1,0:T(8,128)S(1)} %answer.1), channel_id=1, source_target_pairs={{0,1},{1,0},{2,3},{3,2},{4,5},{5,4},{6,7},{7,6},{8,9},{9,8},{10,11... | collective-permute-start | bytes 196616 | tf_op jit(solution)/shard_map/ppermute | solution.py:540

commit v7 on v6

--- a/solution.py
+++ b/solution.py
@@ -163,6 +163,11 @@
     rest = values - first
     second = rest.astype(bf16).astype(f32)
     return first, second, (rest - second).astype(bf16).astype(f32)
+
+
+def ring_place(z):
+    ahead = (z + RING - FIRST_Z) % RING
+    return jnp.where(ahead <= RING // 2, jnp.maximum(2 * ahead - 1, 0), 2 * (RING - ahead))
 
 
 def near_kernel(
@@ -207,7 +212,7 @@
         for a in range(ADM_TOP):
             plane = tops[0, a] // (CORES * RING)
             z = tops[0, a] // CORES % RING
-            plan[row, a] = (plane + PLANES - FIRST_PLANE) % PLANES * RING + (z + RING - FIRST_Z) % RING
+            plan[row, a] = (plane + PLANES - FIRST_PLANE) % PLANES * RING + ring_place(z)
             plan[row + 1, a] = (tops[0, a] % CORES == core).astype(jnp.int32)
 
     count = jnp.int32(0)
@@ -480,7 +485,7 @@
 
 def solution(mesh):
     devices = mesh.devices.size
-    ring = [(FIRST_Z + i) % RING for i in range(RING)]
+    ring = [(FIRST_Z + ((i + 1) // 2 if i % 2 else -(i // 2))) % RING for i in range(RING)]
     planes = [(FIRST_PLANE + i) % PLANES for i in range(PLANES)]
     along_z = [[(p * RING + z) * CORES + c for z in ring] for p in range(PLANES) for c in range(CORES)]
     across = [[(p * RING + z) * CORES + c for p in planes] for z in range(RING) for c in range(CORES)]

time: 55.9 us -> 55.9 us (level)
  no operation moved by 1% of the time
where the time goes in v7:
time: 55.9 us; the launch traced here: 55.5 us
  starting transfers between devices  35.5 us (64%)
  Pallas kernels  14.9 us (27%)
  waiting for transfers between devices  3.1 us (6%)
  local copies, waits for them, and re-layouts  1.79 us (3%)
    all_to_all x1, starting transfers between devices, on_device(): lax.all_to_all(own_top, 'leaf', 0, 0, axis_index_groups=along_z, tiled=True)  16.1 us
    all_to_all x1, starting transfers between devices, on_device(): lax.all_to_all(spread, 'leaf', 0, 0, axis_index_groups=across, tiled=True)  8.98 us
    pallas_call x1, Pallas kernels, near_call(): pl.pallas_call(near_kernel, name='near_and_couplings', out_shape=(jax.Sha...  8.02 us
    ppermute x1, starting transfers between devices, on_device(): lax.ppermute(answers, 'leaf', [(i, i ^ 1) for i in range(devices)])  4.33 us
    ppermute x1, starting transfers between devices, on_device(): lax.ppermute(packed, 'leaf', [(i, (i + 1 ^ 1) - 1) for i in range(1, devi...  4.21 us
    pallas_call x1, Pallas kernels, up_call(): pl.pallas_call(up_kernel, name='up_sweep', out_shape=(jax.ShapeDtypeStruc...  2.68 us
    all_to_all x1, waiting for transfers between devices, on_device(): lax.all_to_all(spread, 'leaf', 0, 0, axis_index_groups=across, tiled=True)  2.4 us
    ppermute x1, starting transfers between devices, on_device(): lax.ppermute(packed, 'leaf', [(i, i ^ 1) for i in range(devices)])  1.92 us
  transfers between devices with their start and end apart: 5, of which 2 were waited for; matrix products, arithmetic and copies ran while one was open for 0% of the time, Pallas kernels for 18%

profile of v7, /device:TPU:1, one launch (start us, length us, event | category | flops | bytes accessed | tf_op | source)
XLA Modules:
  0.0 55.5 jit_solution(14614609889445364191)
XLA Ops:
  0.0 0.0 copy-start.2
  0.0 2.7 %up_sweep.1 = (f32[16,8,128]{2,1,0:T(8,128)}, f32[8,768]{1,0:T(8,128)}) custom-call(f32[16,1024]{1,0:T(8,128)} %dens.3, f32[64,1024]{1,0:T(8,128)} %col_basis.1, f32[4,4096]{1,0:T(4,128)} %up_leaf.1, f32[2,4096]{1,0:T(2,128)} %up_mid.1), custom_call_target="tpu_custom_call" | custom-call | flops 10000000 | bytes 800000 | tf_op jit(solution)/shard_map/up_sweep/pallas_call | solution.py:133
  2.7 16.1 %all-to-all-start = ((f32[16,8,128]{2,1,0:T(8,128)}), f32[16,8,128]{2,1,0:T(8,128)S(1)}, u32[]{:S(2)}, u32[]{:S(2)}) async-start(f32[16,8,128]{2,1,0:T(8,128)} %get-tuple-element.30), calls=%async_computation | async-start | bytes 131072 | tf_op jit(solution)/shard_map/all_to_all | solution.py:517
  18.8 0.0 copy-done.8
  18.8 0.0 copy-done.9
  18.8 0.0 copy-done.14
  18.8 0.0 copy-done.7
  18.8 0.0 copy-done
  18.8 0.0 copy-start.5
  18.8 0.0 copy-start.6
  18.9 4.2 %collective-permute-start.1 = (f32[32,1024]{1,0:T(8,128)S(1)}, f32[32,1024]{1,0:T(8,128)S(1)}, u32[]{:S(2)}, u32[]{:S(2)}) collective-permute-start(f32[32,1024]{1,0:T(8,128)S(1)} %packed_for_neighbours.1.own), channel_id=1, source_target_pairs={{1,2},{2,1},{3,4},{4,3},{5,6},{6,5},{7,8},{8,7},{9,10},{10,9},{11,... | collective-permute-start | bytes 393224 | tf_op jit(solution)/shard_map/ppermute | solution.py:519
  23.1 1.9 %collective-permute-start = (f32[32,1024]{1,0:T(8,128)S(1)}, f32[32,1024]{1,0:T(8,128)S(1)}, u32[]{:S(2)}, u32[]{:S(2)}) collective-permute-start(f32[32,1024]{1,0:T(8,128)S(1)} %packed_for_neighbours.1.own), channel_id=1, source_target_pairs={{0,1},{1,0},{2,3},{3,2},{4,5},{5,4},{6,7},{7,6},{8,9},{9,8},{10,11... | collective-permute-start | bytes 393224 | tf_op jit(solution)/shard_map/ppermute | solution.py:518
  25.0 0.0 copy-done.2
  25.1 1.1 %transposed_matrices.1 = (bf16[256,512]{1,0:T(8,128)(2,1)S(1)}, f32[4,64,64]{2,1,0:T(8,128)S(1)}, bf16[192,1024]{1,0:T(8,128)(2,1)S(1)}) custom-call(f32[1,16,4096]{2,1,0:T(8,128)S(1)} %copy-done.2, f32[2,4096]{1,0:T(2,128)S(1)} %copy-done.6, f32[4,4096]{1,0:T(4,128)S(1)} %copy-done.5, f32[64,1024]{1,0:T(8,128)S(1)} %copy-done.3), custom_call_target="tpu_custom_call" | custom-call | flops 2000000000 | bytes 2000000 | tf_op jit(solution)/shard_map/transposed_matrices/pallas_call | solution.py:372
  26.2 0.7 %collective-permute-done.1.next_chip = f32[32,1024]{1,0:T(8,128)S(1)} collective-permute-done((f32[32,1024]{1,0:T(8,128)S(1)}, f32[32,1024]{1,0:T(8,128)S(1)}, u32[]{:S(2)}, u32[]{:S(2)}) %collective-permute-start.1) | collective-permute-done | bytes 131104 | tf_op jit(solution)/shard_map/ppermute | solution.py:519
  26.9 0.0 collective-permute-done.same_chip
  26.9 0.0 all-to-all-done
  26.9 1.1 %broadcast_in_dim.8 = f32[16,128,128]{2,1,0:T(8,128)} broadcast(f32[128,128]{1,0:T(8,128)S(1)} %bitcast.8), dimensions={1,2} | broadcast | bytes 1114112 | tf_op jit(solution)/shard_map/broadcast_in_dim | solution.py:524
  28.0 9.0 %all-to-all-start.1 = ((f32[16,128,128]{2,1,0:T(8,128)}), f32[16,128,128]{2,1,0:T(8,128)S(1)}, u32[]{:S(2)}, u32[]{:S(2)}) async-start(f32[16,128,128]{2,1,0:T(8,128)} %broadcast_in_dim.8), calls=%async_computation.1 | async-start | bytes 2097152 | tf_op jit(solution)/shard_map/all_to_all | solution.py:525
  37.0 0.0 copy-start.10
  37.0 0.0 copy-start.12
  37.0 0.0 copy-start.13
  37.1 0.6 %copy-done.10 = s32[4,8]{1,0:T(4,128)S(1)} copy-done((s32[4,8]{1,0:T(4,128)S(1)}, s32[4,8]{1,0:T(4,128)}, u32[]{:S(2)}) %copy-start.10) | copy-done | bytes 152
  37.7 0.0 copy-done.12
  37.7 0.0 copy-done.13
  37.7 8.0 %near_and_couplings.1 = (f32[16,1024]{1,0:T(8,128)S(1)}, s32[4,16]{1,0:T(4,128)S(1)}) custom-call(s32[4,8]{1,0:T(4,128)S(1)} %copy-done.10, s32[4]{0:T(128)S(1)} %copy-done.13, s32[4,6]{1,0:T(4,128)S(1)} %copy-done.11, s32[2,6]{1,0:T(2,128)S(1)} %copy-done.12, f32[32,1024]{1,0:T(8,128)S(1)} %packed_for_neighbours.1.own, ...), custom_call_target="tpu_custom_call" | custom-call | flops 4000000000 | bytes 2000000 | tf_op jit(solution)/shard_map/near_and_couplings/pallas_call | solution.py:393
  45.7 2.4 %all-to-all-done.1 = f32[16,128,128]{2,1,0:T(8,128)S(1)} async-done(((f32[16,128,128]{2,1,0:T(8,128)}), f32[16,128,128]{2,1,0:T(8,128)S(1)}, u32[]{:S(2)}, u32[]{:S(2)}) %all-to-all-start.1) | async-done | bytes 1048608 | tf_op jit(solution)/shard_map/all_to_all | solution.py:525
  48.1 0.6 %answer.1 = f32[16,8,128]{2,1,0:T(8,128)S(1)} custom-call(s32[4,16]{1,0:T(4,128)S(1)} %get-tuple-element.46.plan, f32[256,8,128]{2,1,0:T(8,128)S(1)} %bitcast.4), custom_call_target="tpu_custom_call" | custom-call | flops 1000000 | bytes 100000 | tf_op jit(solution)/shard_map/answer/pallas_call | solution.py:440
  48.7 4.3 %collective-permute-start.2 = (f32[16,8,128]{2,1,0:T(8,128)S(1)}, f32[16,8,128]{2,1,0:T(8,128)S(1)}, u32[]{:S(2)}, u32[]{:S(2)}) collective-permute-start(f32[16,8,128]{2,1,0:T(8,128)S(1)} %answer.1), channel_id=1, source_target_pairs={{0,1},{1,0},{2,3},{3,2},{4,5},{5,4},{6,7},{7,6},{8,9},{9,8},{10,11... | collective-permute-start | bytes 196616 | tf_op jit(solution)/shard_map/ppermute | solution.py:545
  53.1 1.1 %own_tops.1.own_share = f32[64,16]{1,0:T(8,128)S(1)} custom-call(s32[4,16]{1,0:T(4,128)S(1)} %get-tuple-element.46.plan, f32[256,8,128]{2,1,0:T(8,128)S(1)} %bitcast.5, bf16[256,512]{1,0:T(8,128)(2,1)S(1)} %get-tuple-element.48.top_mats), custom_call_target="tpu_custom_call" | custom-call | flops 400000000 | bytes 400000 | tf_op jit(solution)/shard_map/own_tops/pallas_call | solution.py:456
  54.1 0.0 collective-permute-done.2.received
  54.1 1.4 %down_sweep.1 = f32[16,1024]{1,0:T(8,128)} custom-call(f32[16,8,128]{2,1,0:T(8,128)S(1)} %collective-permute-done.2.received, f32[64,16]{1,0:T(8,128)S(1)} %own_tops.1.own_share, f32[16,1024]{1,0:T(8,128)S(1)} %get-tuple-element.49.base, bf16[256,512]{1,0:T(8,128)(2,1)S(1)} %get-tuple-element.48.top_mats, bf16[192,1024]{1,0:T(8,128)(2,1)S(1)} %get-tuple-element.50.top_to_points), custom_call_target="tpu_custom_call" | custom-call | flops 10000000 | bytes 800000 | tf_op jit(solution)/shard_map/down_sweep/pallas_call | solution.py:475
  (17 shorter events, 0.0 us)
Async XLA Ops:
  0.0 18.8 %copy-start.8 = (f32[3,1024]{1,0:T(4,128)S(1)}, f32[3,1024]{1,0:T(4,128)}, u32[]{:S(2)}) copy-start(f32[3,1024]{1,0:T(4,128)} %points.1) | copy-start | bytes 36868
  0.0 18.8 %copy-start.9 = (f32[3,1024]{1,0:T(4,128)S(1)}, f32[3,1024]{1,0:T(4,128)}, u32[]{:S(2)}) copy-start(f32[3,1024]{1,0:T(4,128)} %normals.1) | copy-start | bytes 36868
  0.0 18.8 %copy-start.14 = (s32[1,16]{1,0:T(1,128)S(1)}, s32[1,16]{1,0:T(1,128)}, u32[]{:S(2)}) copy-start(s32[1,16]{1,0:T(1,128)} %adm_top.3) | copy-start | bytes 196
  0.0 25.0 %copy-start.2 = (f32[1,16,4096]{2,1,0:T(8,128)S(1)}, f32[1,16,4096]{2,1,0:T(8,128)}, u32[]{:S(2)}) copy-start(f32[1,16,4096]{2,1,0:T(8,128)} %couple_top) | copy-start | bytes 786436
  2.7 16.1 %copy-start.7 = (f32[8,768]{1,0:T(8,128)S(1)}, f32[8,768]{1,0:T(8,128)}, u32[]{:S(2)}) copy-start(f32[8,768]{1,0:T(8,128)} %get-tuple-element.31.coefs) | copy-start | bytes 73732
  2.7 16.1 %copy-start = (f32[16,1024]{1,0:T(8,128)S(1)}, f32[16,1024]{1,0:T(8,128)}, u32[]{:S(2)}) copy-start(f32[16,1024]{1,0:T(8,128)} %dens.3) | copy-start | bytes 196612
  2.7 22.3 %copy-start.3 = (f32[64,1024]{1,0:T(8,128)S(1)}, f32[64,1024]{1,0:T(8,128)}, u32[]{:S(2)}) copy-start(f32[64,1024]{1,0:T(8,128)} %row_basis.3) | copy-start | bytes 786436
  2.7 24.2 %all-to-all-start = ((f32[16,8,128]{2,1,0:T(8,128)}), f32[16,8,128]{2,1,0:T(8,128)S(1)}, u32[]{:S(2)}, u32[]{:S(2)}) async-start(f32[16,8,128]{2,1,0:T(8,128)} %get-tuple-element.30), calls=%async_computation | async-start | bytes 131072 | tf_op jit(solution)/shard_map/all_to_all | solution.py:517
  18.8 6.2 %copy-start.5 = (f32[4,4096]{1,0:T(4,128)S(1)}, f32[4,4096]{1,0:T(4,128)}, u32[]{:S(2)}) copy-start(f32[4,4096]{1,0:T(4,128)} %down_leaf) | copy-start | bytes 196612
  18.8 6.2 %copy-start.6 = (f32[2,4096]{1,0:T(2,128)S(1)}, f32[2,4096]{1,0:T(2,128)}, u32[]{:S(2)}) copy-start(f32[2,4096]{1,0:T(2,128)} %down_mid) | copy-start | bytes 98308
  18.9 8.0 %collective-permute-start.1 = (f32[32,1024]{1,0:T(8,128)S(1)}, f32[32,1024]{1,0:T(8,128)S(1)}, u32[]{:S(2)}, u32[]{:S(2)}) collective-permute-start(f32[32,1024]{1,0:T(8,128)S(1)} %packed_for_neighbours.1.own), channel_id=1, source_target_pairs={{1,2},{2,1},{3,4},{4,3},{5,6},{6,5},{7,8},{8,7},{9,10},{10,9},{11,... | collective-permute-start | bytes 393224 | tf_op jit(solution)/shard_map/ppermute | solution.py:519
  23.1 3.8 %collective-permute-start = (f32[32,1024]{1,0:T(8,128)S(1)}, f32[32,1024]{1,0:T(8,128)S(1)}, u32[]{:S(2)}, u32[]{:S(2)}) collective-permute-start(f32[32,1024]{1,0:T(8,128)S(1)} %packed_for_neighbours.1.own), channel_id=1, source_target_pairs={{0,1},{1,0},{2,3},{3,2},{4,5},{5,4},{6,7},{7,6},{8,9},{9,8},{10,11... | collective-permute-start | bytes 393224 | tf_op jit(solution)/shard_map/ppermute | solution.py:518
  28.0 9.0 %copy-start.1 = (f32[4,6,4096]{2,0,1:T(4,128)S(1)}, f32[4,6,4096]{2,0,1:T(4,128)}, u32[]{:S(2)}) copy-start(f32[4,6,4096]{2,0,1:T(4,128)} %param.26) | copy-start | bytes 1179652
  28.0 9.0 %copy-start.4 = (f32[2,6,4096]{2,0,1:T(2,128)S(1)}, f32[2,6,4096]{2,0,1:T(2,128)}, u32[]{:S(2)}) copy-start(f32[2,6,4096]{2,0,1:T(2,128)} %param.27) | copy-start | bytes 589828
  28.0 9.1 %copy-start.11 = (s32[4,6]{1,0:T(4,128)S(1)}, s32[4,6]{1,0:T(4,128)}, u32[]{:S(2)}) copy-start(s32[4,6]{1,0:T(4,128)} %adm_leaf.1) | copy-start | bytes 292
  28.0 20.1 %all-to-all-start.1 = ((f32[16,128,128]{2,1,0:T(8,128)}), f32[16,128,128]{2,1,0:T(8,128)S(1)}, u32[]{:S(2)}, u32[]{:S(2)}) async-start(f32[16,128,128]{2,1,0:T(8,128)} %broadcast_in_dim.8), calls=%async_computation.1 | async-start | bytes 2097152 | tf_op jit(solution)/shard_map/all_to_all | solution.py:525
  37.0 0.7 %copy-start.10 = (s32[4,8]{1,0:T(4,128)S(1)}, s32[4,8]{1,0:T(4,128)}, u32[]{:S(2)}) copy-start(s32[4,8]{1,0:T(4,128)} %near_list.1) | copy-start | bytes 388
  37.0 0.7 %copy-start.12 = (s32[2,6]{1,0:T(2,128)S(1)}, s32[2,6]{1,0:T(2,128)}, u32[]{:S(2)}) copy-start(s32[2,6]{1,0:T(2,128)} %adm_mid.1) | copy-start | bytes 148
  37.0 0.7 %copy-start.13 = (s32[4]{0:T(128)S(1)}, s32[4]{0:T(128)}, u32[]{:S(2)}) copy-start(s32[4]{0:T(128)} %near_count.1) | copy-start | bytes 52
  48.7 5.4 %collective-permute-start.2 = (f32[16,8,128]{2,1,0:T(8,128)S(1)}, f32[16,8,128]{2,1,0:T(8,128)S(1)}, u32[]{:S(2)}, u32[]{:S(2)}) collective-permute-start(f32[16,8,128]{2,1,0:T(8,128)S(1)} %answer.1), channel_id=1, source_target_pairs={{0,1},{1,0},{2,3},{3,2},{4,5},{5,4},{6,7},{7,6},{8,9},{9,8},{10,11... | collective-permute-start | bytes 196616 | tf_op jit(solution)/shard_map/ppermute | solution.py:545
